TPU v7x, 32 devices: a whole 2x2x4 slice. The times are simulated.
32 devices in a mesh: rows: 8 (over y, x, core), cols: 4 (over z).
Axes of the slice: x: 2, y: 2, z: 4, core: 2. Of those that a mesh axis runs over, the one named last changes fastest.
Arguments:
- krylov: bfloat16 [8192, 256], P(('rows', 'cols')), may hold values from -6 to 6
- geometry: float32 [7, 8192], P(None, ('rows', 'cols')), may hold values from -1 to 2, as said below
- corr_index: int32 [8, 8192], P(None, ('rows', 'cols')), may hold values from 0 to 8191, as said below
- corr_weight: float32 [16, 8192], P(None, ('rows', 'cols')), may hold values from -1.5 to 1.5
- blades: int32 [128], replicated, may hold values from 3 to 8
- harmonic: int32 [128], replicated, may hold values from 1 to 4
- observer_angles: float32 [2, 2048], replicated, may hold values from -3.140625 to 3.140625
Outputs:
- residual: float32 [8192, 256], P(('rows', 'cols'))
- far_field: float32 [2048, 256], P(('rows', 'cols'))
Inputs may be any that keep to these rules, and one draw needn't show every extreme that they name: `geometry`: centers lie on a duct of radius about 1 with heights 0 to 2 and on a centerbody of radius 0.35; normals have unit length; areas are positive. corr_index[c, i] lies in the same aligned block of 256 consecutive panels as panel i.
All inputs are finite; a program needn't handle non-finite values.
Results may differ from a plain program's by a relative error of at most 0.0029.
Values may be sent and summed in bfloat16 or wider, within the bound.
No kernel may reach another device: no remote copies, remote signals or barrier semaphores. Data moves between devices by JAX's collectives and lax.ppermute only.
A program may use at most 64 MiB of HBM per device.

v0:
```python
import math

import jax
import jax.numpy as jnp
from jax import lax
from jax.sharding import PartitionSpec as P

NS = 64


wavenumber = 20.0
cycle_radius = 0.7
cycle_height = 1.0
four_pi = 4.0 * math.pi


def green_parts(r_sq):
    inverse = lax.rsqrt(r_sq)
    phase = wavenumber * r_sq * inverse
    g_re = jnp.cos(phase) * inverse / four_pi
    g_im = jnp.sin(phase) * inverse / four_pi
    f_re = (-g_re * inverse - wavenumber * g_im) * inverse
    f_im = (-g_im * inverse + wavenumber * g_re) * inverse
    return (g_re, g_im, f_re, f_im)


def panel_tile(row_geom, col_geom, row_ids, col_ids, soft_sq):
    dx = row_geom[0][:, None] - col_geom[0][None, :]
    dy = row_geom[1][:, None] - col_geom[1][None, :]
    dz = row_geom[2][:, None] - col_geom[2][None, :]
    r_sq = dx * dx + dy * dy + dz * dz + soft_sq
    g_re, g_im, f_re, f_im = green_parts(r_sq)
    along_col = -(dx * col_geom[3][None, :] + dy * col_geom[4][None, :] + dz * col_geom[5][None, :])
    along_row = (
        dx * row_geom[3][:, None] + dy * row_geom[4][:, None] + dz * row_geom[5][:, None]
    ) / wavenumber
    area = col_geom[6][None, :]
    t_re = area * (f_re * along_col - f_im * along_row)
    t_im = area * (f_re * along_row + f_im * along_col)
    same = row_ids[:, None] == col_ids[None, :]
    zeros = jnp.zeros_like(t_re)
    return (
        jnp.where(same, zeros, t_re).astype(jnp.bfloat16),
        jnp.where(same, zeros, t_im).astype(jnp.bfloat16),
    )


def apply_tile(t_re, t_im, vectors):
    nvec = vectors.shape[1] // 2
    first = jnp.dot(t_re, vectors, preferred_element_type=jnp.float32)
    second = jnp.dot(t_im, vectors, preferred_element_type=jnp.float32)
    return jnp.concatenate(
        [first[:, :nvec] - second[:, nvec:], first[:, nvec:] + second[:, :nvec]], axis=1
    )


def far_tile(angles, geom):
    sin_t = jnp.sin(angles[0])
    dir_x = sin_t * jnp.cos(angles[1])
    dir_y = sin_t * jnp.sin(angles[1])
    dir_z = jnp.cos(angles[0])
    along = (
        dir_x[:, None] * geom[0][None, :]
        + dir_y[:, None] * geom[1][None, :]
        + dir_z[:, None] * geom[2][None, :]
    )
    normal_part = (
        dir_x[:, None] * geom[3][None, :]
        + dir_y[:, None] * geom[4][None, :]
        + dir_z[:, None] * geom[5][None, :]
    )
    phase = -wavenumber * along
    scale = geom[6][None, :] * wavenumber * normal_part
    t_re = scale * jnp.sin(phase)
    t_im = -scale * jnp.cos(phase)
    return (t_re.astype(jnp.bfloat16), t_im.astype(jnp.bfloat16))


def incident(geom, blades, harmonic):
    angle = 2.0 * math.pi * jnp.arange(NS, dtype=jnp.float32) / NS
    src_x = cycle_radius * jnp.cos(angle)
    src_y = cycle_radius * jnp.sin(angle)
    dx = geom[0][:, None] - src_x[None, :]
    dy = geom[1][:, None] - src_y[None, :]
    dz = geom[2][:, None] - cycle_height
    r_sq = dx * dx + dy * dy + dz * dz
    g_re, g_im, f_re, f_im = green_parts(r_sq)
    normal_part = (
        dx * geom[3][:, None] + dy * geom[4][:, None] + dz * geom[5][:, None]
    ) / wavenumber
    h_re = g_re - f_im * normal_part
    h_im = g_im + f_re * normal_part
    modes = (blades * harmonic).astype(jnp.float32)
    e_re = jnp.cos(angle[:, None] * modes[None, :])
    e_im = jnp.sin(angle[:, None] * modes[None, :])
    high = lax.Precision.HIGHEST
    b_re = jnp.dot(h_re, e_re, precision=high) - jnp.dot(h_im, e_im, precision=high)
    b_im = jnp.dot(h_re, e_im, precision=high) + jnp.dot(h_im, e_re, precision=high)
    return jnp.concatenate([b_re, b_im], axis=1)


def correction(values, index_local, weights):
    count = index_local.shape[0]
    nvec = values.shape[1] // 2
    nearby = values[index_local]
    w_re = weights[:count][:, :, None]
    w_im = weights[count:][:, :, None]
    part_re = jnp.sum(w_re * nearby[:, :, :nvec] - w_im * nearby[:, :, nvec:], axis=0)
    part_im = jnp.sum(w_re * nearby[:, :, nvec:] + w_im * nearby[:, :, :nvec], axis=0)
    return jnp.concatenate([part_re, part_im], axis=1)


def local(krylov, geometry, corr_index, corr_weight, blades, harmonic, observer_angles):
    nrows = lax.axis_size("rows")
    ncols = lax.axis_size("cols")
    row_at = lax.axis_index("rows")
    col_at = lax.axis_index("cols")
    piece = krylov.shape[0]
    width = krylov.shape[1]
    panels = piece * nrows * ncols
    soft_sq = 4.0 / panels
    row_geom = lax.all_gather(geometry, "cols", axis=1, tiled=True)
    col_geom = lax.all_gather(geometry, "rows", axis=1, tiled=True)
    col_vectors = lax.all_gather(krylov, "rows", axis=0, tiled=True)
    row_ids = row_at * (ncols * piece) + jnp.arange(ncols * piece, dtype=jnp.int32)
    col_pos = jnp.arange(nrows * piece, dtype=jnp.int32)
    col_ids = (col_pos // piece * ncols + col_at) * piece + col_pos % piece
    block = math.gcd(piece * lax.axis_size("cols"), 256)

    def one_block(step):
        begin = step * block
        geom = lax.dynamic_slice_in_dim(row_geom, begin, block, 1)
        ids = lax.dynamic_slice_in_dim(row_ids, begin, block, 0)
        t_re, t_im = panel_tile(geom, col_geom, ids, col_ids, soft_sq)
        return apply_tile(t_re, t_im, col_vectors)

    applied = lax.psum_scatter(
        lax.map(
            one_block, jnp.arange(piece * lax.axis_size("cols") // block, dtype=jnp.int32)
        ).reshape(piece * lax.axis_size("cols"), width),
        "cols",
        scatter_dimension=0,
        tiled=True,
    )
    first_panel = (row_at * ncols + col_at) * piece
    values = krylov.astype(jnp.float32)
    near = correction(values, corr_index - first_panel, corr_weight)
    source = incident(geometry, blades, harmonic)
    residual = source - (0.5 * values + near + applied)
    obs_each = observer_angles.shape[1] // (nrows * ncols)
    group_first = row_at * (ncols * obs_each)
    group_block = math.gcd(obs_each * lax.axis_size("cols"), 512)

    def one_group(step):
        angles = lax.dynamic_slice_in_dim(
            observer_angles, group_first + step * group_block, group_block, 1
        )
        t_re, t_im = far_tile(angles, col_geom)
        return apply_tile(t_re, t_im, col_vectors)

    far_field = lax.psum_scatter(
        lax.map(
            one_group, jnp.arange(obs_each * lax.axis_size("cols") // group_block, dtype=jnp.int32)
        ).reshape(obs_each * lax.axis_size("cols"), width),
        "cols",
        scatter_dimension=0,
        tiled=True,
    )
    return (residual, far_field)


def solution(mesh):
    placed = (
        P(("rows", "cols"), None),
        P(None, ("rows", "cols")),
        P(None, ("rows", "cols")),
        P(None, ("rows", "cols")),
        P(),
        P(),
        P(),
    )
    return jax.shard_map(
        local,
        mesh=mesh,
        in_specs=placed,
        out_specs=(P(("rows", "cols"), None), P(("rows", "cols"), None)),
        check_vma=False,
    )
```

profile of v0, /device:TPU:0, one launch (start us, length us, event | category | flops | bytes accessed | tf_op | source)
XLA Modules:
  0.0 232.8 jit_solution(850533381953709542)
XLA Ops:
  9.9 6.6 %gather_fusion = f32[2048,256]{1,0:T(8,128)S(1)} fusion(f32[256,256]{1,0:T(8,128)S(1)} %copy.22, s32[2048]{0:T(1024)S(1)} %broadcast_clamp_fusion), kind=kCustom, calls=%fused_computation | custom fusion | bytes 4202496 | tf_op jit(solution)/shard_map/gather | solution.py:105
  16.5 14.8 %all_gather.10 = f32[7,1024]{1,0:T(8,128)S(1)} all-gather(f32[7,256]{1,0:T(8,128)S(1)} %copy-done), channel_id=1, replica_groups=mesh['rows'=8,'cols'=4] {'cols'}, dimensions={1}, use_global_device_ids=true | all-gather | bytes 35840 | tf_op jit(solution)/shard_map/all_gather | solution.py:122
  31.3 9.2 %all_gather.9 = f32[7,2048]{1,0:T(8,128)S(1)} all-gather(f32[7,256]{1,0:T(8,128)S(1)} %copy-done), channel_id=1, replica_groups=mesh['rows'=8,'cols'=4] {'rows'}, dimensions={1}, use_global_device_ids=true | all-gather | bytes 64512 | tf_op jit(solution)/shard_map/all_gather | solution.py:123
  40.7 1.4 fusion.96
  42.1 132.7 %while.18 = (s32[]{:T(128)}, f32[4,256,256]{1,0,2:T(4,128)}, s32[4]{0:T(128)S(1)}, s32[1024]{0:T(1024)S(1)}, f32[7,2048]{1,0:T(8,128)S(1)}, /*index=5*/f32[7,102...) while((s32[]{:T(128)}, f32[4,256,256]{1,0,2:T(4,128)}, ...), condition=%wide.region_3.4_spmd.clone, body=%wide.region_2.3_spmd.clone.sunk | while | flops 583172096 | bytes 9458011 | solution.py:138
  43.5 11.9 %fusion.150 = f32[256,256]{0,1:T(8,128)S(1)} fusion(bf16[2048,256]{1,0:T(8,128)(2,1)} %get-tuple-element.343, f32[256]{0:T(256)S(1)} %bitcast.107, f32[256]{0:T(256)S(1)} %bitcast.99, f32[256]{0:T(256)S(1)} %bitcast.101, f32[2048]{0:T(1024)S(1)} %bitcast.84, f32[2048]{0:T(1024)S(1)} %bitcast.86, f32[2048]{0:T(1024)S(1)} %bitcast.88, ...), kind=kOutput, calls=%fused_computation.30.clone.1 | convolution fusion | flops 291504128 | bytes 1383424 | tf_op jit(solution)/shard_map/while/body/eval_jaxpr/dot_general | solution.py:51
  55.4 10.6 %fusion.151 = f32[256,256]{0,1:T(8,128)S(1)} fusion(bf16[2048,256]{1,0:T(8,128)(2,1)S(1)} %copy-done.2, f32[256]{0:T(256)S(1)} %bitcast.108, f32[256]{0:T(256)S(1)} %bitcast.100, f32[256]{0:T(256)S(1)} %bitcast.102, f32[2048]{0:T(1024)S(1)} %bitcast.85, f32[2048]{0:T(1024)S(1)} %bitcast.87, f32[2048]{0:T(1024)S(1)} %bitcast.89, ...), kind=kOutput, calls=%fused_computation.31.clone.1 | convolution fusion | flops 291504128 | bytes 1383424 | tf_op jit(solution)/shard_map/while/body/eval_jaxpr/dot_general | solution.py:50
  66.4 6.7 %dynamic_update_slice.13 = f32[4,256,256]{1,0,2:T(4,128)} dynamic-update-slice(f32[4,256,256]{1,0,2:T(4,128)} %get-tuple-element.321, f32[1,256,256]{1,0,2:T(1,128)S(1)} %copy.37, s32[]{:T(128)S(6)} %copy.41, s32[]{:T(128)} %constant.159.clone.1..sunk, s32[]{:T(128)} %constant.159.clone.1..sunk) | dynamic-update-slice | bytes 524292 | tf_op jit(solution)/shard_map/while/body/jit(dynamic_update_index_in_dim)/dynamic_update_slice | solution.py:138
  74.5 11.9 %fusion.150 = f32[256,256]{0,1:T(8,128)S(1)} fusion(bf16[2048,256]{1,0:T(8,128)(2,1)} %get-tuple-element.343, f32[256]{0:T(256)S(1)} %bitcast.107, f32[256]{0:T(256)S(1)} %bitcast.99, f32[256]{0:T(256)S(1)} %bitcast.101, f32[2048]{0:T(1024)S(1)} %bitcast.84, f32[2048]{0:T(1024)S(1)} %bitcast.86, f32[2048]{0:T(1024)S(1)} %bitcast.88, ...), kind=kOutput, calls=%fused_computation.30.clone.1 | convolution fusion | flops 291504128 | bytes 1383424 | tf_op jit(solution)/shard_map/while/body/eval_jaxpr/dot_general | solution.py:51
  86.5 10.6 %fusion.151 = f32[256,256]{0,1:T(8,128)S(1)} fusion(bf16[2048,256]{1,0:T(8,128)(2,1)S(1)} %copy-done.2, f32[256]{0:T(256)S(1)} %bitcast.108, f32[256]{0:T(256)S(1)} %bitcast.100, f32[256]{0:T(256)S(1)} %bitcast.102, f32[2048]{0:T(1024)S(1)} %bitcast.85, f32[2048]{0:T(1024)S(1)} %bitcast.87, f32[2048]{0:T(1024)S(1)} %bitcast.89, ...), kind=kOutput, calls=%fused_computation.31.clone.1 | convolution fusion | flops 291504128 | bytes 1383424 | tf_op jit(solution)/shard_map/while/body/eval_jaxpr/dot_general | solution.py:50
  97.4 6.7 %dynamic_update_slice.13 = f32[4,256,256]{1,0,2:T(4,128)} dynamic-update-slice(f32[4,256,256]{1,0,2:T(4,128)} %get-tuple-element.321, f32[1,256,256]{1,0,2:T(1,128)S(1)} %copy.37, s32[]{:T(128)S(6)} %copy.41, s32[]{:T(128)} %constant.159.clone.1..sunk, s32[]{:T(128)} %constant.159.clone.1..sunk) | dynamic-update-slice | bytes 524292 | tf_op jit(solution)/shard_map/while/body/jit(dynamic_update_index_in_dim)/dynamic_update_slice | solution.py:138
  105.6 11.9 %fusion.150 = f32[256,256]{0,1:T(8,128)S(1)} fusion(bf16[2048,256]{1,0:T(8,128)(2,1)} %get-tuple-element.343, f32[256]{0:T(256)S(1)} %bitcast.107, f32[256]{0:T(256)S(1)} %bitcast.99, f32[256]{0:T(256)S(1)} %bitcast.101, f32[2048]{0:T(1024)S(1)} %bitcast.84, f32[2048]{0:T(1024)S(1)} %bitcast.86, f32[2048]{0:T(1024)S(1)} %bitcast.88, ...), kind=kOutput, calls=%fused_computation.30.clone.1 | convolution fusion | flops 291504128 | bytes 1383424 | tf_op jit(solution)/shard_map/while/body/eval_jaxpr/dot_general | solution.py:51
  117.5 10.6 %fusion.151 = f32[256,256]{0,1:T(8,128)S(1)} fusion(bf16[2048,256]{1,0:T(8,128)(2,1)S(1)} %copy-done.2, f32[256]{0:T(256)S(1)} %bitcast.108, f32[256]{0:T(256)S(1)} %bitcast.100, f32[256]{0:T(256)S(1)} %bitcast.102, f32[2048]{0:T(1024)S(1)} %bitcast.85, f32[2048]{0:T(1024)S(1)} %bitcast.87, f32[2048]{0:T(1024)S(1)} %bitcast.89, ...), kind=kOutput, calls=%fused_computation.31.clone.1 | convolution fusion | flops 291504128 | bytes 1383424 | tf_op jit(solution)/shard_map/while/body/eval_jaxpr/dot_general | solution.py:50
  128.5 6.7 %dynamic_update_slice.13 = f32[4,256,256]{1,0,2:T(4,128)} dynamic-update-slice(f32[4,256,256]{1,0,2:T(4,128)} %get-tuple-element.321, f32[1,256,256]{1,0,2:T(1,128)S(1)} %copy.37, s32[]{:T(128)S(6)} %copy.41, s32[]{:T(128)} %constant.159.clone.1..sunk, s32[]{:T(128)} %constant.159.clone.1..sunk) | dynamic-update-slice | bytes 524292 | tf_op jit(solution)/shard_map/while/body/jit(dynamic_update_index_in_dim)/dynamic_update_slice | solution.py:138
  136.6 11.9 %fusion.150 = f32[256,256]{0,1:T(8,128)S(1)} fusion(bf16[2048,256]{1,0:T(8,128)(2,1)} %get-tuple-element.343, f32[256]{0:T(256)S(1)} %bitcast.107, f32[256]{0:T(256)S(1)} %bitcast.99, f32[256]{0:T(256)S(1)} %bitcast.101, f32[2048]{0:T(1024)S(1)} %bitcast.84, f32[2048]{0:T(1024)S(1)} %bitcast.86, f32[2048]{0:T(1024)S(1)} %bitcast.88, ...), kind=kOutput, calls=%fused_computation.30.clone.1 | convolution fusion | flops 291504128 | bytes 1383424 | tf_op jit(solution)/shard_map/while/body/eval_jaxpr/dot_general | solution.py:51
  148.5 10.6 %fusion.151 = f32[256,256]{0,1:T(8,128)S(1)} fusion(bf16[2048,256]{1,0:T(8,128)(2,1)S(1)} %copy-done.2, f32[256]{0:T(256)S(1)} %bitcast.108, f32[256]{0:T(256)S(1)} %bitcast.100, f32[256]{0:T(256)S(1)} %bitcast.102, f32[2048]{0:T(1024)S(1)} %bitcast.85, f32[2048]{0:T(1024)S(1)} %bitcast.87, f32[2048]{0:T(1024)S(1)} %bitcast.89, ...), kind=kOutput, calls=%fused_computation.31.clone.1 | convolution fusion | flops 291504128 | bytes 1383424 | tf_op jit(solution)/shard_map/while/body/eval_jaxpr/dot_general | solution.py:50
  159.5 6.7 %dynamic_update_slice.13 = f32[4,256,256]{1,0,2:T(4,128)} dynamic-update-slice(f32[4,256,256]{1,0,2:T(4,128)} %get-tuple-element.321, f32[1,256,256]{1,0,2:T(1,128)S(1)} %copy.37, s32[]{:T(128)S(6)} %copy.41, s32[]{:T(128)} %constant.159.clone.1..sunk, s32[]{:T(128)} %constant.159.clone.1..sunk) | dynamic-update-slice | bytes 524292 | tf_op jit(solution)/shard_map/while/body/jit(dynamic_update_index_in_dim)/dynamic_update_slice | solution.py:138
  174.8 2.5 %copy.35 = f32[32,8,4,256]{3,1,2,0:T(8,128)} copy(f32[32,8,4,256]{3,2,1,0:T(4,128)} %bitcast.81) | data formatting | bytes 2097152
  178.3 1.4 fusion.95
  179.6 1.6 convolution_add_fusion
  181.3 8.2 %fusion.51 = f32[256,256]{0,1:T(8,128)S(1)} fusion(bf16[2048,256]{1,0:T(8,128)(2,1)S(1)} %copy-done.3, f32[2048]{0:T(1024)S(1)} %bitcast.111, f32[2048]{0:T(1024)S(1)} %bitcast.113, f32[2048]{0:T(1024)S(1)} %bitcast.115, f32[2048]{0:T(1024)S(1)} %bitcast.117, f32[256]{0:T(256)S(1)} %bitcast.149, f32[2048]{0:T(1024)S(1)} %bitcast.119, f32[256]{0:T(256)S(1)} %bitcast.151, ...), kind=kOutput, calls=%fused_computation.78 | convolution fusion | flops 276299776 | bytes 1371136 | tf_op jit(solution)/shard_map/while/body/eval_jaxpr/dot_general | solution.py:51
  189.5 8.4 %fusion.50 = f32[256,256]{0,1:T(8,128)S(1)} fusion(bf16[2048,256]{1,0:T(8,128)(2,1)S(1)} %copy-done.3, f32[2048]{0:T(1024)S(1)} %bitcast.112, f32[2048]{0:T(1024)S(1)} %bitcast.114, f32[2048]{0:T(1024)S(1)} %bitcast.116, f32[2048]{0:T(1024)S(1)} %bitcast.118, f32[256]{0:T(256)S(1)} %bitcast.150, f32[2048]{0:T(1024)S(1)} %bitcast.120, f32[256]{0:T(256)S(1)} %bitcast.152, ...), kind=kOutput, calls=%fused_computation.77 | convolution fusion | flops 275775488 | bytes 1371136 | tf_op jit(solution)/shard_map/while/body/eval_jaxpr/dot_general | solution.py:50
  200.5 4.2 %reduce-scatter.5.cloned.1.call-done = f32[256,256]{0,1:T(8,128)} async-done(((f32[1024,256]{0,1:T(8,128)}), f32[256,256]{0,1:T(8,128)}) %reduce-scatter.5.cloned.1.call-update) | async-done | bytes 262160 | tf_op jit(solution)/shard_map/reduce_scatter | solution.py:137
  206.6 19.4 %reduce-scatter.7.cloned.1.call-done = f32[64,256]{1,0:T(8,128)} async-done(((f32[256,256]{1,0:T(8,128)}), f32[64,256]{1,0:T(8,128)}) %reduce-scatter.7.cloned.1.call-update) | async-done | bytes 65552
  (83 shorter events, 12.7 us)
Async XLA Ops:
  7.2 34.9 %all-gather.2.cloned.1.call-start = ((), (), s32[]{:S(2)}) async-start(), calls=%async_computation.2 | async-start | bytes 1179648 | tf_op jit(solution)/shard_map/all_gather | solution.py:124
  7.9 196.8 %reduce-scatter.5.cloned.1.call-start = ((), (), s32[]{:S(2)}) async-start(), calls=%async_computation.3 | async-start | bytes 1310720 | tf_op jit(solution)/shard_map/reduce_scatter | solution.py:137
  9.8 6.7 %copy-start = (f32[7,256]{1,0:T(8,128)S(1)}, f32[7,256]{1,0:T(8,128)}, u32[]{:S(2)}) copy-start(f32[7,256]{1,0:T(8,128)} %param.10) | copy-start | bytes 21508
  9.8 30.8 %copy-start.4 = (s32[128]{0:T(128)S(1)}, s32[128]{0:T(128)}, u32[]{:S(2)}) copy-start(s32[128]{0:T(128)} %param.13) | copy-start | bytes 1540
  9.8 30.8 %copy-start.5 = (s32[128]{0:T(128)S(1)}, s32[128]{0:T(128)}, u32[]{:S(2)}) copy-start(s32[128]{0:T(128)} %param.14) | copy-start | bytes 1540
  9.8 30.8 %copy-start.1 = (f32[16,256]{1,0:T(8,128)S(1)}, f32[16,256]{1,0:T(8,128)}, u32[]{:S(2)}) copy-start(f32[16,256]{1,0:T(8,128)} %param.12) | copy-start | bytes 49156
  43.5 11.9 %copy-start.2 = (bf16[2048,256]{1,0:T(8,128)(2,1)S(1)}, bf16[2048,256]{1,0:T(8,128)(2,1)}, u32[]{:S(2)}) copy-start(bf16[2048,256]{1,0:T(8,128)(2,1)} %get-tuple-element.343) | copy-start | bytes 3145732 | tf_op jit(solution)/shard_map/while
  74.5 11.9 %copy-start.2 = (bf16[2048,256]{1,0:T(8,128)(2,1)S(1)}, bf16[2048,256]{1,0:T(8,128)(2,1)}, u32[]{:S(2)}) copy-start(bf16[2048,256]{1,0:T(8,128)(2,1)} %get-tuple-element.343) | copy-start | bytes 3145732 | tf_op jit(solution)/shard_map/while
  105.6 11.9 %copy-start.2 = (bf16[2048,256]{1,0:T(8,128)(2,1)S(1)}, bf16[2048,256]{1,0:T(8,128)(2,1)}, u32[]{:S(2)}) copy-start(bf16[2048,256]{1,0:T(8,128)(2,1)} %get-tuple-element.343) | copy-start | bytes 3145732 | tf_op jit(solution)/shard_map/while
  136.6 11.9 %copy-start.2 = (bf16[2048,256]{1,0:T(8,128)(2,1)S(1)}, bf16[2048,256]{1,0:T(8,128)(2,1)}, u32[]{:S(2)}) copy-start(bf16[2048,256]{1,0:T(8,128)(2,1)} %get-tuple-element.343) | copy-start | bytes 3145732 | tf_op jit(solution)/shard_map/while
  174.8 6.5 %copy-start.3 = (bf16[2048,256]{1,0:T(8,128)(2,1)S(1)}, bf16[2048,256]{1,0:T(8,128)(2,1)}, u32[]{:S(2)}) copy-start(bf16[2048,256]{1,0:T(8,128)(2,1)} %get-tuple-element.366) | copy-start | bytes 3145732
  177.3 48.6 %reduce-scatter.7.cloned.1.call-start = ((), (), s32[]{:S(2)}) async-start(), calls=%async_computation.4 | async-start | bytes 327680
  197.9 1.8 copy-start.6
Sparse Core Ops, SparseCore 0:
  9.9 26.1 all-gather.1
  177.5 27.1 reduce-scatter.4
  207.6 18.2 reduce-scatter.6
where the time goes:
time: 234 us; the launch traced here: 233 us
  matrix products  112 us (48%)
  local copies, waits for them, and re-layouts  43.1 us (18%)
  waiting for transfers between devices  24.3 us (10%)
  blocking collectives  24 us (10%)
  between operations  14.3 us (6%)
  loops' own time  11.4 us (5%)
  other arithmetic  3.8 us (2%)
    dot_general x5, matrix products, apply_tile(): second = jnp.dot(t_im, vectors, preferred_element_type=jnp.float32)  55.8 us
    dot_general x5, matrix products, apply_tile(): first = jnp.dot(t_re, vectors, preferred_element_type=jnp.float32)  50.8 us
    dynamic_update_slice x8, local copies, waits for them, and re-layouts, local(): lax.map(one_block, jnp.arange(piece * lax.axis_size('cols') // block, dty...  27.7 us
    unnamed x4, waiting for transfers between devices  20.1 us
    all_gather x1, blocking collectives, local(): row_geom = lax.all_gather(geometry, 'cols', axis=1, tiled=True)  14.8 us
    another operation x1, loops' own time, local(): lax.map(one_block, jnp.arange(piece * lax.axis_size('cols') // block, dty...  11.4 us
    all_gather x1, blocking collectives, local(): col_geom = lax.all_gather(geometry, 'rows', axis=1, tiled=True)  9.22 us
    gather x1, local copies, waits for them, and re-layouts, correction(): nearby = values[index_local]  6.64 us
  transfers between devices with their start and end apart: 3, of which 2 were waited for; matrix products, arithmetic and copies ran while one was open for 15% of the time, Pallas kernels for 0%

commit v1 on v0

v1 whole, which is shorter than its diff:
```python
import functools
import math

import jax
import jax.numpy as jnp
from jax import lax
from jax.experimental import pallas as pl
from jax.experimental.pallas import tpu as pltpu
from jax.sharding import PartitionSpec as P

NS = 64
wavenumber = 20.0
cycle_radius = 0.7
cycle_height = 1.0
four_pi = 4.0 * math.pi
two_pi = 2.0 * math.pi

COARSE_D = (-4.203673078505327, 0.9884209687656514)
COARSE_N = (-2.9883226762430346, 3.1051740325541175)
FINE_D = (-2.7704097493600783, 0.6301024476540067)
FINE_N = (0.21837236917008357, -2.1911377274692434, 1.9795254225510943)
ROUNDER = 12582912.0

turns_sq = (wavenumber / two_pi) ** 2
tile_scale = wavenumber**3 / four_pi / two_pi**2
DEPTH = 48
CHUNK = 256
SUB = 16
BF16 = jnp.bfloat16
F32 = jnp.float32


def half_tangent(turn, fine=False):
    f = turn - ((turn + ROUNDER) - ROUNDER)
    z = f * f
    if fine:
        d = (z + FINE_D[0]) * z + FINE_D[1]
        x = f * ((z * FINE_N[0] + FINE_N[1]) * z + FINE_N[2])
    else:
        d = (z + COARSE_D[0]) * z + COARSE_D[1]
        x = f * (z * COARSE_N[0] + COARSE_N[1])
    return d, x


def cos_sin(turn):
    d, x = half_tangent(turn, fine=True)
    q = 1.0 / (d * d + x * x)
    return (d * d - x * x) * q, 2.0 * d * x * q


def parts(v):
    high = v.astype(BF16).astype(F32)
    rest = v - high
    mid = rest.astype(BF16).astype(F32)
    return high, mid, rest - mid


def column_features(geom_refs, out_s, out_u, out_w, vec):
    at = 0
    for ref in geom_refs:
        g = ref[...]
        piece = g.shape[1]
        where = pl.ds(at, piece)
        x, y, z = g[0:1], g[1:2], g[2:3] - 1.0
        area = g[6:7] * tile_scale
        zero = jnp.zeros((4, piece), F32)
        dot_cn = x * g[3:4] + y * g[4:5] + z * g[5:6]
        vec[0:1], vec[1:2], vec[2:3] = x, y, z
        vec[3:4] = jnp.ones((1, piece), F32)
        vec[4:8] = zero
        vec[4:5] = turns_sq * (x * x + y * y + z * z)
        put_columns(out_s, where, vec[...])
        vec[0:3] = -area * g[3:6]
        vec[3:4] = area * dot_cn
        vec[4:8] = zero
        put_columns(out_u, where, vec[...])
        vec[0:1], vec[1:2], vec[2:3] = area * x, area * y, area * z
        vec[3:4] = area
        put_columns(out_w, where, vec[...])
        at += piece


def put_columns(out, where, v):
    high, mid, low = parts(v)
    out[0:16, where] = jnp.concatenate([high, mid], axis=0).astype(BF16)
    out[16:32, where] = jnp.concatenate([high, low], axis=0).astype(BF16)
    out[32:48, where] = jnp.concatenate([high, mid], axis=0).astype(BF16)


def columns_kernel(count, *refs):
    column_features(refs[:count], *refs[count:])


def row_part(v):
    high, mid, low = parts(v)
    stacked = jnp.concatenate([high, high, mid, high, low, mid], axis=0)
    return stacked.T.astype(BF16)


def row_features(g, dirs, soft_sq, out_s, out_u, out_w, vec, small):
    piece = g.shape[1]
    each = dirs.shape[1]
    x, y, z = g[0:1], g[1:2], g[2:3] - 1.0
    zero = jnp.zeros((4, piece), F32)
    vec[4:8] = zero
    vec[0:1], vec[1:2], vec[2:3] = (-2.0 * turns_sq) * x, (-2.0 * turns_sq) * y, (-2.0 * turns_sq) * z
    vec[3:4] = turns_sq * (x * x + y * y + z * z + soft_sq)
    vec[4:5] = jnp.ones((1, piece), F32)
    out_s[0:piece] = row_part(vec[...])
    vec[0:1], vec[1:2], vec[2:3] = x, y, z
    vec[3:4] = jnp.ones((1, piece), F32)
    vec[4:8] = zero
    out_u[0:piece] = row_part(vec[...])
    vec[0:3] = g[3:6] * (-1.0 / wavenumber)
    vec[3:4] = (x * g[3:4] + y * g[4:5] + z * g[5:6]) * (1.0 / wavenumber)
    out_w[...] = row_part(vec[...])
    small[4:8] = jnp.zeros((4, each), F32)
    small[0:3] = dirs[0:3] * (-wavenumber / two_pi)
    small[3:4] = dirs[2:3] * (-wavenumber / two_pi)
    out_s[piece:] = row_part(small[...])
    small[0:3] = dirs[0:3] * (-wavenumber / tile_scale)
    small[3:4] = jnp.zeros((1, each), F32)
    out_u[piece:] = row_part(small[...])


def panel_entries(s, u, w):
    inverse = lax.rsqrt(s)
    d, x = half_tangent(s * inverse)
    d2, x2 = d * d, x * x
    q = pl.reciprocal((d2 + x2) * s)
    re = (d2 - x2) * q
    h = d * q
    im = (h + h) * x
    p = inverse * (1.0 / two_pi)
    a = p * u + w
    b = u - p * w
    return -(re * a + im * b), re * b - im * a


def far_entries(turn, scale):
    d, x = half_tangent(turn)
    d2, x2 = d * d, x * x
    q = scale * pl.reciprocal(d2 + x2)
    h = d * q
    return (h + h) * x, (x2 - d2) * q


def tiles_kernel(masked, soft_sq, g_ref, dirs_ref, cs, cu, cw, t_re, t_im, rs, ru, rw, vec, small, *bufs):
    piece = g_ref.shape[1]
    rows = t_re.shape[0]
    total = t_re.shape[1]
    row_features(g_ref[...], dirs_ref[...], soft_sq, rs, ru, rw, vec, small)

    def multiply(at, buf):
        where = pl.ds(pl.multiple_of(at * CHUNK, CHUNK), CHUNK)
        for row_ref, col_ref, out in ((rs, cs, buf[0]), (ru, cu, buf[1]), (rw, cw, buf[2])):
            out[...] = jnp.dot(row_ref[...], col_ref[:, where], preferred_element_type=F32)

    def entries(at, buf):
        where = pl.ds(pl.multiple_of(at * CHUNK, CHUNK), CHUNK)
        for begin in range(0, rows, SUB):
            take = pl.ds(begin, SUB)
            if begin < piece:
                re, im = panel_entries(buf[0][take], buf[1][take], buf[2][take])
            else:
                re, im = far_entries(buf[0][take], buf[1][take])
            t_re[take, where] = re.astype(BF16)
            t_im[take, where] = im.astype(BF16)

    first, second = bufs[:3], bufs[3:]
    multiply(0, first)

    def two(step, carry):
        multiply(2 * step + 1, second)
        entries(2 * step, first)
        multiply(jnp.minimum(2 * step + 2, total // CHUNK - 1), first)
        entries(2 * step + 1, second)
        return carry

    lax.fori_loop(0, total // (2 * CHUNK), two, 0)
    if masked:
        for begin in range(0, piece, CHUNK):
            corner = (pl.ds(begin, CHUNK), pl.ds(begin, CHUNK))
            down = lax.broadcasted_iota(jnp.int32, (CHUNK, CHUNK), 0)
            across = lax.broadcasted_iota(jnp.int32, (CHUNK, CHUNK), 1)
            for t in (t_re, t_im):
                held = t[corner].astype(F32)
                t[corner] = jnp.where(down == across, 0.0, held).astype(BF16)


def apply_kernel(count, out_dtype, t_re, t_im, *refs):
    vectors, out = refs[:count], refs[count]
    piece, width = vectors[0].shape
    half = width // 2
    first = jnp.zeros(out.shape, F32)
    second = jnp.zeros(out.shape, F32)
    for at, ref in enumerate(vectors):
        where = pl.ds(at * piece, piece)
        first += jnp.dot(t_re[:, where], ref[...], preferred_element_type=F32)
        second += jnp.dot(t_im[:, where], ref[...], preferred_element_type=F32)
    out[:, :half] = (first[:, :half] - second[:, half:]).astype(out_dtype)
    out[:, half:] = (first[:, half:] + second[:, :half]).astype(out_dtype)


def dot_first(left, right, precision=None):
    return lax.dot_general(
        left, right, (((0,), (0,)), ((), ())), precision=precision, preferred_element_type=F32
    )


def local_kernel(x_ref, g_ref, index_ref, weight_ref, mode_ref, out):
    piece, width = x_ref.shape
    half = width // 2
    count = index_ref.shape[0]
    rows = lax.axis_index("rows")
    cols = lax.axis_index("cols")
    base = (rows * lax.axis_size("cols") + cols) * piece
    ids = lax.broadcasted_iota(jnp.int32, (piece, piece), 0) + base
    m_re = jnp.zeros((piece, piece), F32)
    m_im = jnp.zeros((piece, piece), F32)
    for c in range(count):
        hit = ids == index_ref[c : c + 1]
        m_re += jnp.where(hit, weight_ref[c : c + 1], 0.0)
        m_im += jnp.where(hit, weight_ref[count + c : count + c + 1], 0.0)
    x = x_ref[...]
    first = jnp.zeros((piece, width), F32)
    second = jnp.zeros((piece, width), F32)
    for part in parts(m_re):
        first += dot_first(part.astype(BF16), x)
    for part in parts(m_im):
        second += dot_first(part.astype(BF16), x)
    g = g_ref[...]
    source = lax.broadcasted_iota(jnp.int32, (NS, 1), 0)
    src_cos, src_sin = cos_sin(source.astype(F32) * (1.0 / NS))
    dx = g[0:1] - cycle_radius * src_cos
    dy = g[1:2] - cycle_radius * src_sin
    dz = g[2:3] - cycle_height
    r_sq = dx * dx + dy * dy + dz * dz
    inverse = lax.rsqrt(r_sq)
    c, s = cos_sin(r_sq * inverse * (wavenumber / two_pi))
    g_re = c * inverse * (1.0 / four_pi)
    g_im = s * inverse * (1.0 / four_pi)
    slope = (dx * g[3:4] + dy * g[4:5] + dz * g[5:6]) * inverse
    f_re = 1.0 - slope
    f_im = slope * inverse * (-1.0 / wavenumber)
    h_re = g_re * f_re - g_im * f_im
    h_im = g_re * f_im + g_im * f_re
    turn = lax.rem(source * mode_ref[...], NS).astype(F32) * (1.0 / NS)
    e_re, e_im = cos_sin(turn)
    lhs = jnp.concatenate([h_re, h_im], axis=0)
    rhs = jnp.concatenate(
        [jnp.concatenate([e_re, e_im], axis=1), jnp.concatenate([-e_im, e_re], axis=1)], axis=0
    )
    b = dot_first(lhs, rhs, lax.Precision.HIGHEST)
    xf = x.astype(F32)
    out[:, :half] = b[:, :half] - 0.5 * xf[:, :half] - (first[:, :half] - second[:, half:])
    out[:, half:] = b[:, half:] - 0.5 * xf[:, half:] - (first[:, half:] + second[:, :half])


def final_kernel(count, base, own, *refs):
    got, residual, far = refs[:count], refs[count], refs[count + 1]
    piece = residual.shape[0]
    total = own[...]
    for ref in got:
        total += ref[...].astype(F32)
    residual[...] = base[...] - total[:piece]
    far[...] = total[piece:]


def call(kernel, out_shape, scratch=(), name=None, cost=None):
    return pl.pallas_call(
        kernel,
        out_shape=out_shape,
        scratch_shapes=list(scratch),
        compiler_params=pltpu.CompilerParams(vmem_limit_bytes=40 * 2**20),
        cost_estimate=cost,
        name=name,
    )


def xor_permute(value, axis, mask):
    size = lax.axis_size(axis)
    return lax.ppermute(value, axis, [(i, i ^ mask) for i in range(size)])


def local(krylov, geometry, corr_index, corr_weight, blades, harmonic, observer_angles):
    nrows = lax.axis_size("rows")
    ncols = lax.axis_size("cols")
    row_at = lax.axis_index("rows")
    col_at = lax.axis_index("cols")
    piece, width = krylov.shape
    panels = piece * nrows * ncols
    soft_sq = 4.0 / panels
    each = observer_angles.shape[1] // (nrows * ncols)
    rows = piece + each

    line_masks = list(range(1, ncols))
    plane_masks = list(range(2, nrows, 2))
    geom_line = [geometry] + [xor_permute(geometry, "cols", m) for m in line_masks]
    geom_plane = [geometry] + [xor_permute(geometry, "rows", m) for m in plane_masks]
    geom_other = [xor_permute(g, "rows", 1) for g in geom_line]
    x_line = [krylov] + [xor_permute(krylov, "cols", m) for m in line_masks]
    x_other = [xor_permute(x, "rows", 1) for x in x_line]
    sources = geom_line + geom_other
    vectors = x_line + x_other
    total = len(sources) * piece

    sin_t = jnp.sin(observer_angles[0])
    directions = jnp.stack(
        [sin_t * jnp.cos(observer_angles[1]), sin_t * jnp.sin(observer_angles[1]), jnp.cos(observer_angles[0])]
    )
    directions = directions.reshape(3, nrows * ncols, each).transpose(1, 0, 2)

    modes = (blades * harmonic).reshape(1, -1)
    base = call(local_kernel, jax.ShapeDtypeStruct((piece, width), F32), name="near_and_incident")(
        krylov, geometry, corr_index, corr_weight, modes
    )

    feature = jax.ShapeDtypeStruct((DEPTH, total), BF16)
    columns = call(
        functools.partial(columns_kernel, len(sources)),
        (feature,) * 3,
        [pltpu.VMEM((8, piece), F32)],
        name="column_features",
    )(*sources)

    tile = jax.ShapeDtypeStruct((rows, total), BF16)
    held = []
    for mask, geom in zip([0] + plane_masks, geom_plane):
        at = (row_at ^ mask) * ncols + col_at
        dirs = lax.dynamic_index_in_dim(directions, at, 0, keepdims=False)
        buf = [pltpu.VMEM((rows, CHUNK), F32)] * 2 + [pltpu.VMEM((piece, CHUNK), F32)]
        held.append(
            call(
                functools.partial(tiles_kernel, mask == 0, soft_sq),
                (tile, tile),
                [pltpu.VMEM((rows, DEPTH), BF16)] * 2
                + [pltpu.VMEM((piece, DEPTH), BF16), pltpu.VMEM((8, piece), F32), pltpu.VMEM((8, each), F32)]
                + buf * 2,
                name="tiles",
                cost=pl.CostEstimate(flops=40 * rows * total, bytes_accessed=4 * rows * total, transcendentals=2 * rows * total),
            )(geom, dirs, *columns)
        )

    got = []
    for mask, (t_re, t_im) in list(zip([0] + plane_masks, held))[::-1]:
        dtype = F32 if mask == 0 else BF16
        partial = call(
            functools.partial(apply_kernel, len(vectors), dtype),
            jax.ShapeDtypeStruct((rows, width), dtype),
            name="apply",
            cost=pl.CostEstimate(flops=4 * rows * total * width, bytes_accessed=4 * rows * total, transcendentals=0),
        )(t_re, t_im, *vectors)
        got.append(partial if mask == 0 else xor_permute(partial, "rows", mask))

    return call(
        functools.partial(final_kernel, len(got) - 1),
        (jax.ShapeDtypeStruct((piece, width), F32), jax.ShapeDtypeStruct((each, width), F32)),
        name="combine",
    )(base, got[-1], *got[:-1])


def solution(mesh):
    placed = (
        P(("rows", "cols"), None),
        P(None, ("rows", "cols")),
        P(None, ("rows", "cols")),
        P(None, ("rows", "cols")),
        P(),
        P(),
        P(),
    )
    return jax.shard_map(
        local,
        mesh=mesh,
        in_specs=placed,
        out_specs=(P(("rows", "cols"), None), P(("rows", "cols"), None)),
        check_vma=False,
    )
```

time: 234 us -> 51.4 us (0.22)
  matrix products: 112 us -> 0 us
  local copies, waits for them, and re-layouts: 43.1 us -> 0.97 us
  blocking collectives: 24 us -> 0 us
  Pallas kernels: 0 us -> 22.3 us
  starting transfers between devices: 0.12 us -> 21.1 us
  waiting for transfers between devices: 24.3 us -> 4.37 us
  between operations: 14.3 us -> 0.88 us
  loops' own time: 11.4 us -> 0 us
  other arithmetic: 3.8 us -> 1.38 us
    dot_general x14 -> x0, matrix products: 112 us -> none  [the longest x5 55.8 us: apply_tile(): second = jnp.dot(t_im, vectors, preferred_element_type=jnp.float32)]
    dynamic_update_slice x8 -> x0, local copies, waits for them, and re-layouts: 27.7 us -> none  [local(): lax.map(one_block, jnp.arange(piece * lax.axis_size('cols') // block, dty...]
    all_gather x2 -> x0, blocking collectives: 24 us -> none  [the longest x1 14.8 us: local(): row_geom = lax.all_gather(geometry, 'cols', axis=1, tiled=True)]
    pallas_call x0 -> x11, Pallas kernels: none -> 22.3 us  [the longest x4 16.8 us: local(): call(functools.partial(tiles_kernel, mask == 0, soft_sq), (tile, tile), [...]
    ppermute x0 -> x20, starting transfers between devices: none -> 21.1 us  [xor_permute(): return lax.ppermute(value, axis, [(i, i ^ mask) for i in range(size)])]
    unnamed x4 -> x0, waiting for transfers between devices: 20.1 us -> none
    another operation x1 -> x0, loops' own time: 11.4 us -> none  [local(): lax.map(one_block, jnp.arange(piece * lax.axis_size('cols') // block, dty...]
    gather x1 -> x0, local copies, waits for them, and re-layouts: 6.64 us -> none  [correction(): nearby = values[index_local]]
  transfers between devices with their start and end apart: 3 -> 20, of which waited for: 2 -> 4; matrix products, arithmetic and copies ran while one was open for 15% -> 3% of each run, Pallas kernels for 0% -> 40%
where the time goes in v1:
time: 51.4 us; the launch traced here: 51 us
  Pallas kernels  22.3 us (43%)
  starting transfers between devices  21.1 us (41%)
  waiting for transfers between devices  4.37 us (9%)
  other arithmetic  1.38 us (3%)
  local copies, waits for them, and re-layouts  0.97 us (2%)
  between operations  0.88 us (2%)
    ppermute x20, starting transfers between devices, xor_permute(): return lax.ppermute(value, axis, [(i, i ^ mask) for i in range(size)])  21.1 us
    pallas_call x4, Pallas kernels, local(): call(functools.partial(tiles_kernel, mask == 0, soft_sq), (tile, tile), [...  16.8 us
    ppermute x20, waiting for transfers between devices, xor_permute(): return lax.ppermute(value, axis, [(i, i ^ mask) for i in range(size)])  4.37 us
    pallas_call x4, Pallas kernels, local(): call(functools.partial(apply_kernel, len(vectors), dtype), jax.ShapeDtype...  3.39 us
    mul x1, other arithmetic, local(): sin_t * jnp.cos(observer_angles[1])  1.32 us
    pallas_call x1, Pallas kernels, local(): call(local_kernel, jax.ShapeDtypeStruct((piece, width), F32), name='near_...  1.07 us
  transfers between devices with their start and end apart: 20, of which 4 were waited for; matrix products, arithmetic and copies ran while one was open for 3% of the time, Pallas kernels for 40%

profile of v1, /device:TPU:0, one launch (start us, length us, event | category | flops | bytes accessed | tf_op | source)
XLA Modules:
  0.0 51.0 jit_solution(11199186493731699341)
XLA Ops:
  0.6 3.1 %collective-permute-start = (f32[7,256]{1,0:T(8,128)}, f32[7,256]{1,0:T(8,128)S(1)}, u32[]{:S(2)}, u32[]{:S(2)}) collective-permute-start(f32[7,256]{1,0:T(8,128)} %g_ref.3), channel_id=1, source_target_pairs={{0,1},{1,0},{2,3},{3,2},{4,5},{5,4},{6,7},{7,6},{8,9},{9,8},{10,11... | collective-permute-start | bytes 21512 | tf_op jit(solution)/shard_map/ppermute | solution.py:283
  3.7 2.6 %collective-permute-start.1 = (f32[7,256]{1,0:T(8,128)}, f32[7,256]{1,0:T(8,128)S(1)}, u32[]{:S(2)}, u32[]{:S(2)}) collective-permute-start(f32[7,256]{1,0:T(8,128)} %g_ref.3), channel_id=1, source_target_pairs={{0,2},{1,3},{2,0},{3,1},{4,6},{5,7},{6,4},{7,5},{8,10},{9,11},{10,... | collective-permute-start | bytes 21512 | tf_op jit(solution)/shard_map/ppermute | solution.py:283
  6.3 0.9 %collective-permute-start.7 = (bf16[256,256]{1,0:T(8,128)(2,1)}, bf16[256,256]{1,0:T(8,128)(2,1)S(1)}, u32[]{:S(2)}, u32[]{:S(2)}) collective-permute-start(bf16[256,256]{1,0:T(8,128)(2,1)} %refs_0_.9), channel_id=1, source_target_pairs={{0,1},{1,0},{2,3},{3,2},{4,5},{5,4},{6,7},{7,6},{8,9},{9,8},{10,11... | collective-permute-start | bytes 393224 | tf_op jit(solution)/shard_map/ppermute | solution.py:283
  7.2 3.5 %collective-permute-start.8 = (bf16[256,256]{1,0:T(8,128)(2,1)}, bf16[256,256]{1,0:T(8,128)(2,1)S(1)}, u32[]{:S(2)}, u32[]{:S(2)}) collective-permute-start(bf16[256,256]{1,0:T(8,128)(2,1)} %refs_0_.9), channel_id=1, source_target_pairs={{0,2},{1,3},{2,0},{3,1},{4,6},{5,7},{6,4},{7,5},{8,10},{9,11},{10,... | collective-permute-start | bytes 393224 | tf_op jit(solution)/shard_map/ppermute | solution.py:283
  11.0 1.2 %collective-permute-done.2.refs_3_ = f32[7,256]{1,0:T(8,128)S(1)} collective-permute-done((f32[7,256]{1,0:T(8,128)}, f32[7,256]{1,0:T(8,128)S(1)}, u32[]{:S(2)}, u32[]{:S(2)}) %collective-permute-start.2) | collective-permute-done | bytes 7200 | tf_op jit(solution)/shard_map/ppermute | solution.py:283
  12.2 1.5 %collective-permute-start.18 = (f32[7,256]{1,0:T(8,128)}, f32[7,256]{1,0:T(8,128)S(1)}, u32[]{:S(2)}, u32[]{:S(2)}) collective-permute-start(f32[7,256]{1,0:T(8,128)} %g_ref.3), channel_id=1, source_target_pairs={{0,8},{4,12},{8,0},{12,4},{16,24},{20,28},{24,16},{28,20},{1,9},{5... | collective-permute-start | bytes 21512 | tf_op jit(solution)/shard_map/ppermute | solution.py:283
  13.6 1.5 %collective-permute-start.16 = (f32[7,256]{1,0:T(8,128)}, f32[7,256]{1,0:T(8,128)S(1)}, u32[]{:S(2)}, u32[]{:S(2)}) collective-permute-start(f32[7,256]{1,0:T(8,128)} %g_ref.3), channel_id=1, source_target_pairs={{0,16},{4,20},{8,24},{12,28},{16,0},{20,4},{24,8},{28,12},{1,17},{... | collective-permute-start | bytes 21512 | tf_op jit(solution)/shard_map/ppermute | solution.py:283
  15.2 0.8 %collective-permute-done.18.g_ref = f32[7,256]{1,0:T(8,128)S(1)} collective-permute-done((f32[7,256]{1,0:T(8,128)}, f32[7,256]{1,0:T(8,128)S(1)}, u32[]{:S(2)}, u32[]{:S(2)}) %collective-permute-start.18) | collective-permute-done | bytes 7200 | tf_op jit(solution)/shard_map/ppermute | solution.py:283
  16.0 1.5 %collective-permute-done.16.g_ref = f32[7,256]{1,0:T(8,128)S(1)} collective-permute-done((f32[7,256]{1,0:T(8,128)}, f32[7,256]{1,0:T(8,128)S(1)}, u32[]{:S(2)}, u32[]{:S(2)}) %collective-permute-start.16) | collective-permute-done | bytes 7200 | tf_op jit(solution)/shard_map/ppermute | solution.py:283
  17.5 1.3 %multiply_reduce_fusion.1 = (f32[2048]{0:T(1024)S(1)}, f32[2048]{0:T(1024)S(1)}, f32[2048]{0:T(1024)S(1)}) fusion(f32[2,2048]{1,0:T(2,128)} %param.13), kind=kLoop, calls=%fused_computation.3 | loop fusion | flops 4096 | bytes 40960 | tf_op jit(solution)/shard_map/mul | solution.py:310
  20.1 0.8 %collective-permute-done.8.refs_2_ = bf16[256,256]{1,0:T(8,128)(2,1)S(1)} collective-permute-done((bf16[256,256]{1,0:T(8,128)(2,1)}, bf16[256,256]{1,0:T(8,128)(2,1)S(1)}, u32[]{:S(2)}, u32[]{:S(2)}) %collective-permute-start.8) | collective-permute-done | bytes 131104 | tf_op jit(solution)/shard_map/ppermute | solution.py:283
  21.5 2.5 %collective-permute-start.14 = (f32[7,256]{1,0:T(8,128)}, f32[7,256]{1,0:T(8,128)S(1)}, u32[]{:S(2)}, u32[]{:S(2)}) collective-permute-start(f32[7,256]{1,0:T(8,128)} %g_ref.3), channel_id=1, source_target_pairs={{0,24},{4,28},{8,16},{12,20},{16,8},{20,12},{24,0},{28,4},{1,25},{... | collective-permute-start | bytes 21512 | tf_op jit(solution)/shard_map/ppermute | solution.py:283
  24.0 0.7 %copy-done.1 = f32[7,256]{1,0:T(8,128)S(1)} copy-done((f32[7,256]{1,0:T(8,128)S(1)}, f32[7,256]{1,0:T(8,128)}, u32[]{:S(2)}) %copy-start.1) | copy-done | bytes 7192
  24.9 4.2 %tiles.7 = (bf16[320,2048]{1,0:T(8,128)(2,1)S(1)}, bf16[320,2048]{1,0:T(8,128)(2,1)S(1)}) custom-call(f32[7,256]{1,0:T(8,128)S(1)} %collective-permute-done.18.g_ref, f32[3,64]{1,0:T(4,128)S(1)} %get-tuple-element.27.dirs_ref, bf16[48,2048]{1,0:T(8,128)(2,1)S(1)} %get-tuple-element.13.cs, bf16[48,2048]{1,0:T(8,128)(2,1)S(1)} %get-tuple-element.14.cu, ...), custom_call_target="tpu_custom_call" | custom-call | flops 26214400 | bytes 2621440 | tf_op jit(solution)/shard_map/tiles/pallas_call | solution.py:334
  29.1 4.2 %tiles.6 = (bf16[320,2048]{1,0:T(8,128)(2,1)S(1)}, bf16[320,2048]{1,0:T(8,128)(2,1)S(1)}) custom-call(f32[7,256]{1,0:T(8,128)S(1)} %collective-permute-done.16.g_ref, f32[3,64]{1,0:T(4,128)S(1)} %get-tuple-element.28.dirs_ref, bf16[48,2048]{1,0:T(8,128)(2,1)S(1)} %get-tuple-element.13.cs, bf16[48,2048]{1,0:T(8,128)(2,1)S(1)} %get-tuple-element.14.cu, ...), custom_call_target="tpu_custom_call" | custom-call | flops 26214400 | bytes 2621440 | tf_op jit(solution)/shard_map/tiles/pallas_call | solution.py:334
  33.4 4.2 %tiles.5 = (bf16[320,2048]{1,0:T(8,128)(2,1)S(1)}, bf16[320,2048]{1,0:T(8,128)(2,1)S(1)}) custom-call(f32[7,256]{1,0:T(8,128)S(1)} %collective-permute-done.14.g_ref, f32[3,64]{1,0:T(4,128)S(1)} %get-tuple-element.29.dirs_ref, bf16[48,2048]{1,0:T(8,128)(2,1)S(1)} %get-tuple-element.13.cs, bf16[48,2048]{1,0:T(8,128)(2,1)S(1)} %get-tuple-element.14.cu, ...), custom_call_target="tpu_custom_call" | custom-call | flops 26214400 | bytes 2621440 | tf_op jit(solution)/shard_map/tiles/pallas_call | solution.py:334
  37.6 0.8 %apply.7 = bf16[320,256]{1,0:T(8,128)(2,1)S(1)} custom-call(bf16[320,2048]{1,0:T(8,128)(2,1)S(1)} %get-tuple-element.22.t_re, bf16[320,2048]{1,0:T(8,128)(2,1)S(1)} %get-tuple-element.23.t_im, bf16[256,256]{1,0:T(8,128)(2,1)S(1)} %copy-done, bf16[256,256]{1,0:T(8,128)(2,1)S(1)} %collective-permute-done.7.refs_1_, ...), custom_call_target="tpu_custom_call" | custom-call | flops 671088640 | bytes 2621440 | tf_op jit(solution)/shard_map/apply/pallas_call | solution.py:348
  39.1 0.8 %apply.6 = bf16[320,256]{1,0:T(8,128)(2,1)S(1)} custom-call(bf16[320,2048]{1,0:T(8,128)(2,1)S(1)} %get-tuple-element.20.t_re, bf16[320,2048]{1,0:T(8,128)(2,1)S(1)} %get-tuple-element.21.t_im, bf16[256,256]{1,0:T(8,128)(2,1)S(1)} %copy-done, bf16[256,256]{1,0:T(8,128)(2,1)S(1)} %collective-permute-done.7.refs_1_, ...), custom_call_target="tpu_custom_call" | custom-call | flops 671088640 | bytes 2621440 | tf_op jit(solution)/shard_map/apply/pallas_call | solution.py:348
  40.5 0.8 %apply.5 = bf16[320,256]{1,0:T(8,128)(2,1)S(1)} custom-call(bf16[320,2048]{1,0:T(8,128)(2,1)S(1)} %get-tuple-element.18.t_re, bf16[320,2048]{1,0:T(8,128)(2,1)S(1)} %get-tuple-element.19.t_im, bf16[256,256]{1,0:T(8,128)(2,1)S(1)} %copy-done, bf16[256,256]{1,0:T(8,128)(2,1)S(1)} %collective-permute-done.7.refs_1_, ...), custom_call_target="tpu_custom_call" | custom-call | flops 671088640 | bytes 2621440 | tf_op jit(solution)/shard_map/apply/pallas_call | solution.py:348
  41.4 2.5 %collective-permute-start.15 = (bf16[320,256]{1,0:T(8,128)(2,1)S(1)}, bf16[320,256]{1,0:T(8,128)(2,1)S(1)}, u32[]{:S(2)}, u32[]{:S(2)}) collective-permute-start(bf16[320,256]{1,0:T(8,128)(2,1)S(1)} %apply.5), channel_id=1, source_target_pairs={{0,24},{4,28},{8,16},{12,20},{16,8},{20,12},{24,0},{28,4},{1,25},{... | collective-permute-start | bytes 491528 | tf_op jit(solution)/shard_map/ppermute | solution.py:283
  43.9 1.1 %near_and_incident.1.base = f32[256,256]{1,0:T(8,128)S(1)} custom-call(bf16[256,256]{1,0:T(8,128)(2,1)S(1)} %copy-done, f32[7,256]{1,0:T(8,128)S(1)} %copy-done.2, s32[8,256]{1,0:T(8,128)S(1)} %copy-done.4, f32[16,256]{1,0:T(8,128)S(1)} %copy-done.3, s32[1,128]{1,0:T(1,128)S(1)} %multiply_bitcast_fusion.mode_ref), custom_call_target="tpu_custom_call" | custom-call | tf_op jit(solution)/shard_map/near_and_incident/pallas_call | solution.py:315
  45.0 4.2 %tiles.4 = (bf16[320,2048]{1,0:T(8,128)(2,1)S(1)}, bf16[320,2048]{1,0:T(8,128)(2,1)S(1)}) custom-call(f32[7,256]{1,0:T(8,128)S(1)} %copy-done.2, f32[3,64]{1,0:T(4,128)S(1)} %get-tuple-element.30.dirs_ref, bf16[48,2048]{1,0:T(8,128)(2,1)S(1)} %get-tuple-element.13.cs, bf16[48,2048]{1,0:T(8,128)(2,1)S(1)} %get-tuple-element.14.cu, ...), custom_call_target="tpu_custom_call" | custom-call | flops 26214400 | bytes 2621440 | tf_op jit(solution)/shard_map/tiles/pallas_call | solution.py:334
  49.3 0.8 %apply.4.own = f32[320,256]{1,0:T(8,128)S(1)} custom-call(bf16[320,2048]{1,0:T(8,128)(2,1)S(1)} %get-tuple-element.16.t_re, bf16[320,2048]{1,0:T(8,128)(2,1)S(1)} %get-tuple-element.17.t_im, bf16[256,256]{1,0:T(8,128)(2,1)S(1)} %copy-done, bf16[256,256]{1,0:T(8,128)(2,1)S(1)} %collective-permute-done.7.refs_1_, ...), custom_call_target="tpu_custom_call" | custom-call | flops 671088640 | bytes 2621440 | tf_op jit(solution)/shard_map/apply/pallas_call | solution.py:348
  50.1 0.8 %combine.1 = (f32[256,256]{1,0:T(8,128)}, f32[64,256]{1,0:T(8,128)}) custom-call(f32[256,256]{1,0:T(8,128)S(1)} %near_and_incident.1.base, f32[320,256]{1,0:T(8,128)S(1)} %apply.4.own, bf16[320,256]{1,0:T(8,128)(2,1)S(1)} %collective-permute-done.15.refs_0_, bf16[320,256]{1,0:T(8,128)(2,1)S(1)} %collective-permute-done.17.refs_1_, ...), custom_call_target="tpu_custom_call" | custom-call | tf_op jit(solution)/shard_map/combine/pallas_call | solution.py:356
  (48 shorter events, 3.5 us)
Async XLA Ops:
  0.6 6.6 %collective-permute-start = (f32[7,256]{1,0:T(8,128)}, f32[7,256]{1,0:T(8,128)S(1)}, u32[]{:S(2)}, u32[]{:S(2)}) collective-permute-start(f32[7,256]{1,0:T(8,128)} %g_ref.3), channel_id=1, source_target_pairs={{0,1},{1,0},{2,3},{3,2},{4,5},{5,4},{6,7},{7,6},{8,9},{9,8},{10,11... | collective-permute-start | bytes 21512 | tf_op jit(solution)/shard_map/ppermute | solution.py:283
  3.7 7.0 %collective-permute-start.1 = (f32[7,256]{1,0:T(8,128)}, f32[7,256]{1,0:T(8,128)S(1)}, u32[]{:S(2)}, u32[]{:S(2)}) collective-permute-start(f32[7,256]{1,0:T(8,128)} %g_ref.3), channel_id=1, source_target_pairs={{0,2},{1,3},{2,0},{3,1},{4,6},{5,7},{6,4},{7,5},{8,10},{9,11},{10,... | collective-permute-start | bytes 21512 | tf_op jit(solution)/shard_map/ppermute | solution.py:283
  6.3 5.8 %collective-permute-start.2 = (f32[7,256]{1,0:T(8,128)}, f32[7,256]{1,0:T(8,128)S(1)}, u32[]{:S(2)}, u32[]{:S(2)}) collective-permute-start(f32[7,256]{1,0:T(8,128)} %g_ref.3), channel_id=1, source_target_pairs={{0,3},{1,2},{2,1},{3,0},{4,7},{5,6},{6,5},{7,4},{8,11},{9,10},{10,... | collective-permute-start | bytes 21512 | tf_op jit(solution)/shard_map/ppermute | solution.py:283
  6.3 7.3 %collective-permute-start.3 = (f32[7,256]{1,0:T(8,128)}, f32[7,256]{1,0:T(8,128)S(1)}, u32[]{:S(2)}, u32[]{:S(2)}) collective-permute-start(f32[7,256]{1,0:T(8,128)} %g_ref.3), channel_id=1, source_target_pairs={{0,4},{4,0},{8,12},{12,8},{16,20},{20,16},{24,28},{28,24},{1,5},{5... | collective-permute-start | bytes 21512 | tf_op jit(solution)/shard_map/ppermute | solution.py:283
  6.3 13.3 %collective-permute-start.7 = (bf16[256,256]{1,0:T(8,128)(2,1)}, bf16[256,256]{1,0:T(8,128)(2,1)S(1)}, u32[]{:S(2)}, u32[]{:S(2)}) collective-permute-start(bf16[256,256]{1,0:T(8,128)(2,1)} %refs_0_.9), channel_id=1, source_target_pairs={{0,1},{1,0},{2,3},{3,2},{4,5},{5,4},{6,7},{7,6},{8,9},{9,8},{10,11... | collective-permute-start | bytes 393224 | tf_op jit(solution)/shard_map/ppermute | solution.py:283
  7.2 13.7 %collective-permute-start.8 = (bf16[256,256]{1,0:T(8,128)(2,1)}, bf16[256,256]{1,0:T(8,128)(2,1)S(1)}, u32[]{:S(2)}, u32[]{:S(2)}) collective-permute-start(bf16[256,256]{1,0:T(8,128)(2,1)} %refs_0_.9), channel_id=1, source_target_pairs={{0,2},{1,3},{2,0},{3,1},{4,6},{5,7},{6,4},{7,5},{8,10},{9,11},{10,... | collective-permute-start | bytes 393224 | tf_op jit(solution)/shard_map/ppermute | solution.py:283
  10.7 10.2 %collective-permute-start.9 = (bf16[256,256]{1,0:T(8,128)(2,1)}, bf16[256,256]{1,0:T(8,128)(2,1)S(1)}, u32[]{:S(2)}, u32[]{:S(2)}) collective-permute-start(bf16[256,256]{1,0:T(8,128)(2,1)} %refs_0_.9), channel_id=1, source_target_pairs={{0,3},{1,2},{2,1},{3,0},{4,7},{5,6},{6,5},{7,4},{8,11},{9,10},{10,... | collective-permute-start | bytes 393224 | tf_op jit(solution)/shard_map/ppermute | solution.py:283
  12.2 3.9 %collective-permute-start.18 = (f32[7,256]{1,0:T(8,128)}, f32[7,256]{1,0:T(8,128)S(1)}, u32[]{:S(2)}, u32[]{:S(2)}) collective-permute-start(f32[7,256]{1,0:T(8,128)} %g_ref.3), channel_id=1, source_target_pairs={{0,8},{4,12},{8,0},{12,4},{16,24},{20,28},{24,16},{28,20},{1,9},{5... | collective-permute-start | bytes 21512 | tf_op jit(solution)/shard_map/ppermute | solution.py:283
  13.6 3.9 %collective-permute-start.16 = (f32[7,256]{1,0:T(8,128)}, f32[7,256]{1,0:T(8,128)S(1)}, u32[]{:S(2)}, u32[]{:S(2)}) collective-permute-start(f32[7,256]{1,0:T(8,128)} %g_ref.3), channel_id=1, source_target_pairs={{0,16},{4,20},{8,24},{12,28},{16,0},{20,4},{24,8},{28,12},{1,17},{... | collective-permute-start | bytes 21512 | tf_op jit(solution)/shard_map/ppermute | solution.py:283
  16.0 3.0 %collective-permute-start.4 = (f32[7,256]{1,0:T(8,128)S(1)}, f32[7,256]{1,0:T(8,128)S(1)}, u32[]{:S(2)}, u32[]{:S(2)}) collective-permute-start(f32[7,256]{1,0:T(8,128)S(1)} %collective-permute-done.refs_1_), channel_id=1, source_target_pairs={{0,4},{4,0},{8,12},{12,8},{16,20},{20,16},{24,28},{28,24},{1,5},{5... | collective-permute-start | bytes 21512 | tf_op jit(solution)/shard_map/ppermute | solution.py:283
  17.5 2.1 %collective-permute-start.5 = (f32[7,256]{1,0:T(8,128)S(1)}, f32[7,256]{1,0:T(8,128)S(1)}, u32[]{:S(2)}, u32[]{:S(2)}) collective-permute-start(f32[7,256]{1,0:T(8,128)S(1)} %collective-permute-done.1.refs_2_), channel_id=1, source_target_pairs={{0,4},{4,0},{8,12},{12,8},{16,20},{20,16},{24,28},{28,24},{1,5},{5... | collective-permute-start | bytes 21512 | tf_op jit(solution)/shard_map/ppermute | solution.py:283
  19.1 18.5 %collective-permute-start.10 = (bf16[256,256]{1,0:T(8,128)(2,1)}, bf16[256,256]{1,0:T(8,128)(2,1)S(1)}, u32[]{:S(2)}, u32[]{:S(2)}) collective-permute-start(bf16[256,256]{1,0:T(8,128)(2,1)} %refs_0_.9), channel_id=1, source_target_pairs={{0,4},{4,0},{8,12},{12,8},{16,20},{20,16},{24,28},{28,24},{1,5},{5... | collective-permute-start | bytes 393224 | tf_op jit(solution)/shard_map/ppermute | solution.py:283
  19.6 1.9 %collective-permute-start.6 = (f32[7,256]{1,0:T(8,128)S(1)}, f32[7,256]{1,0:T(8,128)S(1)}, u32[]{:S(2)}, u32[]{:S(2)}) collective-permute-start(f32[7,256]{1,0:T(8,128)S(1)} %collective-permute-done.2.refs_3_), channel_id=1, source_target_pairs={{0,4},{4,0},{8,12},{12,8},{16,20},{20,16},{24,28},{28,24},{1,5},{5... | collective-permute-start | bytes 21512 | tf_op jit(solution)/shard_map/ppermute | solution.py:283
  19.7 17.9 %collective-permute-start.11 = (bf16[256,256]{1,0:T(8,128)(2,1)S(1)}, bf16[256,256]{1,0:T(8,128)(2,1)S(1)}, u32[]{:S(2)}, u32[]{:S(2)}) collective-permute-start(bf16[256,256]{1,0:T(8,128)(2,1)S(1)} %collective-permute-done.7.refs_1_), channel_id=1, source_target_pairs={{0,4},{4,0},{8,12},{12,8},{16,20},{20,16},{24,28},{28,24},{1,5},{5... | collective-permute-start | bytes 393224 | tf_op jit(solution)/shard_map/ppermute | solution.py:283
  20.9 16.7 %collective-permute-start.12 = (bf16[256,256]{1,0:T(8,128)(2,1)S(1)}, bf16[256,256]{1,0:T(8,128)(2,1)S(1)}, u32[]{:S(2)}, u32[]{:S(2)}) collective-permute-start(bf16[256,256]{1,0:T(8,128)(2,1)S(1)} %collective-permute-done.8.refs_2_), channel_id=1, source_target_pairs={{0,4},{4,0},{8,12},{12,8},{16,20},{20,16},{24,28},{28,24},{1,5},{5... | collective-permute-start | bytes 393224 | tf_op jit(solution)/shard_map/ppermute | solution.py:283
  20.9 16.7 %collective-permute-start.13 = (bf16[256,256]{1,0:T(8,128)(2,1)S(1)}, bf16[256,256]{1,0:T(8,128)(2,1)S(1)}, u32[]{:S(2)}, u32[]{:S(2)}) collective-permute-start(bf16[256,256]{1,0:T(8,128)(2,1)S(1)} %collective-permute-done.9.refs_3_), channel_id=1, source_target_pairs={{0,4},{4,0},{8,12},{12,8},{16,20},{20,16},{24,28},{28,24},{1,5},{5... | collective-permute-start | bytes 393224 | tf_op jit(solution)/shard_map/ppermute | solution.py:283
  21.5 11.9 %collective-permute-start.14 = (f32[7,256]{1,0:T(8,128)}, f32[7,256]{1,0:T(8,128)S(1)}, u32[]{:S(2)}, u32[]{:S(2)}) collective-permute-start(f32[7,256]{1,0:T(8,128)} %g_ref.3), channel_id=1, source_target_pairs={{0,24},{4,28},{8,16},{12,20},{16,8},{20,12},{24,0},{28,4},{1,25},{... | collective-permute-start | bytes 21512 | tf_op jit(solution)/shard_map/ppermute | solution.py:283
  33.3 4.3 %copy-start = (bf16[256,256]{1,0:T(8,128)(2,1)S(1)}, bf16[256,256]{1,0:T(8,128)(2,1)}, u32[]{:S(2)}) copy-start(bf16[256,256]{1,0:T(8,128)(2,1)} %refs_0_.9) | copy-start | bytes 393220
  38.5 11.6 %collective-permute-start.19 = (bf16[320,256]{1,0:T(8,128)(2,1)S(1)}, bf16[320,256]{1,0:T(8,128)(2,1)S(1)}, u32[]{:S(2)}, u32[]{:S(2)}) collective-permute-start(bf16[320,256]{1,0:T(8,128)(2,1)S(1)} %apply.7), channel_id=1, source_target_pairs={{0,8},{4,12},{8,0},{12,4},{16,24},{20,28},{24,16},{28,20},{1,9},{5... | collective-permute-start | bytes 491528 | tf_op jit(solution)/shard_map/ppermute | solution.py:283
  39.9 10.2 %collective-permute-start.17 = (bf16[320,256]{1,0:T(8,128)(2,1)S(1)}, bf16[320,256]{1,0:T(8,128)(2,1)S(1)}, u32[]{:S(2)}, u32[]{:S(2)}) collective-permute-start(bf16[320,256]{1,0:T(8,128)(2,1)S(1)} %apply.6), channel_id=1, source_target_pairs={{0,16},{4,20},{8,24},{12,28},{16,0},{20,4},{24,8},{28,12},{1,17},{... | collective-permute-start | bytes 491528 | tf_op jit(solution)/shard_map/ppermute | solution.py:283
  40.5 3.4 %copy-start.2 = (f32[7,256]{1,0:T(8,128)S(1)}, f32[7,256]{1,0:T(8,128)}, u32[]{:S(2)}) copy-start(f32[7,256]{1,0:T(8,128)} %g_ref.3) | copy-start | bytes 21508
  40.5 3.4 %copy-start.3 = (f32[16,256]{1,0:T(8,128)S(1)}, f32[16,256]{1,0:T(8,128)}, u32[]{:S(2)}) copy-start(f32[16,256]{1,0:T(8,128)} %weight_ref.1) | copy-start | bytes 49156
  40.5 3.4 %copy-start.4 = (s32[8,256]{1,0:T(8,128)S(1)}, s32[8,256]{1,0:T(8,128)}, u32[]{:S(2)}) copy-start(s32[8,256]{1,0:T(8,128)} %index_ref.1) | copy-start | bytes 24580
  41.4 8.7 %collective-permute-start.15 = (bf16[320,256]{1,0:T(8,128)(2,1)S(1)}, bf16[320,256]{1,0:T(8,128)(2,1)S(1)}, u32[]{:S(2)}, u32[]{:S(2)}) collective-permute-start(bf16[320,256]{1,0:T(8,128)(2,1)S(1)} %apply.5), channel_id=1, source_target_pairs={{0,24},{4,28},{8,16},{12,20},{16,8},{20,12},{24,0},{28,4},{1,25},{... | collective-permute-start | bytes 491528 | tf_op jit(solution)/shard_map/ppermute | solution.py:283
  (3 other events, 7.5 us)

commit v2 on v1

v2 whole, which is shorter than its diff:
```python
import functools
import math

import jax
import jax.numpy as jnp
from jax import lax
from jax.experimental import pallas as pl
from jax.experimental.pallas import tpu as pltpu
from jax.sharding import PartitionSpec as P

NS = 64
wavenumber = 20.0
cycle_radius = 0.7
cycle_height = 1.0
four_pi = 4.0 * math.pi
two_pi = 2.0 * math.pi

COARSE_D = (-4.203673078505327, 0.9884209687656514)
COARSE_N = (-2.9883226762430346, 3.1051740325541175)
FINE_D = (-2.7704097493600783, 0.6301024476540067)
FINE_N = (0.21837236917008357, -2.1911377274692434, 1.9795254225510943)
ROUNDER = 12582912.0

turns_sq = (wavenumber / two_pi) ** 2
tile_scale = wavenumber**3 / four_pi / two_pi**2
DEPTH = 48
CHUNK = 256
SUB = 16
BF16 = jnp.bfloat16
F32 = jnp.float32


def half_tangent(turn, fine=False):
    f = turn - ((turn + ROUNDER) - ROUNDER)
    z = f * f
    if fine:
        d = (z + FINE_D[0]) * z + FINE_D[1]
        x = f * ((z * FINE_N[0] + FINE_N[1]) * z + FINE_N[2])
    else:
        d = (z + COARSE_D[0]) * z + COARSE_D[1]
        x = f * (z * COARSE_N[0] + COARSE_N[1])
    return d, x


def cos_sin(turn):
    d, x = half_tangent(turn, fine=True)
    q = 1.0 / (d * d + x * x)
    return (d * d - x * x) * q, 2.0 * d * x * q


def parts(v):
    high = v.astype(BF16).astype(F32)
    rest = v - high
    mid = rest.astype(BF16).astype(F32)
    return high, mid, rest - mid


def payload_kernel(masks, x_hbm, g_hbm, angle_hbm, out, dirs_out, vec, x_buf, angles, sem):
    piece = x_hbm.shape[0]
    each = angles.shape[1] // (lax.axis_size("rows") * lax.axis_size("cols"))
    copies = [
        pltpu.make_async_copy(src, dst, sem.at[i])
        for i, (src, dst) in enumerate(((g_hbm, vec), (angle_hbm, angles), (x_hbm, x_buf)))
    ]
    for copy in copies:
        copy.start()
    copies[0].wait()
    g = jnp.concatenate([vec[...], jnp.zeros((1, vec.shape[1]), F32)], axis=0)
    high, mid, low = parts(g)
    out[piece : piece + 16] = jnp.concatenate([high, mid], axis=0).astype(BF16)
    out[piece + 16 : piece + 32] = jnp.concatenate([low, jnp.zeros_like(low)], axis=0).astype(BF16)
    copies[1].wait()
    dirs_out[...] = jnp.zeros_like(dirs_out)
    for i, mask in enumerate(masks):
        owner = (lax.axis_index("rows") ^ mask) * lax.axis_size("cols") + lax.axis_index("cols")
        for j, value in enumerate(directions(angles, owner, each)):
            dirs_out[8 * i + j : 8 * i + j + 1] = value
    copies[2].wait()
    out[0:piece] = x_buf[...]


def shard_features(shard, at, out_s, out_u, out_w, out_x, vec):
    piece = shard.shape[0] - 32
    half = out_x.shape[1] // 2
    x = shard[0:piece]
    out_x[2 * at * piece : (2 * at + 1) * piece] = x
    turned = jnp.concatenate([-x[:, half:], x[:, :half]], axis=1)
    out_x[(2 * at + 1) * piece : (2 * at + 2) * piece] = turned
    held = shard[piece : piece + 32].astype(F32)
    g = held[0:8] + held[8:16] + held[16:24]
    where = pl.ds(at * piece, piece)
    x, y, z = g[0:1], g[1:2], g[2:3] - 1.0
    area = g[6:7] * tile_scale
    zero = jnp.zeros((4, piece), F32)
    vec[0:1], vec[1:2], vec[2:3] = x, y, z
    vec[3:4] = jnp.ones((1, piece), F32)
    vec[4:8] = zero
    vec[4:5] = turns_sq * (x * x + y * y + z * z)
    put_columns(out_s, where, vec[...])
    vec[0:3] = area * g[3:6]
    vec[3:4] = -area * (x * g[3:4] + y * g[4:5] + z * g[5:6])
    vec[4:8] = zero
    put_columns(out_u, where, vec[...])
    vec[0:1], vec[1:2], vec[2:3] = area * x, area * y, area * z
    vec[3:4] = area
    put_columns(out_w, where, vec[...])


def pack_kernel(count, *refs):
    packed = refs[count]
    size = refs[0].shape[0]
    for at in range(count):
        packed[at * size : (at + 1) * size] = refs[at][...]


def columns_kernel(size, count, *refs):
    shards = []
    for ref in refs[:count]:
        shards += [ref.at[at : at + size] for at in range(0, ref.shape[0], size)]
    for at, shard in enumerate(shards):
        shard_features(shard, at, *refs[count:])


def put_columns(out, where, v):
    high, mid, low = parts(v)
    out[0:16, where] = jnp.concatenate([high, mid], axis=0).astype(BF16)
    out[16:32, where] = jnp.concatenate([high, low], axis=0).astype(BF16)
    out[32:48, where] = jnp.concatenate([high, mid], axis=0).astype(BF16)


def row_part(v):
    high, mid, low = parts(v)
    stacked = jnp.concatenate([high, high, mid, high, low, mid], axis=0)
    return stacked.T.astype(BF16)


def row_features(g, dirs, soft_sq, out_s, out_u, out_w, vec, small):
    piece = g.shape[1]
    each = small.shape[1]
    x, y, z = g[0:1], g[1:2], g[2:3] - 1.0
    zero = jnp.zeros((4, piece), F32)
    vec[4:8] = zero
    vec[0:1], vec[1:2], vec[2:3] = (-2.0 * turns_sq) * x, (-2.0 * turns_sq) * y, (-2.0 * turns_sq) * z
    vec[3:4] = turns_sq * (x * x + y * y + z * z + soft_sq)
    vec[4:5] = jnp.ones((1, piece), F32)
    out_s[0:piece] = row_part(vec[...])
    vec[0:1], vec[1:2], vec[2:3] = x, y, z
    vec[3:4] = jnp.ones((1, piece), F32)
    vec[4:8] = zero
    out_u[0:piece] = row_part(vec[...])
    vec[0:3] = g[3:6] * (1.0 / wavenumber)
    vec[3:4] = (x * g[3:4] + y * g[4:5] + z * g[5:6]) * (-1.0 / wavenumber)
    out_w[...] = row_part(vec[...])
    dir_x, dir_y, dir_z = dirs
    small[4:8] = jnp.zeros((4, each), F32)
    small[0:1], small[1:2], small[2:3] = (value * (-wavenumber / two_pi) for value in dirs)
    small[3:4] = dir_z * (-wavenumber / two_pi)
    out_s[piece:] = row_part(small[...])
    small[0:1], small[1:2], small[2:3] = (value * (wavenumber / tile_scale) for value in dirs)
    small[3:4] = jnp.zeros((1, each), F32)
    out_u[piece:] = row_part(small[...])


def directions(angle_ref, owner, each):
    lanes = max(each, 128)
    fit = lanes // each
    window = angle_ref[:, pl.ds(pl.multiple_of(owner // fit * lanes, lanes), lanes)]
    angles = window[:, :each]
    for k in range(1, fit):
        angles = jnp.where(lax.rem(owner, fit) == k, window[:, k * each : (k + 1) * each], angles)
    c, s = cos_sin(angles * (1.0 / two_pi))
    sin_t = s[0:1]
    return sin_t * c[1:2], sin_t * s[1:2], c[0:1]


def panel_entries(s, u, w):
    inverse = lax.rsqrt(s)
    d, x = half_tangent(s * inverse)
    d2, x2 = d * d, x * x
    q = pl.reciprocal((d2 + x2) * s)
    re = (d2 - x2) * q
    h = d * q
    im = (h + h) * x
    p = inverse * (1.0 / two_pi)
    a = p * u + w
    b = p * w - u
    return re * a - im * b, re * b + im * a


def far_entries(turn, scale):
    d, x = half_tangent(turn)
    d2, x2 = d * d, x * x
    q = scale * pl.reciprocal(d2 + x2)
    h = d * q
    return (h + h) * x, (x2 - d2) * q


def tiles_kernel(at_mask, masked, soft_sq, resume, *refs):
    if resume:
        before, rs, ru, rw, cs, cu, cw, x_ref, out, acc, *bufs = refs
        piece = rw.shape[0]
    else:
        g_ref, dirs_ref, cs, cu, cw, x_ref, out, rs, ru, rw, vec, small, acc, *bufs = refs
        piece = g_ref.shape[1]
        dirs = [dirs_ref[8 * at_mask + j : 8 * at_mask + j + 1] for j in range(3)]
        row_features(g_ref[...], dirs, soft_sq, rs, ru, rw, vec, small)
    rows = out.shape[0]
    count = cs.shape[1] // CHUNK

    def multiply(at, buf):
        where = pl.ds(pl.multiple_of(at * CHUNK, CHUNK), CHUNK)
        for row_ref, col_ref, hold in ((rs, cs, buf[0]), (ru, cu, buf[1]), (rw, cw, buf[2])):
            hold[...] = jnp.dot(row_ref[...], col_ref[:, where], preferred_element_type=F32)

    def entries(buf, tile, diagonal=None):
        for begin in range(0, rows, SUB):
            take = pl.ds(begin, SUB)
            if begin < piece:
                re, im = panel_entries(buf[0][take], buf[1][take], buf[2][take])
                if diagonal is not None:
                    down = lax.broadcasted_iota(jnp.int32, (SUB, CHUNK), 0) + begin
                    across = lax.broadcasted_iota(jnp.int32, (SUB, CHUNK), 1) + diagonal
                    re = jnp.where(down == across, 0.0, re)
                    im = jnp.where(down == across, 0.0, im)
            else:
                re, im = far_entries(buf[0][take], buf[1][take])
            tile[take, :CHUNK] = re.astype(BF16)
            tile[take, CHUNK:] = im.astype(BF16)

    def apply(at, tile, begin=False):
        where = pl.ds(pl.multiple_of(at * 2 * CHUNK, 2 * CHUNK), 2 * CHUNK)
        product = jnp.dot(tile[...], x_ref[where], preferred_element_type=F32)
        if not begin:
            acc[...] += product
        elif resume:
            acc[...] = before[...] + product
        else:
            acc[...] = product

    first, second, tile_a, tile_b = bufs[:3], bufs[3:6], bufs[6], bufs[7]
    multiply(0, first)

    def two(step, begin, last):
        own = last and masked
        multiply(2 * step + 1, second)
        if not begin:
            apply(2 * step - 1, tile_b)
        entries(first, tile_a, 0 if own and piece == 2 * CHUNK else None)
        if not last:
            multiply(2 * step + 2, first)
        apply(2 * step, tile_a, begin)
        entries(second, tile_b, piece - CHUNK if own else None)

    def body(step, carry):
        two(step, False, False)
        return carry

    steps = count // 2
    two(0, True, steps == 1)
    if steps > 1:
        lax.fori_loop(1, steps - 1, body, 0)
        two(steps - 1, False, True)
    apply(count - 1, tile_b)
    out[...] = acc[...].astype(out.dtype)


def dot_first(left, right, precision=None):
    return lax.dot_general(
        left, right, (((0,), (0,)), ((), ())), precision=precision, preferred_element_type=F32
    )


def local_kernel(x_ref, g_ref, index_ref, weight_ref, blade_ref, harmonic_ref, out):
    piece, width = x_ref.shape
    half = width // 2
    count = index_ref.shape[0]
    rows = lax.axis_index("rows")
    cols = lax.axis_index("cols")
    base = (rows * lax.axis_size("cols") + cols) * piece
    ids = lax.broadcasted_iota(jnp.int32, (piece, piece), 0) + base
    m_re = jnp.zeros((piece, piece), F32)
    m_im = jnp.zeros((piece, piece), F32)
    for c in range(count):
        hit = ids == index_ref[c : c + 1]
        m_re += jnp.where(hit, weight_ref[c : c + 1], 0.0)
        m_im += jnp.where(hit, weight_ref[count + c : count + c + 1], 0.0)
    x = x_ref[...]
    first = jnp.zeros((piece, width), F32)
    second = jnp.zeros((piece, width), F32)
    for part in parts(m_re):
        first += dot_first(part.astype(BF16), x)
    for part in parts(m_im):
        second += dot_first(part.astype(BF16), x)
    g = g_ref[...]
    source = lax.broadcasted_iota(jnp.int32, (NS, 1), 0)
    src_cos, src_sin = cos_sin(source.astype(F32) * (1.0 / NS))
    dx = g[0:1] - cycle_radius * src_cos
    dy = g[1:2] - cycle_radius * src_sin
    dz = g[2:3] - cycle_height
    r_sq = dx * dx + dy * dy + dz * dz
    inverse = lax.rsqrt(r_sq)
    c, s = cos_sin(r_sq * inverse * (wavenumber / two_pi))
    g_re = c * inverse * (1.0 / four_pi)
    g_im = s * inverse * (1.0 / four_pi)
    slope = (dx * g[3:4] + dy * g[4:5] + dz * g[5:6]) * inverse
    f_re = 1.0 - slope
    f_im = slope * inverse * (-1.0 / wavenumber)
    h_re = g_re * f_re - g_im * f_im
    h_im = g_re * f_im + g_im * f_re
    turn = lax.rem(source * (blade_ref[...] * harmonic_ref[...]), NS).astype(F32) * (1.0 / NS)
    e_re, e_im = cos_sin(turn)
    lhs = jnp.concatenate([h_re, h_im], axis=0)
    rhs = jnp.concatenate(
        [jnp.concatenate([e_re, e_im], axis=1), jnp.concatenate([-e_im, e_re], axis=1)], axis=0
    )
    b = dot_first(lhs, rhs, lax.Precision.HIGHEST)
    xf = x.astype(F32)
    out[:, :half] = b[:, :half] - 0.5 * xf[:, :half] - (first[:, :half] - second[:, half:])
    out[:, half:] = b[:, half:] - 0.5 * xf[:, half:] - (first[:, half:] + second[:, :half])


def final_kernel(count, base, own, *refs):
    got, residual, far = refs[:count], refs[count], refs[count + 1]
    piece = residual.shape[0]
    total = own[...]
    for ref in got:
        total += ref[...].astype(F32)
    residual[...] = base[...] - total[:piece]
    far[...] = total[piece:]


def call(kernel, out_shape, scratch=(), name=None, cost=None, inputs=None, limit=40):
    return pl.pallas_call(
        kernel,
        out_shape=out_shape,
        scratch_shapes=list(scratch),
        compiler_params=pltpu.CompilerParams(vmem_limit_bytes=limit * 2**20),
        cost_estimate=cost,
        name=name,
        **({} if inputs is None else {"in_specs": inputs}),
    )


def TILE_COST(entries):
    return pl.CostEstimate(flops=4 * entries, bytes_accessed=entries, transcendentals=0)


NEAR_COST = pl.CostEstimate(flops=10**7, bytes_accessed=10**6, transcendentals=10**5)


def xor_permute(value, axis, mask):
    size = lax.axis_size(axis)
    return lax.ppermute(value, axis, [(i, i ^ mask) for i in range(size)])


def local(krylov, geometry, corr_index, corr_weight, blades, harmonic, observer_angles):
    nrows = lax.axis_size("rows")
    ncols = lax.axis_size("cols")
    piece, width = krylov.shape
    soft_sq = 4.0 / (piece * nrows * ncols)
    each = observer_angles.shape[1] // (nrows * ncols)
    rows = piece + each

    masks = list(range(2, nrows, 2))
    order = [0] + masks
    payload, dirs = call(
        functools.partial(payload_kernel, order),
        (
            jax.ShapeDtypeStruct((piece + 32, width), BF16),
            jax.ShapeDtypeStruct((8 * len(order), each), F32),
        ),
        [pltpu.VMEM(a.shape, a.dtype) for a in (geometry, krylov, observer_angles)] + [pltpu.SemaphoreType.DMA((3,))],
        name="payload",
        inputs=[pl.BlockSpec(memory_space=pltpu.HBM)] * 3,
        limit=64,
    )(krylov, geometry, observer_angles)
    line = [payload] + [xor_permute(payload, "cols", m) for m in range(1, ncols)]
    near_half, far_half = line[: ncols // 2][::-1], line[ncols // 2 :]

    plane = {m: xor_permute(geometry, "rows", m) for m in masks}

    base = call(
        local_kernel,
        jax.ShapeDtypeStruct((piece, width), F32),
        name="near_and_incident",
        cost=NEAR_COST,
    )(krylov, geometry, corr_index, corr_weight, blades.reshape(1, -1), harmonic.reshape(1, -1))

    def exchange(shards):
        packed = call(
            functools.partial(pack_kernel, len(shards)),
            jax.ShapeDtypeStruct((len(shards) * (piece + 32), width), BF16),
            name="pack",
        )(*shards)
        return xor_permute(packed, "rows", 1)

    def features(*shards):
        panels = sum(shard.shape[0] for shard in shards) // (piece + 32) * piece
        feature = jax.ShapeDtypeStruct((DEPTH, panels), BF16)
        return call(
            functools.partial(columns_kernel, piece + 32, len(shards)),
            (feature, feature, feature, jax.ShapeDtypeStruct((2 * panels, width), BF16)),
            [pltpu.VMEM((8, piece), F32)],
            name="columns",
        )(*shards)

    def buffers():
        buf = [pltpu.VMEM((rows, CHUNK), F32)] * 2 + [pltpu.VMEM((piece, CHUNK), F32)]
        return [pltpu.VMEM((rows, width), F32)] + buf * 2 + [pltpu.VMEM((rows, 2 * CHUNK), BF16)] * 2

    def tiles(mask, columns, geom):
        return call(
            functools.partial(tiles_kernel, order.index(mask), mask == 0, soft_sq, False),
            (
                jax.ShapeDtypeStruct((rows, width), F32),
                jax.ShapeDtypeStruct((rows, DEPTH), BF16),
                jax.ShapeDtypeStruct((rows, DEPTH), BF16),
                jax.ShapeDtypeStruct((piece, DEPTH), BF16),
            ),
            [pltpu.VMEM((8, piece), F32), pltpu.VMEM((8, each), F32)] + buffers(),
            name="tiles",
            cost=TILE_COST(rows * columns[0].shape[1]),
        )(geom, dirs, *columns)

    def resume(mask, columns, before):
        return call(
            functools.partial(tiles_kernel, 0, False, soft_sq, True),
            jax.ShapeDtypeStruct((rows, width), BF16 if mask else F32),
            buffers(),
            name="resume",
            cost=TILE_COST(rows * columns[0].shape[1]),
        )(*before, *columns)

    early = {m: plane[m] for m in masks[:2]}
    received, dirs, early = lax.optimization_barrier((near_half[:-1], dirs, early))
    plane.update(early)
    near_half = received + near_half[-1:]
    columns = features(*near_half)
    held = {0: tiles(0, columns, geometry)}
    held[0], plane = lax.optimization_barrier((held[0], plane))
    for m in masks:
        held[m] = tiles(m, columns, plane[m])

    first = order[:-1]
    far_half, done = lax.optimization_barrier((far_half, [held[m] for m in first]))
    held.update(zip(first, done))
    packed = exchange(near_half + far_half)
    packed, held[masks[-1]] = lax.optimization_barrier((packed, held[masks[-1]]))
    columns = features(packed, *far_half)
    got = [xor_permute(resume(m, columns, held[m]), "rows", m) for m in masks[::-1]]
    got[:-1], held[0] = lax.optimization_barrier((got[:-1], held[0]))
    own = resume(0, columns, held[0])

    return call(
        functools.partial(final_kernel, len(got)),
        (jax.ShapeDtypeStruct((piece, width), F32), jax.ShapeDtypeStruct((each, width), F32)),
        name="combine",
    )(base, own, *got)


def solution(mesh):
    placed = (
        P(("rows", "cols"), None),
        P(None, ("rows", "cols")),
        P(None, ("rows", "cols")),
        P(None, ("rows", "cols")),
        P(),
        P(),
        P(),
    )
    return jax.shard_map(
        local,
        mesh=mesh,
        in_specs=placed,
        out_specs=(P(("rows", "cols"), None), P(("rows", "cols"), None)),
        check_vma=False,
    )
```

time: 51.4 us -> 40.8 us (0.79)
  starting transfers between devices: 21.1 us -> 15.3 us
  Pallas kernels: 22.3 us -> 19.8 us
  waiting for transfers between devices: 4.37 us -> 2.07 us
  local copies, waits for them, and re-layouts: 0.97 us -> 2.36 us
  other arithmetic: 1.38 us -> 0 us
    ppermute x20 -> x10, starting transfers between devices: 21.1 us -> 15.3 us  [xor_permute(): return lax.ppermute(value, axis, [(i, i ^ mask) for i in range(size)])]
    pallas_call x10 -> x13, Pallas kernels: 21.2 us -> 18.7 us  [the longest x4 11 us: resume(): call(functools.partial(tiles_kernel, 0, False, soft_sq, True), jax.ShapeD...]
    ppermute x20 -> x10, waiting for transfers between devices: 4.37 us -> 2.07 us  [xor_permute(): return lax.ppermute(value, axis, [(i, i ^ mask) for i in range(size)])]
    unnamed x14 -> x20, local copies, waits for them, and re-layouts: 0.75 us -> 2.36 us
    mul x1 -> x0, other arithmetic: 1.32 us -> none  [local(): sin_t * jnp.cos(observer_angles[1])]
  transfers between devices with their start and end apart: 20 -> 10, of which waited for: 4 -> 3; matrix products, arithmetic and copies ran while one was open for 3% -> 0% of each run, Pallas kernels for 40% -> 35%
where the time goes in v2:
time: 40.8 us; the launch traced here: 40.4 us
  Pallas kernels  19.8 us (49%)
  starting transfers between devices  15.3 us (38%)
  local copies, waits for them, and re-layouts  2.36 us (6%)
  waiting for transfers between devices  2.07 us (5%)
  between operations  0.86 us (2%)
    ppermute x10, starting transfers between devices, xor_permute(): return lax.ppermute(value, axis, [(i, i ^ mask) for i in range(size)])  15.3 us
    pallas_call x4, Pallas kernels, resume(): call(functools.partial(tiles_kernel, 0, False, soft_sq, True), jax.ShapeD...  11 us
    pallas_call x4, Pallas kernels, tiles(): call(functools.partial(tiles_kernel, order.index(mask), mask == 0, soft_s...  4.86 us
    unnamed x20, local copies, waits for them, and re-layouts  2.36 us
    ppermute x10, waiting for transfers between devices, xor_permute(): return lax.ppermute(value, axis, [(i, i ^ mask) for i in range(size)])  2.07 us
    pallas_call x1, Pallas kernels, local(): call(functools.partial(payload_kernel, order), (jax.ShapeDtypeStruct((pie...  1.64 us
    pallas_call x1, Pallas kernels, local(): call(local_kernel, jax.ShapeDtypeStruct((piece, width), F32), name='near_...  1.07 us
  transfers between devices with their start and end apart: 10, of which 3 were waited for; matrix products, arithmetic and copies ran while one was open for 0% of the time, Pallas kernels for 35%

profile of v2, /device:TPU:0, one launch (start us, length us, event | category | flops | bytes accessed | tf_op | source)
XLA Modules:
  0.0 40.4 jit_solution(12373309273631511291)
XLA Ops:
  0.6 1.6 %payload.1 = (bf16[288,256]{1,0:T(8,128)(2,1)}, f32[32,64]{1,0:T(8,128)}) custom-call(bf16[256,256]{1,0:T(8,128)(2,1)} %x_hbm.1, f32[7,256]{1,0:T(8,128)} %refs_0_.1, f32[2,2048]{1,0:T(2,128)} %angle_hbm.1), custom_call_target="tpu_custom_call" | custom-call | tf_op jit(solution)/shard_map/payload/pallas_call | solution.py:366
  2.3 3.1 %collective-permute-start = (bf16[288,256]{1,0:T(8,128)(2,1)}, bf16[288,256]{1,0:T(8,128)(2,1)S(1)}, u32[]{:S(2)}, u32[]{:S(2)}) collective-permute-start(bf16[288,256]{1,0:T(8,128)(2,1)} %get-tuple-element.64.refs_1_), channel_id=1, source_target_pairs={{0,1},{1,0},{2,3},{3,2},{4,5},{5,4},{6,7},{7,6},{8,9},{9,8},{10,11... | collective-permute-start | bytes 442376 | tf_op jit(solution)/shard_map/ppermute | solution.py:353
  5.4 2.6 %collective-permute-start.3 = (bf16[288,256]{1,0:T(8,128)(2,1)}, bf16[288,256]{1,0:T(8,128)(2,1)S(1)}, u32[]{:S(2)}, u32[]{:S(2)}) collective-permute-start(bf16[288,256]{1,0:T(8,128)(2,1)} %get-tuple-element.64.refs_1_), channel_id=1, source_target_pairs={{0,2},{1,3},{2,0},{3,1},{4,6},{5,7},{6,4},{7,5},{8,10},{9,11},{10,... | collective-permute-start | bytes 442376 | tf_op jit(solution)/shard_map/ppermute | solution.py:353
  8.0 1.7 %collective-permute-start.1 = (f32[7,256]{1,0:T(8,128)}, f32[7,256]{1,0:T(8,128)S(1)}, u32[]{:S(2)}, u32[]{:S(2)}) collective-permute-start(f32[7,256]{1,0:T(8,128)} %refs_0_.1), channel_id=1, source_target_pairs={{0,8},{4,12},{8,0},{12,4},{16,24},{20,28},{24,16},{28,20},{1,9},{5... | collective-permute-start | bytes 21512 | tf_op jit(solution)/shard_map/ppermute | solution.py:353
  9.7 1.5 %collective-permute-start.2 = (f32[7,256]{1,0:T(8,128)}, f32[7,256]{1,0:T(8,128)S(1)}, u32[]{:S(2)}, u32[]{:S(2)}) collective-permute-start(f32[7,256]{1,0:T(8,128)} %refs_0_.1), channel_id=1, source_target_pairs={{0,16},{4,20},{8,24},{12,28},{16,0},{20,4},{24,8},{28,12},{1,17},{... | collective-permute-start | bytes 21512 | tf_op jit(solution)/shard_map/ppermute | solution.py:353
  11.2 0.6 %collective-permute-done.1.refs_0_ = f32[7,256]{1,0:T(8,128)S(1)} collective-permute-done((f32[7,256]{1,0:T(8,128)}, f32[7,256]{1,0:T(8,128)S(1)}, u32[]{:S(2)}, u32[]{:S(2)}) %collective-permute-start.1) | collective-permute-done | bytes 7200 | tf_op jit(solution)/shard_map/ppermute | solution.py:353
  11.8 2.7 %collective-permute-start.5 = (f32[7,256]{1,0:T(8,128)}, f32[7,256]{1,0:T(8,128)S(1)}, u32[]{:S(2)}, u32[]{:S(2)}) collective-permute-start(f32[7,256]{1,0:T(8,128)} %refs_0_.1), channel_id=1, source_target_pairs={{0,24},{4,28},{8,16},{12,20},{16,8},{20,12},{24,0},{28,4},{1,25},{... | collective-permute-start | bytes 21512 | tf_op jit(solution)/shard_map/ppermute | solution.py:353
  14.5 0.9 %copy-done = bf16[288,256]{1,0:T(8,128)(2,1)S(1)} copy-done((bf16[288,256]{1,0:T(8,128)(2,1)S(1)}, bf16[288,256]{1,0:T(8,128)(2,1)}, u32[]{:S(2)}) %copy-start) | copy-done | bytes 147480
  15.5 0.7 %copy-done.3 = f32[32,64]{1,0:T(8,128)S(1)} copy-done((f32[32,64]{1,0:T(8,128)S(1)}, f32[32,64]{1,0:T(8,128)}, u32[]{:S(2)}) %copy-start.3) | copy-done | bytes 8216
  16.2 0.7 %copy-done.4 = f32[7,256]{1,0:T(8,128)S(1)} copy-done((f32[7,256]{1,0:T(8,128)S(1)}, f32[7,256]{1,0:T(8,128)}, u32[]{:S(2)}) %copy-start.4) | copy-done | bytes 7192
  16.9 1.2 %tiles.4 = (f32[320,256]{1,0:T(8,128)S(1)}, bf16[320,48]{1,0:T(8,128)(2,1)S(1)}, bf16[320,48]{1,0:T(8,128)(2,1)S(1)}, bf16[256,48]{1,0:T(8,128)(2,1)S(1)}) custom-call(f32[7,256]{1,0:T(8,128)S(1)} %copy-done.4, f32[32,64]{1,0:T(8,128)S(1)} %copy-done.3, bf16[48,512]{1,0:T(8,128)(2,1)S(1)} %get-tuple-element.68.refs_2_, ...), custom_call_target="tpu_custom_call" | custom-call | flops 655360 | bytes 163840 | tf_op jit(solution)/shard_map/tiles/pallas_call | solution.py:412
  18.2 1.2 %tiles.6 = (f32[320,256]{1,0:T(8,128)S(1)}, bf16[320,48]{1,0:T(8,128)(2,1)S(1)}, bf16[320,48]{1,0:T(8,128)(2,1)S(1)}, bf16[256,48]{1,0:T(8,128)(2,1)S(1)}) custom-call(f32[7,256]{1,0:T(8,128)S(1)} %collective-permute-done.2.refs_0_, f32[32,64]{1,0:T(8,128)S(1)} %copy-done.3, bf16[48,512]{1,0:T(8,128)(2,1)S(1)} %get-tuple-element.68.refs_2_, ...), custom_call_target="tpu_custom_call" | custom-call | flops 655360 | bytes 163840 | tf_op jit(solution)/shard_map/tiles/pallas_call | solution.py:412
  19.4 1.2 %tiles.5 = (f32[320,256]{1,0:T(8,128)S(1)}, bf16[320,48]{1,0:T(8,128)(2,1)S(1)}, bf16[320,48]{1,0:T(8,128)(2,1)S(1)}, bf16[256,48]{1,0:T(8,128)(2,1)S(1)}) custom-call(f32[7,256]{1,0:T(8,128)S(1)} %collective-permute-done.1.refs_0_, f32[32,64]{1,0:T(8,128)S(1)} %copy-done.3, bf16[48,512]{1,0:T(8,128)(2,1)S(1)} %get-tuple-element.68.refs_2_, ...), custom_call_target="tpu_custom_call" | custom-call | flops 655360 | bytes 163840 | tf_op jit(solution)/shard_map/tiles/pallas_call | solution.py:412
  20.8 1.2 %tiles.7 = (f32[320,256]{1,0:T(8,128)S(1)}, bf16[320,48]{1,0:T(8,128)(2,1)S(1)}, bf16[320,48]{1,0:T(8,128)(2,1)S(1)}, bf16[256,48]{1,0:T(8,128)(2,1)S(1)}) custom-call(f32[7,256]{1,0:T(8,128)S(1)} %collective-permute-done.5.refs_0_, f32[32,64]{1,0:T(8,128)S(1)} %copy-done.3, bf16[48,512]{1,0:T(8,128)(2,1)S(1)} %get-tuple-element.68.refs_2_, ...), custom_call_target="tpu_custom_call" | custom-call | flops 655360 | bytes 163840 | tf_op jit(solution)/shard_map/tiles/pallas_call | solution.py:412
  22.0 0.8 %collective-permute-done.6.refs_0_ = bf16[1152,256]{1,0:T(8,128)(2,1)S(1)} collective-permute-done((bf16[1152,256]{1,0:T(8,128)(2,1)S(1)}, bf16[1152,256]{1,0:T(8,128)(2,1)S(1)}, u32[]{:S(2)}, u32[]{:S(2)}) %collective-permute-start.6) | collective-permute-done | bytes 589856 | tf_op jit(solution)/shard_map/ppermute | solution.py:353
  23.1 2.7 %resume.5 = bf16[320,256]{1,0:T(8,128)(2,1)S(1)} custom-call(f32[320,256]{1,0:T(8,128)S(1)} %get-tuple-element.108.refs_0_, bf16[320,48]{1,0:T(8,128)(2,1)S(1)} %get-tuple-element.109.refs_1_, bf16[320,48]{1,0:T(8,128)(2,1)S(1)} %get-tuple-element.110.refs_2_, bf16[256,48]{1,0:T(8,128)(2,1)S(1)} %get-tuple-element.111.refs_3_, ...), custom_call_target="tpu_custom_call" | custom-call | flops 1966080 | bytes 491520 | tf_op jit(solution)/shard_map/resume/pallas_call | solution.py:426
  26.4 2.7 %resume.4 = bf16[320,256]{1,0:T(8,128)(2,1)S(1)} custom-call(f32[320,256]{1,0:T(8,128)S(1)} %get-tuple-element.99.refs_0_, bf16[320,48]{1,0:T(8,128)(2,1)S(1)} %get-tuple-element.100.refs_1_, bf16[320,48]{1,0:T(8,128)(2,1)S(1)} %get-tuple-element.101.refs_2_, bf16[256,48]{1,0:T(8,128)(2,1)S(1)} %get-tuple-element.102.refs_3_, ...), custom_call_target="tpu_custom_call" | custom-call | flops 1966080 | bytes 491520 | tf_op jit(solution)/shard_map/resume/pallas_call | solution.py:426
  29.2 1.5 %collective-permute-start.7 = (bf16[320,256]{1,0:T(8,128)(2,1)S(1)}, bf16[320,256]{1,0:T(8,128)(2,1)S(1)}, u32[]{:S(2)}, u32[]{:S(2)}) collective-permute-start(bf16[320,256]{1,0:T(8,128)(2,1)S(1)} %resume.4), channel_id=1, source_target_pairs={{0,24},{4,28},{8,16},{12,20},{16,8},{20,12},{24,0},{28,4},{1,25},{... | collective-permute-start | bytes 491528 | tf_op jit(solution)/shard_map/ppermute | solution.py:353
  30.7 2.9 %resume.7 = bf16[320,256]{1,0:T(8,128)(2,1)S(1)} custom-call(f32[320,256]{1,0:T(8,128)S(1)} %get-tuple-element.122.refs_0_, bf16[320,48]{1,0:T(8,128)(2,1)S(1)} %get-tuple-element.123.refs_1_, bf16[320,48]{1,0:T(8,128)(2,1)S(1)} %get-tuple-element.124.refs_2_, bf16[256,48]{1,0:T(8,128)(2,1)S(1)} %get-tuple-element.125.refs_3_, ...), custom_call_target="tpu_custom_call" | custom-call | flops 1966080 | bytes 491520 | tf_op jit(solution)/shard_map/resume/pallas_call | solution.py:426
  33.6 1.6 %collective-permute-start.9 = (bf16[320,256]{1,0:T(8,128)(2,1)S(1)}, bf16[320,256]{1,0:T(8,128)(2,1)S(1)}, u32[]{:S(2)}, u32[]{:S(2)}) collective-permute-start(bf16[320,256]{1,0:T(8,128)(2,1)S(1)} %resume.7), channel_id=1, source_target_pairs={{0,8},{4,12},{8,0},{12,4},{16,24},{20,28},{24,16},{28,20},{1,9},{5... | collective-permute-start | bytes 491528 | tf_op jit(solution)/shard_map/ppermute | solution.py:353
  35.2 1.1 %near_and_incident.1.base = f32[256,256]{1,0:T(8,128)S(1)} custom-call(bf16[256,256]{1,0:T(8,128)(2,1)S(1)} %copy-done.2, f32[7,256]{1,0:T(8,128)S(1)} %copy-done.5, s32[8,256]{1,0:T(8,128)S(1)} %copy-done.7, f32[16,256]{1,0:T(8,128)S(1)} %copy-done.6, s32[1,128]{1,0:T(1,128)S(1)} %bitcast.2, s32[1,128]{1,0:T(1,128)S(1)} %bitcast.3), custom_call_target="tpu_custom_call" | custom-call | flops 10000000 | bytes 1000000 | tf_op jit(solution)/shard_map/near_and_incident/pallas_call | solution.py:382
  36.3 2.7 %resume.6.own = f32[320,256]{1,0:T(8,128)S(1)} custom-call(f32[320,256]{1,0:T(8,128)S(1)} %get-tuple-element.116.refs_0_, bf16[320,48]{1,0:T(8,128)(2,1)S(1)} %get-tuple-element.117.refs_1_, bf16[320,48]{1,0:T(8,128)(2,1)S(1)} %get-tuple-element.118.refs_2_, bf16[256,48]{1,0:T(8,128)(2,1)S(1)} %get-tuple-element.119.refs_3_, ...), custom_call_target="tpu_custom_call" | custom-call | flops 1966080 | bytes 491520 | tf_op jit(solution)/shard_map/resume/pallas_call | solution.py:426
  39.0 0.6 %collective-permute-done.9.refs_2_ = bf16[320,256]{1,0:T(8,128)(2,1)S(1)} collective-permute-done((bf16[320,256]{1,0:T(8,128)(2,1)S(1)}, bf16[320,256]{1,0:T(8,128)(2,1)S(1)}, u32[]{:S(2)}, u32[]{:S(2)}) %collective-permute-start.9) | collective-permute-done | bytes 163872 | tf_op jit(solution)/shard_map/ppermute | solution.py:353
  39.7 0.8 %combine.1 = (f32[256,256]{1,0:T(8,128)}, f32[64,256]{1,0:T(8,128)}) custom-call(f32[256,256]{1,0:T(8,128)S(1)} %near_and_incident.1.base, f32[320,256]{1,0:T(8,128)S(1)} %resume.6.own, bf16[320,256]{1,0:T(8,128)(2,1)S(1)} %collective-permute-done.7.refs_0_, bf16[320,256]{1,0:T(8,128)(2,1)S(1)} %collective-permute-done.8.refs_1_, ...), custom_call_target="tpu_custom_call" | custom-call | tf_op jit(solution)/shard_map/combine/pallas_call | solution.py:454
  (30 shorter events, 1.2 us)
Async XLA Ops:
  2.3 12.2 %collective-permute-start = (bf16[288,256]{1,0:T(8,128)(2,1)}, bf16[288,256]{1,0:T(8,128)(2,1)S(1)}, u32[]{:S(2)}, u32[]{:S(2)}) collective-permute-start(bf16[288,256]{1,0:T(8,128)(2,1)} %get-tuple-element.64.refs_1_), channel_id=1, source_target_pairs={{0,1},{1,0},{2,3},{3,2},{4,5},{5,4},{6,7},{7,6},{8,9},{9,8},{10,11... | collective-permute-start | bytes 442376 | tf_op jit(solution)/shard_map/ppermute | solution.py:353
  5.4 15.3 %collective-permute-start.3 = (bf16[288,256]{1,0:T(8,128)(2,1)}, bf16[288,256]{1,0:T(8,128)(2,1)S(1)}, u32[]{:S(2)}, u32[]{:S(2)}) collective-permute-start(bf16[288,256]{1,0:T(8,128)(2,1)} %get-tuple-element.64.refs_1_), channel_id=1, source_target_pairs={{0,2},{1,3},{2,0},{3,1},{4,6},{5,7},{6,4},{7,5},{8,10},{9,11},{10,... | collective-permute-start | bytes 442376 | tf_op jit(solution)/shard_map/ppermute | solution.py:353
  8.0 12.7 %collective-permute-start.4 = (bf16[288,256]{1,0:T(8,128)(2,1)}, bf16[288,256]{1,0:T(8,128)(2,1)S(1)}, u32[]{:S(2)}, u32[]{:S(2)}) collective-permute-start(bf16[288,256]{1,0:T(8,128)(2,1)} %get-tuple-element.64.refs_1_), channel_id=1, source_target_pairs={{0,3},{1,2},{2,1},{3,0},{4,7},{5,6},{6,5},{7,4},{8,11},{9,10},{10,... | collective-permute-start | bytes 442376 | tf_op jit(solution)/shard_map/ppermute | solution.py:353
  8.0 3.9 %collective-permute-start.1 = (f32[7,256]{1,0:T(8,128)}, f32[7,256]{1,0:T(8,128)S(1)}, u32[]{:S(2)}, u32[]{:S(2)}) collective-permute-start(f32[7,256]{1,0:T(8,128)} %refs_0_.1), channel_id=1, source_target_pairs={{0,8},{4,12},{8,0},{12,4},{16,24},{20,28},{24,16},{28,20},{1,9},{5... | collective-permute-start | bytes 21512 | tf_op jit(solution)/shard_map/ppermute | solution.py:353
  9.7 4.8 %collective-permute-start.2 = (f32[7,256]{1,0:T(8,128)}, f32[7,256]{1,0:T(8,128)S(1)}, u32[]{:S(2)}, u32[]{:S(2)}) collective-permute-start(f32[7,256]{1,0:T(8,128)} %refs_0_.1), channel_id=1, source_target_pairs={{0,16},{4,20},{8,24},{12,28},{16,0},{20,4},{24,8},{28,12},{1,17},{... | collective-permute-start | bytes 21512 | tf_op jit(solution)/shard_map/ppermute | solution.py:353
  11.8 6.4 %collective-permute-start.5 = (f32[7,256]{1,0:T(8,128)}, f32[7,256]{1,0:T(8,128)S(1)}, u32[]{:S(2)}, u32[]{:S(2)}) collective-permute-start(f32[7,256]{1,0:T(8,128)} %refs_0_.1), channel_id=1, source_target_pairs={{0,24},{4,28},{8,16},{12,20},{16,8},{20,12},{24,0},{28,4},{1,25},{... | collective-permute-start | bytes 21512 | tf_op jit(solution)/shard_map/ppermute | solution.py:353
  14.5 0.9 %copy-start = (bf16[288,256]{1,0:T(8,128)(2,1)S(1)}, bf16[288,256]{1,0:T(8,128)(2,1)}, u32[]{:S(2)}) copy-start(bf16[288,256]{1,0:T(8,128)(2,1)} %get-tuple-element.64.refs_1_) | copy-start | bytes 442372
  15.4 5.2 %copy-start.1 = (bf16[288,256]{1,0:T(8,128)(2,1)S(1)}, bf16[288,256]{1,0:T(8,128)(2,1)}, u32[]{:S(2)}) copy-start(bf16[288,256]{1,0:T(8,128)(2,1)} %get-tuple-element.64.refs_1_) | copy-start | bytes 442372
  15.5 0.7 %copy-start.3 = (f32[32,64]{1,0:T(8,128)S(1)}, f32[32,64]{1,0:T(8,128)}, u32[]{:S(2)}) copy-start(f32[32,64]{1,0:T(8,128)} %get-tuple-element.67.refs_1_) | copy-start | bytes 24580
  16.2 0.7 %copy-start.4 = (f32[7,256]{1,0:T(8,128)S(1)}, f32[7,256]{1,0:T(8,128)}, u32[]{:S(2)}) copy-start(f32[7,256]{1,0:T(8,128)} %refs_0_.1) | copy-start | bytes 21508
  20.7 2.1 %collective-permute-start.6 = (bf16[1152,256]{1,0:T(8,128)(2,1)S(1)}, bf16[1152,256]{1,0:T(8,128)(2,1)S(1)}, u32[]{:S(2)}, u32[]{:S(2)}) collective-permute-start(bf16[1152,256]{1,0:T(8,128)(2,1)S(1)} %pack.1), channel_id=1, source_target_pairs={{0,4},{4,0},{8,12},{12,8},{16,20},{20,16},{24,28},{28,24},{1,5},{5... | collective-permute-start | bytes 1769480 | tf_op jit(solution)/shard_map/ppermute | solution.py:353
  25.8 10.5 %collective-permute-start.8 = (bf16[320,256]{1,0:T(8,128)(2,1)S(1)}, bf16[320,256]{1,0:T(8,128)(2,1)S(1)}, u32[]{:S(2)}, u32[]{:S(2)}) collective-permute-start(bf16[320,256]{1,0:T(8,128)(2,1)S(1)} %resume.5), channel_id=1, source_target_pairs={{0,16},{4,20},{8,24},{12,28},{16,0},{20,4},{24,8},{28,12},{1,17},{... | collective-permute-start | bytes 491528 | tf_op jit(solution)/shard_map/ppermute | solution.py:353
  29.1 6.0 %copy-start.2 = (bf16[256,256]{1,0:T(8,128)(2,1)S(1)}, bf16[256,256]{1,0:T(8,128)(2,1)}, u32[]{:S(2)}) copy-start(bf16[256,256]{1,0:T(8,128)(2,1)} %x_hbm.1) | copy-start | bytes 393220
  29.2 6.0 %copy-start.5 = (f32[7,256]{1,0:T(8,128)S(1)}, f32[7,256]{1,0:T(8,128)}, u32[]{:S(2)}) copy-start(f32[7,256]{1,0:T(8,128)} %refs_0_.1) | copy-start | bytes 21508
  29.2 6.0 %copy-start.6 = (f32[16,256]{1,0:T(8,128)S(1)}, f32[16,256]{1,0:T(8,128)}, u32[]{:S(2)}) copy-start(f32[16,256]{1,0:T(8,128)} %weight_ref.1) | copy-start | bytes 49156
  29.2 6.0 %copy-start.7 = (s32[8,256]{1,0:T(8,128)S(1)}, s32[8,256]{1,0:T(8,128)}, u32[]{:S(2)}) copy-start(s32[8,256]{1,0:T(8,128)} %index_ref.1) | copy-start | bytes 24580
  29.2 6.0 %copy-start.8 = (s32[128]{0:T(128)S(1)}, s32[128]{0:T(128)}, u32[]{:S(2)}) copy-start(s32[128]{0:T(128)} %param.11) | copy-start | bytes 1540
  29.2 6.0 %copy-start.9 = (s32[128]{0:T(128)S(1)}, s32[128]{0:T(128)}, u32[]{:S(2)}) copy-start(s32[128]{0:T(128)} %param.12) | copy-start | bytes 1540
  29.2 7.1 %collective-permute-start.7 = (bf16[320,256]{1,0:T(8,128)(2,1)S(1)}, bf16[320,256]{1,0:T(8,128)(2,1)S(1)}, u32[]{:S(2)}, u32[]{:S(2)}) collective-permute-start(bf16[320,256]{1,0:T(8,128)(2,1)S(1)} %resume.4), channel_id=1, source_target_pairs={{0,24},{4,28},{8,16},{12,20},{16,8},{20,12},{24,0},{28,4},{1,25},{... | collective-permute-start | bytes 491528 | tf_op jit(solution)/shard_map/ppermute | solution.py:353
  33.6 6.1 %collective-permute-start.9 = (bf16[320,256]{1,0:T(8,128)(2,1)S(1)}, bf16[320,256]{1,0:T(8,128)(2,1)S(1)}, u32[]{:S(2)}, u32[]{:S(2)}) collective-permute-start(bf16[320,256]{1,0:T(8,128)(2,1)S(1)} %resume.7), channel_id=1, source_target_pairs={{0,8},{4,12},{8,0},{12,4},{16,24},{20,28},{24,16},{28,20},{1,9},{5... | collective-permute-start | bytes 491528 | tf_op jit(solution)/shard_map/ppermute | solution.py:353

commit v3 on v2

--- a/solution.py
+++ b/solution.py
@@ -195,21 +195,32 @@
     return (h + h) * x, (x2 - d2) * q
 
 
-def tiles_kernel(at_mask, masked, soft_sq, resume, *refs):
+def tiles_kernel(soft_sq, resume, picks, skip, *refs):
+    count = len(picks)
     if resume:
-        before, rs, ru, rw, cs, cu, cw, x_ref, out, acc, *bufs = refs
-        piece = rw.shape[0]
+        befores, refs = refs[:count], refs[count:]
+        keeps, refs = refs[: 3 * count], refs[3 * count :]
+        cs, cu, cw, x_ref, *refs = refs
+        outs, bufs = refs[:count], refs[count:]
     else:
-        g_ref, dirs_ref, cs, cu, cw, x_ref, out, rs, ru, rw, vec, small, acc, *bufs = refs
-        piece = g_ref.shape[1]
-        dirs = [dirs_ref[8 * at_mask + j : 8 * at_mask + j + 1] for j in range(3)]
-        row_features(g_ref[...], dirs, soft_sq, rs, ru, rw, vec, small)
-    rows = out.shape[0]
-    count = cs.shape[1] // CHUNK
-
-    def multiply(at, buf):
-        where = pl.ds(pl.multiple_of(at * CHUNK, CHUNK), CHUNK)
-        for row_ref, col_ref, hold in ((rs, cs, buf[0]), (ru, cu, buf[1]), (rw, cw, buf[2])):
+        geoms, refs = refs[:count], refs[count:]
+        dirs_ref, cs, cu, cw, x_ref, *refs = refs
+        keeps, refs = refs[: 3 * count], refs[3 * count :]
+        outs, (vec, small, *bufs) = refs[:count], refs[count:]
+    rows, width = keeps[0].shape[0], x_ref.shape[1]
+    piece = keeps[2].shape[0]
+    steps = (cs.shape[1] // CHUNK - skip) // 2
+    first, second, tile_a, tile_b, acc = bufs[:3], bufs[3:6], bufs[6], bufs[7], bufs[8]
+
+    def prepare(index):
+        if not resume:
+            at = 8 * picks[index]
+            dirs = [dirs_ref[at + j : at + j + 1] for j in range(3)]
+            row_features(geoms[index][...], dirs, soft_sq, *keeps[3 * index : 3 * index + 3], vec, small)
+
+    def multiply(index, at, buf):
+        where = pl.ds(pl.multiple_of((at + skip) * CHUNK, CHUNK), CHUNK)
+        for row_ref, col_ref, hold in zip(keeps[3 * index : 3 * index + 3], (cs, cu, cw), buf):
             hold[...] = jnp.dot(row_ref[...], col_ref[:, where], preferred_element_type=F32)
 
     def entries(buf, tile, diagonal=None):
@@ -227,41 +238,46 @@
             tile[take, :CHUNK] = re.astype(BF16)
             tile[take, CHUNK:] = im.astype(BF16)
 
-    def apply(at, tile, begin=False):
-        where = pl.ds(pl.multiple_of(at * 2 * CHUNK, 2 * CHUNK), 2 * CHUNK)
+    def apply(index, at, tile, begin=False, end=False):
+        where = pl.ds(pl.multiple_of((at + skip) * 2 * CHUNK, 2 * CHUNK), 2 * CHUNK)
         product = jnp.dot(tile[...], x_ref[where], preferred_element_type=F32)
         if not begin:
-            acc[...] += product
+            product = acc[...] + product
         elif resume:
-            acc[...] = before[...] + product
+            product = befores[index][...] + product
+        if end:
+            outs[index][...] = product.astype(outs[index].dtype)
         else:
             acc[...] = product
 
-    first, second, tile_a, tile_b = bufs[:3], bufs[3:6], bufs[6], bufs[7]
-    multiply(0, first)
-
-    def two(step, begin, last):
-        own = last and masked
-        multiply(2 * step + 1, second)
+    def two(index, step, begin, last):
+        own = last and not resume and picks[index] == 0
+        multiply(index, 2 * step + 1, second)
         if not begin:
-            apply(2 * step - 1, tile_b)
+            apply(index, 2 * step - 1, tile_b)
+        elif index:
+            apply(index - 1, 2 * steps - 1, tile_b, end=True)
         entries(first, tile_a, 0 if own and piece == 2 * CHUNK else None)
         if not last:
-            multiply(2 * step + 2, first)
-        apply(2 * step, tile_a, begin)
+            multiply(index, 2 * step + 2, first)
+        elif index + 1 < len(picks):
+            prepare(index + 1)
+            multiply(index + 1, 0, first)
+        apply(index, 2 * step, tile_a, begin)
         entries(second, tile_b, piece - CHUNK if own else None)
 
-    def body(step, carry):
-        two(step, False, False)
+    def body(index, step, carry):
+        two(index, step, False, False)
         return carry
 
-    steps = count // 2
-    two(0, True, steps == 1)
-    if steps > 1:
-        lax.fori_loop(1, steps - 1, body, 0)
-        two(steps - 1, False, True)
-    apply(count - 1, tile_b)
-    out[...] = acc[...].astype(out.dtype)
+    prepare(0)
+    multiply(0, 0, first)
+    for index in range(len(picks)):
+        two(index, 0, True, steps == 1)
+        if steps > 1:
+            lax.fori_loop(1, steps - 1, functools.partial(body, index), 0)
+            two(index, steps - 1, False, True)
+    apply(len(picks) - 1, 2 * steps - 1, tile_b, end=True)
 
 
 def dot_first(left, right, precision=None):
@@ -342,10 +358,10 @@
 
 
 def TILE_COST(entries):
-    return pl.CostEstimate(flops=4 * entries, bytes_accessed=entries, transcendentals=0)
-
-
-NEAR_COST = pl.CostEstimate(flops=10**7, bytes_accessed=10**6, transcendentals=10**5)
+    return pl.CostEstimate(flops=1, bytes_accessed=2 * 10**6, transcendentals=0)
+
+
+NEAR_COST = pl.CostEstimate(flops=1, bytes_accessed=2 * 10**6, transcendentals=0)
 
 
 def xor_permute(value, axis, mask):
@@ -363,28 +379,22 @@
 
     masks = list(range(2, nrows, 2))
     order = [0] + masks
-    payload, dirs = call(
+    payload, dirs, geometry_here = call(
         functools.partial(payload_kernel, order),
         (
-            jax.ShapeDtypeStruct((piece + 32, width), BF16),
-            jax.ShapeDtypeStruct((8 * len(order), each), F32),
+            pltpu.VMEM((piece + 32, width), BF16),
+            pltpu.VMEM((8 * len(order), each), F32),
+            pltpu.VMEM(geometry.shape, F32),
         ),
-        [pltpu.VMEM(a.shape, a.dtype) for a in (geometry, krylov, observer_angles)] + [pltpu.SemaphoreType.DMA((3,))],
+        [pltpu.VMEM(a.shape, a.dtype) for a in (krylov, observer_angles)] + [pltpu.SemaphoreType.DMA((3,))],
         name="payload",
         inputs=[pl.BlockSpec(memory_space=pltpu.HBM)] * 3,
-        limit=64,
+        limit=56,
     )(krylov, geometry, observer_angles)
-    line = [payload] + [xor_permute(payload, "cols", m) for m in range(1, ncols)]
+    line = [payload] + [xor_permute(payload, "cols", m) for m in range(ncols - 1, 0, -1)]
     near_half, far_half = line[: ncols // 2][::-1], line[ncols // 2 :]
 
-    plane = {m: xor_permute(geometry, "rows", m) for m in masks}
-
-    base = call(
-        local_kernel,
-        jax.ShapeDtypeStruct((piece, width), F32),
-        name="near_and_incident",
-        cost=NEAR_COST,
-    )(krylov, geometry, corr_index, corr_weight, blades.reshape(1, -1), harmonic.reshape(1, -1))
+    plane = [geometry_here] + [xor_permute(geometry_here, "rows", m) for m in masks]
 
     def exchange(shards):
         packed = call(
@@ -404,52 +414,70 @@
             name="columns",
         )(*shards)
 
-    def buffers():
-        buf = [pltpu.VMEM((rows, CHUNK), F32)] * 2 + [pltpu.VMEM((piece, CHUNK), F32)]
-        return [pltpu.VMEM((rows, width), F32)] + buf * 2 + [pltpu.VMEM((rows, 2 * CHUNK), BF16)] * 2
-
-    def tiles(mask, columns, geom):
-        return call(
-            functools.partial(tiles_kernel, order.index(mask), mask == 0, soft_sq, False),
-            (
-                jax.ShapeDtypeStruct((rows, width), F32),
-                jax.ShapeDtypeStruct((rows, DEPTH), BF16),
-                jax.ShapeDtypeStruct((rows, DEPTH), BF16),
-                jax.ShapeDtypeStruct((piece, DEPTH), BF16),
-            ),
-            [pltpu.VMEM((8, piece), F32), pltpu.VMEM((8, each), F32)] + buffers(),
+    buf = [pltpu.VMEM((rows, CHUNK), F32)] * 2 + [pltpu.VMEM((piece, CHUNK), F32)]
+    buf = buf * 2 + [pltpu.VMEM((rows, 2 * CHUNK), BF16)] * 2 + [pltpu.VMEM((rows, width), F32)]
+
+    partial = jax.ShapeDtypeStruct((rows, width), F32)
+    kept = [jax.ShapeDtypeStruct((size, DEPTH), BF16) for size in (rows, rows, piece)]
+    held, keeps = {}, {}
+
+    def tiles(picks, columns):
+        found = call(
+            functools.partial(tiles_kernel, soft_sq, False, picks, 0),
+            (*kept * len(picks), *[partial] * len(picks)),
+            [pltpu.VMEM((8, piece), F32), pltpu.VMEM((8, each), F32)] + buf,
             name="tiles",
             cost=TILE_COST(rows * columns[0].shape[1]),
-        )(geom, dirs, *columns)
-
-    def resume(mask, columns, before):
-        return call(
-            functools.partial(tiles_kernel, 0, False, soft_sq, True),
-            jax.ShapeDtypeStruct((rows, width), BF16 if mask else F32),
-            buffers(),
+        )(*[plane[pick] for pick in picks], dirs, *columns)
+        for at, pick in enumerate(picks):
+            keeps[pick], held[pick] = found[3 * at : 3 * at + 3], found[3 * len(picks) + at]
+
+    def resume(picks, columns, last=False, skip=0):
+        found = call(
+            functools.partial(tiles_kernel, soft_sq, True, picks, skip),
+            tuple(jax.ShapeDtypeStruct((rows, width), BF16 if pick and last else F32) for pick in picks),
+            buf,
             name="resume",
             cost=TILE_COST(rows * columns[0].shape[1]),
-        )(*before, *columns)
-
-    early = {m: plane[m] for m in masks[:2]}
-    received, dirs, early = lax.optimization_barrier((near_half[:-1], dirs, early))
-    plane.update(early)
+        )(*[held[pick] for pick in picks], *[keep for pick in picks for keep in keeps[pick]], *columns)
+        held.update(zip(picks, found))
+
+    def after(value, *earlier):
+        return lax.optimization_barrier((value, earlier))[0]
+
+    received, dirs, early = lax.optimization_barrier((near_half[:-1], dirs, plane[1:3]))
+    plane[1:3] = early
     near_half = received + near_half[-1:]
     columns = features(*near_half)
-    held = {0: tiles(0, columns, geometry)}
-    held[0], plane = lax.optimization_barrier((held[0], plane))
-    for m in masks:
-        held[m] = tiles(m, columns, plane[m])
-
-    first = order[:-1]
-    far_half, done = lax.optimization_barrier((far_half, [held[m] for m in first]))
-    held.update(zip(first, done))
-    packed = exchange(near_half + far_half)
-    packed, held[masks[-1]] = lax.optimization_barrier((packed, held[masks[-1]]))
-    columns = features(packed, *far_half)
-    got = [xor_permute(resume(m, columns, held[m]), "rows", m) for m in masks[::-1]]
-    got[:-1], held[0] = lax.optimization_barrier((got[:-1], held[0]))
-    own = resume(0, columns, held[0])
+    final = len(order) - 1
+    tiles(list(range(final)), columns)
+    plane[final] = after(plane[final], held[0])
+    tiles([final], columns)
+
+    packed = exchange(near_half)
+    far_half = after(far_half, held)
+    other = exchange(far_half)
+    ahead = list(range(final, final // 2, -1))
+    resume(ahead, features(packed))
+    other = after(other, held)
+    columns = features(packed, other, *far_half)
+    got = []
+    for pick in range(final, 0, -1):
+        resume([pick], columns, True, 2 * piece * (ncols // 2) // 2 // CHUNK if pick in ahead else 0)
+        got.append(xor_permute(held[pick], "rows", order[pick]))
+        held[pick - 1] = after(held[pick - 1], held[pick])
+
+    got[:1], held[0] = lax.optimization_barrier((got[:1], held[0]))
+    resume([0], columns, True)
+    own = held[0]
+
+    got[:-1], near_geometry = lax.optimization_barrier((got[:-1], after(geometry_here, own)))
+    base = call(
+        local_kernel,
+        jax.ShapeDtypeStruct((piece, width), F32),
+        name="near_and_incident",
+        cost=NEAR_COST,
+    )(krylov, near_geometry, corr_index, corr_weight, blades.reshape(1, -1), harmonic.reshape(1, -1))
 
     return call(
         functools.partial(final_kernel, len(got)),

time: 40.8 us -> 38.6 us (0.946)
  local copies, waits for them, and re-layouts: 2.36 us -> 0.03 us
  waiting for transfers between devices: 2.07 us -> 3.12 us
  Pallas kernels: 19.8 us -> 19.1 us
    unnamed x20 -> x10, local copies, waits for them, and re-layouts: 2.36 us -> 0.03 us
    ppermute x10 -> x11, waiting for transfers between devices: 2.07 us -> 3.12 us  [xor_permute(): return lax.ppermute(value, axis, [(i, i ^ mask) for i in range(size)])]
    pallas_call x9 -> x8, Pallas kernels: 17.5 us -> 16.7 us  [the longest x5 11.3 us: resume(): call(functools.partial(tiles_kernel, soft_sq, True, picks, skip), tuple((...]
    ppermute x10 -> x11, starting transfers between devices: 15.3 us -> 15.3 us  [xor_permute(): return lax.ppermute(value, axis, [(i, i ^ mask) for i in range(size)])]
  transfers between devices with their start and end apart: 10 -> 11, of which waited for: 3 -> 3; matrix products, arithmetic and copies ran while one was open for 0% -> 0% of each run, Pallas kernels for 35% -> 39%
where the time goes in v3:
time: 38.6 us; the launch traced here: 38.4 us
  Pallas kernels  19.1 us (49%)
  starting transfers between devices  15.3 us (40%)
  waiting for transfers between devices  3.12 us (8%)
  between operations  0.85 us (2%)
    ppermute x11, starting transfers between devices, xor_permute(): return lax.ppermute(value, axis, [(i, i ^ mask) for i in range(size)])  15.3 us
    pallas_call x5, Pallas kernels, resume(): call(functools.partial(tiles_kernel, soft_sq, True, picks, skip), tuple((...  11.3 us
    pallas_call x2, Pallas kernels, tiles(): call(functools.partial(tiles_kernel, soft_sq, False, picks, 0), (*kept *...  4.37 us
    ppermute x11, waiting for transfers between devices, xor_permute(): return lax.ppermute(value, axis, [(i, i ^ mask) for i in range(size)])  3.12 us
    pallas_call x1, Pallas kernels, local(): call(local_kernel, jax.ShapeDtypeStruct((piece, width), F32), name='near_...  1.07 us
    pallas_call x1, Pallas kernels, local(): call(functools.partial(payload_kernel, order), (pltpu.VMEM((piece + 32, w...  0.97 us
    pallas_call x1, Pallas kernels, local(): call(functools.partial(final_kernel, len(got)), (jax.ShapeDtypeStruct((pi...  0.78 us
  transfers between devices with their start and end apart: 11, of which 3 were waited for; matrix products, arithmetic and copies ran while one was open for 0% of the time, Pallas kernels for 39%

profile of v3, /device:TPU:0, one launch (start us, length us, event | category | flops | bytes accessed | tf_op | source)
XLA Modules:
  0.0 38.4 jit_solution(8309355081371414300)
XLA Ops:
  0.6 1.0 %payload.1 = (bf16[288,256]{1,0:T(8,128)(2,1)S(1)}, f32[32,64]{1,0:T(8,128)S(1)}, f32[7,256]{1,0:T(8,128)S(1)}) custom-call(bf16[256,256]{1,0:T(8,128)(2,1)} %x_ref.1, f32[7,256]{1,0:T(8,128)} %g_hbm.1, f32[2,2048]{1,0:T(2,128)} %angle_hbm.1), custom_call_target="tpu_custom_call" | custom-call | tf_op jit(solution)/shard_map/payload/pallas_call | solution.py:382
  1.6 5.1 %collective-permute-start.1 = (bf16[288,256]{1,0:T(8,128)(2,1)S(1)}, bf16[288,256]{1,0:T(8,128)(2,1)S(1)}, u32[]{:S(2)}, u32[]{:S(2)}) collective-permute-start(bf16[288,256]{1,0:T(8,128)(2,1)S(1)} %get-tuple-element.53.refs_1_), channel_id=1, source_target_pairs={{0,3},{1,2},{2,1},{3,0},{4,7},{5,6},{6,5},{7,4},{8,11},{9,10},{10,... | collective-permute-start | bytes 442376 | tf_op jit(solution)/shard_map/ppermute | solution.py:369
  6.7 0.6 %collective-permute-start.5 = (bf16[288,256]{1,0:T(8,128)(2,1)S(1)}, bf16[288,256]{1,0:T(8,128)(2,1)S(1)}, u32[]{:S(2)}, u32[]{:S(2)}) collective-permute-start(bf16[288,256]{1,0:T(8,128)(2,1)S(1)} %get-tuple-element.53.refs_1_), channel_id=1, source_target_pairs={{0,2},{1,3},{2,0},{3,1},{4,6},{5,7},{6,4},{7,5},{8,10},{9,11},{10,... | collective-permute-start | bytes 442376 | tf_op jit(solution)/shard_map/ppermute | solution.py:369
  7.4 1.7 %collective-permute-start.3 = (f32[7,256]{1,0:T(8,128)S(1)}, f32[7,256]{1,0:T(8,128)S(1)}, u32[]{:S(2)}, u32[]{:S(2)}) collective-permute-start(f32[7,256]{1,0:T(8,128)S(1)} %get-tuple-element.99.refs_0_.g_ref), channel_id=1, source_target_pairs={{0,16},{4,20},{8,24},{12,28},{16,0},{20,4},{24,8},{28,12},{1,17},{... | collective-permute-start | bytes 21512 | tf_op jit(solution)/shard_map/ppermute | solution.py:369
  9.0 1.5 %collective-permute-start.2 = (f32[7,256]{1,0:T(8,128)S(1)}, f32[7,256]{1,0:T(8,128)S(1)}, u32[]{:S(2)}, u32[]{:S(2)}) collective-permute-start(f32[7,256]{1,0:T(8,128)S(1)} %get-tuple-element.99.refs_0_.g_ref), channel_id=1, source_target_pairs={{0,8},{4,12},{8,0},{12,4},{16,24},{20,28},{24,16},{28,20},{1,9},{5... | collective-permute-start | bytes 21512 | tf_op jit(solution)/shard_map/ppermute | solution.py:369
  10.5 0.5 %collective-permute-done.3.refs_2_ = f32[7,256]{1,0:T(8,128)S(1)} collective-permute-done((f32[7,256]{1,0:T(8,128)S(1)}, f32[7,256]{1,0:T(8,128)S(1)}, u32[]{:S(2)}, u32[]{:S(2)}) %collective-permute-start.3) | collective-permute-done | bytes 7200 | tf_op jit(solution)/shard_map/ppermute | solution.py:369
  11.0 2.6 %collective-permute-start = (f32[7,256]{1,0:T(8,128)S(1)}, f32[7,256]{1,0:T(8,128)S(1)}, u32[]{:S(2)}, u32[]{:S(2)}) collective-permute-start(f32[7,256]{1,0:T(8,128)S(1)} %get-tuple-element.99.refs_0_.g_ref), channel_id=1, source_target_pairs={{0,24},{4,28},{8,16},{12,20},{16,8},{20,12},{24,0},{28,4},{1,25},{... | collective-permute-start | bytes 21512 | tf_op jit(solution)/shard_map/ppermute | solution.py:369
  13.6 0.1 columns.3
  13.8 3.1 %tiles.2 = (bf16[320,48]{1,0:T(8,128)(2,1)S(1)}, bf16[320,48]{1,0:T(8,128)(2,1)S(1)}, bf16[256,48]{1,0:T(8,128)(2,1)S(1)}, bf16[320,48]{1,0:T(8,128)(2,1)S(1)}, ...) custom-call(f32[7,256]{1,0:T(8,128)S(1)} %get-tuple-element.99.refs_, ...), custom_call_target="tpu_custom_call" | custom-call | flops 1 | bytes 2000000 | tf_op jit(solution)/shard_map/tiles/pallas_call | solution.py:425
  17.0 1.2 %tiles.3 = (bf16[320,48]{1,0:T(8,128)(2,1)S(1)}, bf16[320,48]{1,0:T(8,128)(2,1)S(1)}, bf16[256,48]{1,0:T(8,128)(2,1)S(1)}, f32[320,256]{1,0:T(8,128)S(1)}) custom-call(f32[7,256]{1,0:T(8,128)S(1)} %collective-permute-done.refs_0_, f32[32,64]{1,0:T(8,128)S(1)} %get-tuple-element.57.refs_3_.refs_1_, bf16[48,512]{1,0:T(8,128)(2,1)S(1)} %get-tuple-element.59.refs_4_.refs_2_, ...), custom_call_target="tpu_custom_call" | custom-call | flops 1 | bytes 2000000 | tf_op jit(solution)/shard_map/tiles/pallas_call | solution.py:425
  18.2 1.0 %collective-permute-done.5.refs_0_.refs_2_ = bf16[288,256]{1,0:T(8,128)(2,1)S(1)} collective-permute-done((bf16[288,256]{1,0:T(8,128)(2,1)S(1)}, bf16[288,256]{1,0:T(8,128)(2,1)S(1)}, u32[]{:S(2)}, u32[]{:S(2)}) %collective-permute-start.5) | collective-permute-done | bytes 147488 | tf_op jit(solution)/shard_map/ppermute | solution.py:369
  19.3 0.1 columns.4
  19.4 1.9 %resume.5 = (f32[320,256]{1,0:T(8,128)S(1)}, f32[320,256]{1,0:T(8,128)S(1)}) custom-call(f32[320,256]{1,0:T(8,128)S(1)} %get-tuple-element.65.refs_0_, f32[320,256]{1,0:T(8,128)S(1)} %get-tuple-element.66.refs_1_, bf16[320,48]{1,0:T(8,128)(2,1)S(1)} %get-tuple-element.67.refs_2_.refs_1_, bf16[320,48]{1,0:T(8,128)(2,1)S(1)} %get-tuple-element.68.refs_3_.refs_2_, ...), custom_call_target="tpu_custom_call" | custom-call | flops 1 | bytes 2000000 | tf_op jit(solution)/shard_map/resume/pallas_call | solution.py:436
  21.4 0.3 columns.5
  21.7 1.9 %resume.6 = bf16[320,256]{1,0:T(8,128)(2,1)S(1)} custom-call(f32[320,256]{1,0:T(8,128)S(1)} %get-tuple-element.77.refs_0_, bf16[320,48]{1,0:T(8,128)(2,1)S(1)} %get-tuple-element.67.refs_2_.refs_1_, bf16[320,48]{1,0:T(8,128)(2,1)S(1)} %get-tuple-element.68.refs_3_.refs_2_, bf16[256,48]{1,0:T(8,128)(2,1)S(1)} %get-tuple-element.69.refs_4_.refs_3_, ...), custom_call_target="tpu_custom_call" | custom-call | flops 1 | bytes 2000000 | tf_op jit(solution)/shard_map/resume/pallas_call | solution.py:436
  23.6 2.5 %collective-permute-start.8 = (bf16[320,256]{1,0:T(8,128)(2,1)S(1)}, bf16[320,256]{1,0:T(8,128)(2,1)S(1)}, u32[]{:S(2)}, u32[]{:S(2)}) collective-permute-start(bf16[320,256]{1,0:T(8,128)(2,1)S(1)} %resume.6), channel_id=1, source_target_pairs={{0,24},{4,28},{8,16},{12,20},{16,8},{20,12},{24,0},{28,4},{1,25},{... | collective-permute-start | bytes 491528 | tf_op jit(solution)/shard_map/ppermute | solution.py:369
  26.1 1.9 %resume.7 = bf16[320,256]{1,0:T(8,128)(2,1)S(1)} custom-call(f32[320,256]{1,0:T(8,128)S(1)} %get-tuple-element.87.refs_0_, bf16[320,48]{1,0:T(8,128)(2,1)S(1)} %get-tuple-element.70.refs_5_.refs_1_, bf16[320,48]{1,0:T(8,128)(2,1)S(1)} %get-tuple-element.71.refs_6_.refs_2_, bf16[256,48]{1,0:T(8,128)(2,1)S(1)} %get-tuple-element.72.refs_7_.refs_3_, ...), custom_call_target="tpu_custom_call" | custom-call | flops 1 | bytes 2000000 | tf_op jit(solution)/shard_map/resume/pallas_call | solution.py:436
  28.0 0.6 %collective-permute-start.9 = (bf16[320,256]{1,0:T(8,128)(2,1)S(1)}, bf16[320,256]{1,0:T(8,128)(2,1)S(1)}, u32[]{:S(2)}, u32[]{:S(2)}) collective-permute-start(bf16[320,256]{1,0:T(8,128)(2,1)S(1)} %resume.7), channel_id=1, source_target_pairs={{0,16},{4,20},{8,24},{12,28},{16,0},{20,4},{24,8},{28,12},{1,17},{... | collective-permute-start | bytes 491528 | tf_op jit(solution)/shard_map/ppermute | solution.py:369
  28.6 2.9 %resume.8 = bf16[320,256]{1,0:T(8,128)(2,1)S(1)} custom-call(f32[320,256]{1,0:T(8,128)S(1)} %get-tuple-element.88.refs_0_, bf16[320,48]{1,0:T(8,128)(2,1)S(1)} %get-tuple-element.89.refs_1_, bf16[320,48]{1,0:T(8,128)(2,1)S(1)} %get-tuple-element.90.refs_2_, bf16[256,48]{1,0:T(8,128)(2,1)S(1)} %get-tuple-element.91.refs_3_, ...), custom_call_target="tpu_custom_call" | custom-call | flops 1 | bytes 2000000 | tf_op jit(solution)/shard_map/resume/pallas_call | solution.py:436
  31.5 0.6 %collective-permute-start.10 = (bf16[320,256]{1,0:T(8,128)(2,1)S(1)}, bf16[320,256]{1,0:T(8,128)(2,1)S(1)}, u32[]{:S(2)}, u32[]{:S(2)}) collective-permute-start(bf16[320,256]{1,0:T(8,128)(2,1)S(1)} %resume.8), channel_id=1, source_target_pairs={{0,8},{4,12},{8,0},{12,4},{16,24},{20,28},{24,16},{28,20},{1,9},{5... | collective-permute-start | bytes 491528 | tf_op jit(solution)/shard_map/ppermute | solution.py:369
  32.2 2.7 %resume.9.own = f32[320,256]{1,0:T(8,128)S(1)} custom-call(f32[320,256]{1,0:T(8,128)S(1)} %get-tuple-element.94.refs_0_, bf16[320,48]{1,0:T(8,128)(2,1)S(1)} %get-tuple-element.95.refs_1_, bf16[320,48]{1,0:T(8,128)(2,1)S(1)} %get-tuple-element.96.refs_2_, bf16[256,48]{1,0:T(8,128)(2,1)S(1)} %get-tuple-element.97.refs_3_, ...), custom_call_target="tpu_custom_call" | custom-call | flops 1 | bytes 2000000 | tf_op jit(solution)/shard_map/resume/pallas_call | solution.py:436
  34.9 1.1 %near_and_incident.1.base = f32[256,256]{1,0:T(8,128)S(1)} custom-call(bf16[256,256]{1,0:T(8,128)(2,1)S(1)} %copy-done, f32[7,256]{1,0:T(8,128)S(1)} %get-tuple-element.99.refs_0_.g_ref, s32[8,256]{1,0:T(8,128)S(1)} %copy-done.2, f32[16,256]{1,0:T(8,128)S(1)} %copy-done.1, s32[1,128]{1,0:T(1,128)S(1)} %bitcast.2, s32[1,128]{1,0:T(1,128)S(1)} %bitcast.3), custom_call_target="tpu_custom_call" | custom-call | flops 1 | bytes 2000000 | tf_op jit(solution)/shard_map/near_and_incident/pallas_call | solution.py:475
  36.0 1.6 %collective-permute-done.10.refs_2_ = bf16[320,256]{1,0:T(8,128)(2,1)S(1)} collective-permute-done((bf16[320,256]{1,0:T(8,128)(2,1)S(1)}, bf16[320,256]{1,0:T(8,128)(2,1)S(1)}, u32[]{:S(2)}, u32[]{:S(2)}) %collective-permute-start.10) | collective-permute-done | bytes 163872 | tf_op jit(solution)/shard_map/ppermute | solution.py:369
  37.6 0.8 %combine.1 = (f32[256,256]{1,0:T(8,128)}, f32[64,256]{1,0:T(8,128)}) custom-call(f32[256,256]{1,0:T(8,128)S(1)} %near_and_incident.1.base, f32[320,256]{1,0:T(8,128)S(1)} %resume.9.own, bf16[320,256]{1,0:T(8,128)(2,1)S(1)} %collective-permute-done.8.refs_0_, bf16[320,256]{1,0:T(8,128)(2,1)S(1)} %collective-permute-done.9.refs_1_, ...), custom_call_target="tpu_custom_call" | custom-call | tf_op jit(solution)/shard_map/combine/pallas_call | solution.py:482
  (23 shorter events, 0.2 us)
Async XLA Ops:
  1.6 12.0 %collective-permute-start.1 = (bf16[288,256]{1,0:T(8,128)(2,1)S(1)}, bf16[288,256]{1,0:T(8,128)(2,1)S(1)}, u32[]{:S(2)}, u32[]{:S(2)}) collective-permute-start(bf16[288,256]{1,0:T(8,128)(2,1)S(1)} %get-tuple-element.53.refs_1_), channel_id=1, source_target_pairs={{0,3},{1,2},{2,1},{3,0},{4,7},{5,6},{6,5},{7,4},{8,11},{9,10},{10,... | collective-permute-start | bytes 442376 | tf_op jit(solution)/shard_map/ppermute | solution.py:369
  6.7 11.5 %collective-permute-start.6 = (bf16[288,256]{1,0:T(8,128)(2,1)S(1)}, bf16[288,256]{1,0:T(8,128)(2,1)S(1)}, u32[]{:S(2)}, u32[]{:S(2)}) collective-permute-start(bf16[288,256]{1,0:T(8,128)(2,1)S(1)} %get-tuple-element.53.refs_1_), channel_id=1, source_target_pairs={{0,1},{1,0},{2,3},{3,2},{4,5},{5,4},{6,7},{7,6},{8,9},{9,8},{10,11... | collective-permute-start | bytes 442376 | tf_op jit(solution)/shard_map/ppermute | solution.py:369
  6.7 12.5 %collective-permute-start.5 = (bf16[288,256]{1,0:T(8,128)(2,1)S(1)}, bf16[288,256]{1,0:T(8,128)(2,1)S(1)}, u32[]{:S(2)}, u32[]{:S(2)}) collective-permute-start(bf16[288,256]{1,0:T(8,128)(2,1)S(1)} %get-tuple-element.53.refs_1_), channel_id=1, source_target_pairs={{0,2},{1,3},{2,0},{3,1},{4,6},{5,7},{6,4},{7,5},{8,10},{9,11},{10,... | collective-permute-start | bytes 442376 | tf_op jit(solution)/shard_map/ppermute | solution.py:369
  7.4 3.7 %collective-permute-start.3 = (f32[7,256]{1,0:T(8,128)S(1)}, f32[7,256]{1,0:T(8,128)S(1)}, u32[]{:S(2)}, u32[]{:S(2)}) collective-permute-start(f32[7,256]{1,0:T(8,128)S(1)} %get-tuple-element.99.refs_0_.g_ref), channel_id=1, source_target_pairs={{0,16},{4,20},{8,24},{12,28},{16,0},{20,4},{24,8},{28,12},{1,17},{... | collective-permute-start | bytes 21512 | tf_op jit(solution)/shard_map/ppermute | solution.py:369
  9.0 4.6 %collective-permute-start.2 = (f32[7,256]{1,0:T(8,128)S(1)}, f32[7,256]{1,0:T(8,128)S(1)}, u32[]{:S(2)}, u32[]{:S(2)}) collective-permute-start(f32[7,256]{1,0:T(8,128)S(1)} %get-tuple-element.99.refs_0_.g_ref), channel_id=1, source_target_pairs={{0,8},{4,12},{8,0},{12,4},{16,24},{20,28},{24,16},{28,20},{1,9},{5... | collective-permute-start | bytes 21512 | tf_op jit(solution)/shard_map/ppermute | solution.py:369
  11.0 6.0 %collective-permute-start = (f32[7,256]{1,0:T(8,128)S(1)}, f32[7,256]{1,0:T(8,128)S(1)}, u32[]{:S(2)}, u32[]{:S(2)}) collective-permute-start(f32[7,256]{1,0:T(8,128)S(1)} %get-tuple-element.99.refs_0_.g_ref), channel_id=1, source_target_pairs={{0,24},{4,28},{8,16},{12,20},{16,8},{20,12},{24,0},{28,4},{1,25},{... | collective-permute-start | bytes 21512 | tf_op jit(solution)/shard_map/ppermute | solution.py:369
  13.8 5.6 %collective-permute-start.4 = (bf16[576,256]{1,0:T(8,128)(2,1)S(1)}, bf16[576,256]{1,0:T(8,128)(2,1)S(1)}, u32[]{:S(2)}, u32[]{:S(2)}) collective-permute-start(bf16[576,256]{1,0:T(8,128)(2,1)S(1)} %pack.2), channel_id=1, source_target_pairs={{0,4},{4,0},{8,12},{12,8},{16,20},{20,16},{24,28},{28,24},{1,5},{5... | collective-permute-start | bytes 884744 | tf_op jit(solution)/shard_map/ppermute | solution.py:369
  19.2 2.1 %collective-permute-start.7 = (bf16[576,256]{1,0:T(8,128)(2,1)S(1)}, bf16[576,256]{1,0:T(8,128)(2,1)S(1)}, u32[]{:S(2)}, u32[]{:S(2)}) collective-permute-start(bf16[576,256]{1,0:T(8,128)(2,1)S(1)} %pack.3), channel_id=1, source_target_pairs={{0,4},{4,0},{8,12},{12,8},{16,20},{20,16},{24,28},{28,24},{1,5},{5... | collective-permute-start | bytes 884744 | tf_op jit(solution)/shard_map/ppermute | solution.py:369
  23.6 8.6 %collective-permute-start.8 = (bf16[320,256]{1,0:T(8,128)(2,1)S(1)}, bf16[320,256]{1,0:T(8,128)(2,1)S(1)}, u32[]{:S(2)}, u32[]{:S(2)}) collective-permute-start(bf16[320,256]{1,0:T(8,128)(2,1)S(1)} %resume.6), channel_id=1, source_target_pairs={{0,24},{4,28},{8,16},{12,20},{16,8},{20,12},{24,0},{28,4},{1,25},{... | collective-permute-start | bytes 491528 | tf_op jit(solution)/shard_map/ppermute | solution.py:369
  28.0 6.9 %collective-permute-start.9 = (bf16[320,256]{1,0:T(8,128)(2,1)S(1)}, bf16[320,256]{1,0:T(8,128)(2,1)S(1)}, u32[]{:S(2)}, u32[]{:S(2)}) collective-permute-start(bf16[320,256]{1,0:T(8,128)(2,1)S(1)} %resume.7), channel_id=1, source_target_pairs={{0,16},{4,20},{8,24},{12,28},{16,0},{20,4},{24,8},{28,12},{1,17},{... | collective-permute-start | bytes 491528 | tf_op jit(solution)/shard_map/ppermute | solution.py:369
  31.5 3.4 %copy-start = (bf16[256,256]{1,0:T(8,128)(2,1)S(1)}, bf16[256,256]{1,0:T(8,128)(2,1)}, u32[]{:S(2)}) copy-start(bf16[256,256]{1,0:T(8,128)(2,1)} %x_ref.1) | copy-start | bytes 393220
  31.5 3.4 %copy-start.1 = (f32[16,256]{1,0:T(8,128)S(1)}, f32[16,256]{1,0:T(8,128)}, u32[]{:S(2)}) copy-start(f32[16,256]{1,0:T(8,128)} %weight_ref.1) | copy-start | bytes 49156
  31.5 3.4 %copy-start.2 = (s32[8,256]{1,0:T(8,128)S(1)}, s32[8,256]{1,0:T(8,128)}, u32[]{:S(2)}) copy-start(s32[8,256]{1,0:T(8,128)} %index_ref.1) | copy-start | bytes 24580
  31.5 3.4 %copy-start.3 = (s32[128]{0:T(128)S(1)}, s32[128]{0:T(128)}, u32[]{:S(2)}) copy-start(s32[128]{0:T(128)} %param.11) | copy-start | bytes 1540
  31.5 3.4 %copy-start.4 = (s32[128]{0:T(128)S(1)}, s32[128]{0:T(128)}, u32[]{:S(2)}) copy-start(s32[128]{0:T(128)} %param.12) | copy-start | bytes 1540
  31.5 6.1 %collective-permute-start.10 = (bf16[320,256]{1,0:T(8,128)(2,1)S(1)}, bf16[320,256]{1,0:T(8,128)(2,1)S(1)}, u32[]{:S(2)}, u32[]{:S(2)}) collective-permute-start(bf16[320,256]{1,0:T(8,128)(2,1)S(1)} %resume.8), channel_id=1, source_target_pairs={{0,8},{4,12},{8,0},{12,4},{16,24},{20,28},{24,16},{28,20},{1,9},{5... | collective-permute-start | bytes 491528 | tf_op jit(solution)/shard_map/ppermute | solution.py:369

commit v4 on v3

--- a/solution.py
+++ b/solution.py
@@ -462,11 +462,13 @@
     other = after(other, held)
     columns = features(packed, other, *far_half)
     got = []
-    for pick in range(final, 0, -1):
-        resume([pick], columns, True, 2 * piece * (ncols // 2) // 2 // CHUNK if pick in ahead else 0)
-        got.append(xor_permute(held[pick], "rows", order[pick]))
-        held[pick - 1] = after(held[pick - 1], held[pick])
-
+    groups = [ahead[i : i + 2] for i in range(0, len(ahead), 2)]
+    groups += [[pick] for pick in range(final // 2, 0, -1)]
+    for picks in groups:
+        resume(picks, columns, True, 2 * piece * (ncols // 2) // 2 // CHUNK if picks[0] in ahead else 0)
+        got += [xor_permute(held[pick], "rows", order[pick]) for pick in picks]
+        coming = picks[-1] - 1
+        held[coming] = after(held[coming], held[picks[-1]])
     got[:1], held[0] = lax.optimization_barrier((got[:1], held[0]))
     resume([0], columns, True)
     own = held[0]

time: 38.6 us -> 38.4 us (level)
    pallas_call x5 -> x4, Pallas kernels: 11.3 us -> 11.1 us  [resume(): call(functools.partial(tiles_kernel, soft_sq, True, picks, skip), tuple((...]
  transfers between devices with their start and end apart: 11 -> 11, of which waited for: 3 -> 4; matrix products, arithmetic and copies ran while one was open for 0% -> 0% of each run, Pallas kernels for 39% -> 35%
where the time goes in v4:
time: 38.4 us; the launch traced here: 38.2 us
  Pallas kernels  18.9 us (49%)
  starting transfers between devices  15.3 us (40%)
  waiting for transfers between devices  3.22 us (8%)
  between operations  0.82 us (2%)
    ppermute x11, starting transfers between devices, xor_permute(): return lax.ppermute(value, axis, [(i, i ^ mask) for i in range(size)])  15.3 us
    pallas_call x4, Pallas kernels, resume(): call(functools.partial(tiles_kernel, soft_sq, True, picks, skip), tuple((...  11.1 us
    pallas_call x2, Pallas kernels, tiles(): call(functools.partial(tiles_kernel, soft_sq, False, picks, 0), (*kept *...  4.37 us
    ppermute x11, waiting for transfers between devices, xor_permute(): return lax.ppermute(value, axis, [(i, i ^ mask) for i in range(size)])  3.22 us
    pallas_call x1, Pallas kernels, local(): call(local_kernel, jax.ShapeDtypeStruct((piece, width), F32), name='near_...  1.07 us
    pallas_call x1, Pallas kernels, local(): call(functools.partial(payload_kernel, order), (pltpu.VMEM((piece + 32, w...  0.97 us
    pallas_call x1, Pallas kernels, local(): call(functools.partial(final_kernel, len(got)), (jax.ShapeDtypeStruct((pi...  0.78 us
  transfers between devices with their start and end apart: 11, of which 4 were waited for; matrix products, arithmetic and copies ran while one was open for 0% of the time, Pallas kernels for 35%

profile of v4, /device:TPU:0, one launch (start us, length us, event | category | flops | bytes accessed | tf_op | source)
XLA Modules:
  0.0 38.2 jit_solution(3401366344698027167)
XLA Ops:
  0.6 1.0 %payload.1 = (bf16[288,256]{1,0:T(8,128)(2,1)S(1)}, f32[32,64]{1,0:T(8,128)S(1)}, f32[7,256]{1,0:T(8,128)S(1)}) custom-call(bf16[256,256]{1,0:T(8,128)(2,1)} %x_ref.1, f32[7,256]{1,0:T(8,128)} %g_hbm.1, f32[2,2048]{1,0:T(2,128)} %angle_hbm.1), custom_call_target="tpu_custom_call" | custom-call | tf_op jit(solution)/shard_map/payload/pallas_call | solution.py:382
  1.6 5.1 %collective-permute-start.1 = (bf16[288,256]{1,0:T(8,128)(2,1)S(1)}, bf16[288,256]{1,0:T(8,128)(2,1)S(1)}, u32[]{:S(2)}, u32[]{:S(2)}) collective-permute-start(bf16[288,256]{1,0:T(8,128)(2,1)S(1)} %get-tuple-element.54.refs_1_), channel_id=1, source_target_pairs={{0,3},{1,2},{2,1},{3,0},{4,7},{5,6},{6,5},{7,4},{8,11},{9,10},{10,... | collective-permute-start | bytes 442376 | tf_op jit(solution)/shard_map/ppermute | solution.py:369
  6.7 0.6 %collective-permute-start.5 = (bf16[288,256]{1,0:T(8,128)(2,1)S(1)}, bf16[288,256]{1,0:T(8,128)(2,1)S(1)}, u32[]{:S(2)}, u32[]{:S(2)}) collective-permute-start(bf16[288,256]{1,0:T(8,128)(2,1)S(1)} %get-tuple-element.54.refs_1_), channel_id=1, source_target_pairs={{0,2},{1,3},{2,0},{3,1},{4,6},{5,7},{6,4},{7,5},{8,10},{9,11},{10,... | collective-permute-start | bytes 442376 | tf_op jit(solution)/shard_map/ppermute | solution.py:369
  7.4 1.7 %collective-permute-start.3 = (f32[7,256]{1,0:T(8,128)S(1)}, f32[7,256]{1,0:T(8,128)S(1)}, u32[]{:S(2)}, u32[]{:S(2)}) collective-permute-start(f32[7,256]{1,0:T(8,128)S(1)} %get-tuple-element.101.refs_0_.g_ref), channel_id=1, source_target_pairs={{0,16},{4,20},{8,24},{12,28},{16,0},{20,4},{24,8},{28,12},{1,17},{... | collective-permute-start | bytes 21512 | tf_op jit(solution)/shard_map/ppermute | solution.py:369
  9.0 1.5 %collective-permute-start.2 = (f32[7,256]{1,0:T(8,128)S(1)}, f32[7,256]{1,0:T(8,128)S(1)}, u32[]{:S(2)}, u32[]{:S(2)}) collective-permute-start(f32[7,256]{1,0:T(8,128)S(1)} %get-tuple-element.101.refs_0_.g_ref), channel_id=1, source_target_pairs={{0,8},{4,12},{8,0},{12,4},{16,24},{20,28},{24,16},{28,20},{1,9},{5... | collective-permute-start | bytes 21512 | tf_op jit(solution)/shard_map/ppermute | solution.py:369
  10.5 0.5 %collective-permute-done.3.refs_2_ = f32[7,256]{1,0:T(8,128)S(1)} collective-permute-done((f32[7,256]{1,0:T(8,128)S(1)}, f32[7,256]{1,0:T(8,128)S(1)}, u32[]{:S(2)}, u32[]{:S(2)}) %collective-permute-start.3) | collective-permute-done | bytes 7200 | tf_op jit(solution)/shard_map/ppermute | solution.py:369
  11.0 2.6 %collective-permute-start = (f32[7,256]{1,0:T(8,128)S(1)}, f32[7,256]{1,0:T(8,128)S(1)}, u32[]{:S(2)}, u32[]{:S(2)}) collective-permute-start(f32[7,256]{1,0:T(8,128)S(1)} %get-tuple-element.101.refs_0_.g_ref), channel_id=1, source_target_pairs={{0,24},{4,28},{8,16},{12,20},{16,8},{20,12},{24,0},{28,4},{1,25},{... | collective-permute-start | bytes 21512 | tf_op jit(solution)/shard_map/ppermute | solution.py:369
  13.6 0.1 columns.3
  13.8 3.1 %tiles.2 = (bf16[320,48]{1,0:T(8,128)(2,1)S(1)}, bf16[320,48]{1,0:T(8,128)(2,1)S(1)}, bf16[256,48]{1,0:T(8,128)(2,1)S(1)}, bf16[320,48]{1,0:T(8,128)(2,1)S(1)}, ...) custom-call(f32[7,256]{1,0:T(8,128)S(1)} %get-tuple-element.101.refs, ...), custom_call_target="tpu_custom_call" | custom-call | flops 1 | bytes 2000000 | tf_op jit(solution)/shard_map/tiles/pallas_call | solution.py:425
  17.0 1.2 %tiles.3 = (bf16[320,48]{1,0:T(8,128)(2,1)S(1)}, bf16[320,48]{1,0:T(8,128)(2,1)S(1)}, bf16[256,48]{1,0:T(8,128)(2,1)S(1)}, f32[320,256]{1,0:T(8,128)S(1)}) custom-call(f32[7,256]{1,0:T(8,128)S(1)} %collective-permute-done.refs_0_, f32[32,64]{1,0:T(8,128)S(1)} %get-tuple-element.58.refs_3_.refs_1_, bf16[48,512]{1,0:T(8,128)(2,1)S(1)} %get-tuple-element.60.refs_4_.refs_2_, ...), custom_call_target="tpu_custom_call" | custom-call | flops 1 | bytes 2000000 | tf_op jit(solution)/shard_map/tiles/pallas_call | solution.py:425
  18.2 1.0 %collective-permute-done.5.refs_0_.refs_2_ = bf16[288,256]{1,0:T(8,128)(2,1)S(1)} collective-permute-done((bf16[288,256]{1,0:T(8,128)(2,1)S(1)}, bf16[288,256]{1,0:T(8,128)(2,1)S(1)}, u32[]{:S(2)}, u32[]{:S(2)}) %collective-permute-start.5) | collective-permute-done | bytes 147488 | tf_op jit(solution)/shard_map/ppermute | solution.py:369
  19.3 0.1 columns.4
  19.4 1.9 %resume.4 = (f32[320,256]{1,0:T(8,128)S(1)}, f32[320,256]{1,0:T(8,128)S(1)}) custom-call(f32[320,256]{1,0:T(8,128)S(1)} %get-tuple-element.66.refs_0_, f32[320,256]{1,0:T(8,128)S(1)} %get-tuple-element.67.refs_1_, bf16[320,48]{1,0:T(8,128)(2,1)S(1)} %get-tuple-element.68.refs_2_, bf16[320,48]{1,0:T(8,128)(2,1)S(1)} %get-tuple-element.69.refs_3_, ...), custom_call_target="tpu_custom_call" | custom-call | flops 1 | bytes 2000000 | tf_op jit(solution)/shard_map/resume/pallas_call | solution.py:436
  21.4 0.3 columns.5
  21.7 3.5 %resume.5 = (bf16[320,256]{1,0:T(8,128)(2,1)S(1)}, bf16[320,256]{1,0:T(8,128)(2,1)S(1)}) custom-call(f32[320,256]{1,0:T(8,128)S(1)} %get-tuple-element.78.refs_0_, f32[320,256]{1,0:T(8,128)S(1)} %get-tuple-element.79.refs_1_, bf16[320,48]{1,0:T(8,128)(2,1)S(1)} %get-tuple-element.68.refs_2_, bf16[320,48]{1,0:T(8,128)(2,1)S(1)} %get-tuple-element.69.refs_3_, ...), custom_call_target="tpu_custom_call" | custom-call | flops 1 | bytes 2000000 | tf_op jit(solution)/shard_map/resume/pallas_call | solution.py:436
  25.2 2.5 %collective-permute-start.8 = (bf16[320,256]{1,0:T(8,128)(2,1)S(1)}, bf16[320,256]{1,0:T(8,128)(2,1)S(1)}, u32[]{:S(2)}, u32[]{:S(2)}) collective-permute-start(bf16[320,256]{1,0:T(8,128)(2,1)S(1)} %get-tuple-element.88), channel_id=1, source_target_pairs={{0,24},{4,28},{8,16},{12,20},{16,8},{20,12},{24,0},{28,4},{1,25},{... | collective-permute-start | bytes 491528 | tf_op jit(solution)/shard_map/ppermute | solution.py:369
  27.7 0.5 %collective-permute-start.9 = (bf16[320,256]{1,0:T(8,128)(2,1)S(1)}, bf16[320,256]{1,0:T(8,128)(2,1)S(1)}, u32[]{:S(2)}, u32[]{:S(2)}) collective-permute-start(bf16[320,256]{1,0:T(8,128)(2,1)S(1)} %get-tuple-element.89), channel_id=1, source_target_pairs={{0,16},{4,20},{8,24},{12,28},{16,0},{20,4},{24,8},{28,12},{1,17},{... | collective-permute-start | bytes 491528 | tf_op jit(solution)/shard_map/ppermute | solution.py:369
  28.2 2.9 %resume.6 = bf16[320,256]{1,0:T(8,128)(2,1)S(1)} custom-call(f32[320,256]{1,0:T(8,128)S(1)} %get-tuple-element.90.refs_0_, bf16[320,48]{1,0:T(8,128)(2,1)S(1)} %get-tuple-element.91.refs_1_, bf16[320,48]{1,0:T(8,128)(2,1)S(1)} %get-tuple-element.92.refs_2_, bf16[256,48]{1,0:T(8,128)(2,1)S(1)} %get-tuple-element.93.refs_3_, ...), custom_call_target="tpu_custom_call" | custom-call | flops 1 | bytes 2000000 | tf_op jit(solution)/shard_map/resume/pallas_call | solution.py:436
  31.2 0.6 %collective-permute-start.10 = (bf16[320,256]{1,0:T(8,128)(2,1)S(1)}, bf16[320,256]{1,0:T(8,128)(2,1)S(1)}, u32[]{:S(2)}, u32[]{:S(2)}) collective-permute-start(bf16[320,256]{1,0:T(8,128)(2,1)S(1)} %resume.6), channel_id=1, source_target_pairs={{0,8},{4,12},{8,0},{12,4},{16,24},{20,28},{24,16},{28,20},{1,9},{5... | collective-permute-start | bytes 491528 | tf_op jit(solution)/shard_map/ppermute | solution.py:369
  31.8 1.0 %collective-permute-done.8.refs_0_ = bf16[320,256]{1,0:T(8,128)(2,1)S(1)} collective-permute-done((bf16[320,256]{1,0:T(8,128)(2,1)S(1)}, bf16[320,256]{1,0:T(8,128)(2,1)S(1)}, u32[]{:S(2)}, u32[]{:S(2)}) %collective-permute-start.8) | collective-permute-done | bytes 163872 | tf_op jit(solution)/shard_map/ppermute | solution.py:369
  32.9 2.7 %resume.7.own = f32[320,256]{1,0:T(8,128)S(1)} custom-call(f32[320,256]{1,0:T(8,128)S(1)} %get-tuple-element.96.refs_0_, bf16[320,48]{1,0:T(8,128)(2,1)S(1)} %get-tuple-element.97.refs_1_, bf16[320,48]{1,0:T(8,128)(2,1)S(1)} %get-tuple-element.98.refs_2_, bf16[256,48]{1,0:T(8,128)(2,1)S(1)} %get-tuple-element.99.refs_3_, ...), custom_call_target="tpu_custom_call" | custom-call | flops 1 | bytes 2000000 | tf_op jit(solution)/shard_map/resume/pallas_call | solution.py:436
  35.6 0.7 %collective-permute-done.9.refs_1_ = bf16[320,256]{1,0:T(8,128)(2,1)S(1)} collective-permute-done((bf16[320,256]{1,0:T(8,128)(2,1)S(1)}, bf16[320,256]{1,0:T(8,128)(2,1)S(1)}, u32[]{:S(2)}, u32[]{:S(2)}) %collective-permute-start.9) | collective-permute-done | bytes 163872 | tf_op jit(solution)/shard_map/ppermute | solution.py:369
  36.3 1.1 %near_and_incident.1.base = f32[256,256]{1,0:T(8,128)S(1)} custom-call(bf16[256,256]{1,0:T(8,128)(2,1)S(1)} %copy-done, f32[7,256]{1,0:T(8,128)S(1)} %get-tuple-element.101.refs_0_.g_ref, s32[8,256]{1,0:T(8,128)S(1)} %copy-done.2, f32[16,256]{1,0:T(8,128)S(1)} %copy-done.1, s32[1,128]{1,0:T(1,128)S(1)} %bitcast.2, s32[1,128]{1,0:T(1,128)S(1)} %bitcast.3), custom_call_target="tpu_custom_call" | custom-call | flops 1 | bytes 2000000 | tf_op jit(solution)/shard_map/near_and_incident/pallas_call | solution.py:477
  37.4 0.8 %combine.1 = (f32[256,256]{1,0:T(8,128)}, f32[64,256]{1,0:T(8,128)}) custom-call(f32[256,256]{1,0:T(8,128)S(1)} %near_and_incident.1.base, f32[320,256]{1,0:T(8,128)S(1)} %resume.7.own, bf16[320,256]{1,0:T(8,128)(2,1)S(1)} %collective-permute-done.8.refs_0_, bf16[320,256]{1,0:T(8,128)(2,1)S(1)} %collective-permute-done.9.refs_1_, ...), custom_call_target="tpu_custom_call" | custom-call | tf_op jit(solution)/shard_map/combine/pallas_call | solution.py:484
  (22 shorter events, 0.2 us)
Async XLA Ops:
  1.6 12.0 %collective-permute-start.1 = (bf16[288,256]{1,0:T(8,128)(2,1)S(1)}, bf16[288,256]{1,0:T(8,128)(2,1)S(1)}, u32[]{:S(2)}, u32[]{:S(2)}) collective-permute-start(bf16[288,256]{1,0:T(8,128)(2,1)S(1)} %get-tuple-element.54.refs_1_), channel_id=1, source_target_pairs={{0,3},{1,2},{2,1},{3,0},{4,7},{5,6},{6,5},{7,4},{8,11},{9,10},{10,... | collective-permute-start | bytes 442376 | tf_op jit(solution)/shard_map/ppermute | solution.py:369
  6.7 11.5 %collective-permute-start.6 = (bf16[288,256]{1,0:T(8,128)(2,1)S(1)}, bf16[288,256]{1,0:T(8,128)(2,1)S(1)}, u32[]{:S(2)}, u32[]{:S(2)}) collective-permute-start(bf16[288,256]{1,0:T(8,128)(2,1)S(1)} %get-tuple-element.54.refs_1_), channel_id=1, source_target_pairs={{0,1},{1,0},{2,3},{3,2},{4,5},{5,4},{6,7},{7,6},{8,9},{9,8},{10,11... | collective-permute-start | bytes 442376 | tf_op jit(solution)/shard_map/ppermute | solution.py:369
  6.7 12.5 %collective-permute-start.5 = (bf16[288,256]{1,0:T(8,128)(2,1)S(1)}, bf16[288,256]{1,0:T(8,128)(2,1)S(1)}, u32[]{:S(2)}, u32[]{:S(2)}) collective-permute-start(bf16[288,256]{1,0:T(8,128)(2,1)S(1)} %get-tuple-element.54.refs_1_), channel_id=1, source_target_pairs={{0,2},{1,3},{2,0},{3,1},{4,6},{5,7},{6,4},{7,5},{8,10},{9,11},{10,... | collective-permute-start | bytes 442376 | tf_op jit(solution)/shard_map/ppermute | solution.py:369
  7.4 3.7 %collective-permute-start.3 = (f32[7,256]{1,0:T(8,128)S(1)}, f32[7,256]{1,0:T(8,128)S(1)}, u32[]{:S(2)}, u32[]{:S(2)}) collective-permute-start(f32[7,256]{1,0:T(8,128)S(1)} %get-tuple-element.101.refs_0_.g_ref), channel_id=1, source_target_pairs={{0,16},{4,20},{8,24},{12,28},{16,0},{20,4},{24,8},{28,12},{1,17},{... | collective-permute-start | bytes 21512 | tf_op jit(solution)/shard_map/ppermute | solution.py:369
  9.0 4.6 %collective-permute-start.2 = (f32[7,256]{1,0:T(8,128)S(1)}, f32[7,256]{1,0:T(8,128)S(1)}, u32[]{:S(2)}, u32[]{:S(2)}) collective-permute-start(f32[7,256]{1,0:T(8,128)S(1)} %get-tuple-element.101.refs_0_.g_ref), channel_id=1, source_target_pairs={{0,8},{4,12},{8,0},{12,4},{16,24},{20,28},{24,16},{28,20},{1,9},{5... | collective-permute-start | bytes 21512 | tf_op jit(solution)/shard_map/ppermute | solution.py:369
  11.0 6.0 %collective-permute-start = (f32[7,256]{1,0:T(8,128)S(1)}, f32[7,256]{1,0:T(8,128)S(1)}, u32[]{:S(2)}, u32[]{:S(2)}) collective-permute-start(f32[7,256]{1,0:T(8,128)S(1)} %get-tuple-element.101.refs_0_.g_ref), channel_id=1, source_target_pairs={{0,24},{4,28},{8,16},{12,20},{16,8},{20,12},{24,0},{28,4},{1,25},{... | collective-permute-start | bytes 21512 | tf_op jit(solution)/shard_map/ppermute | solution.py:369
  13.8 5.6 %collective-permute-start.4 = (bf16[576,256]{1,0:T(8,128)(2,1)S(1)}, bf16[576,256]{1,0:T(8,128)(2,1)S(1)}, u32[]{:S(2)}, u32[]{:S(2)}) collective-permute-start(bf16[576,256]{1,0:T(8,128)(2,1)S(1)} %pack.2), channel_id=1, source_target_pairs={{0,4},{4,0},{8,12},{12,8},{16,20},{20,16},{24,28},{28,24},{1,5},{5... | collective-permute-start | bytes 884744 | tf_op jit(solution)/shard_map/ppermute | solution.py:369
  19.2 2.1 %collective-permute-start.7 = (bf16[576,256]{1,0:T(8,128)(2,1)S(1)}, bf16[576,256]{1,0:T(8,128)(2,1)S(1)}, u32[]{:S(2)}, u32[]{:S(2)}) collective-permute-start(bf16[576,256]{1,0:T(8,128)(2,1)S(1)} %pack.3), channel_id=1, source_target_pairs={{0,4},{4,0},{8,12},{12,8},{16,20},{20,16},{24,28},{28,24},{1,5},{5... | collective-permute-start | bytes 884744 | tf_op jit(solution)/shard_map/ppermute | solution.py:369
  25.2 7.7 %collective-permute-start.8 = (bf16[320,256]{1,0:T(8,128)(2,1)S(1)}, bf16[320,256]{1,0:T(8,128)(2,1)S(1)}, u32[]{:S(2)}, u32[]{:S(2)}) collective-permute-start(bf16[320,256]{1,0:T(8,128)(2,1)S(1)} %get-tuple-element.88), channel_id=1, source_target_pairs={{0,24},{4,28},{8,16},{12,20},{16,8},{20,12},{24,0},{28,4},{1,25},{... | collective-permute-start | bytes 491528 | tf_op jit(solution)/shard_map/ppermute | solution.py:369
  27.7 8.6 %collective-permute-start.9 = (bf16[320,256]{1,0:T(8,128)(2,1)S(1)}, bf16[320,256]{1,0:T(8,128)(2,1)S(1)}, u32[]{:S(2)}, u32[]{:S(2)}) collective-permute-start(bf16[320,256]{1,0:T(8,128)(2,1)S(1)} %get-tuple-element.89), channel_id=1, source_target_pairs={{0,16},{4,20},{8,24},{12,28},{16,0},{20,4},{24,8},{28,12},{1,17},{... | collective-permute-start | bytes 491528 | tf_op jit(solution)/shard_map/ppermute | solution.py:369
  31.2 5.1 %copy-start = (bf16[256,256]{1,0:T(8,128)(2,1)S(1)}, bf16[256,256]{1,0:T(8,128)(2,1)}, u32[]{:S(2)}) copy-start(bf16[256,256]{1,0:T(8,128)(2,1)} %x_ref.1) | copy-start | bytes 393220
  31.2 5.1 %copy-start.1 = (f32[16,256]{1,0:T(8,128)S(1)}, f32[16,256]{1,0:T(8,128)}, u32[]{:S(2)}) copy-start(f32[16,256]{1,0:T(8,128)} %weight_ref.1) | copy-start | bytes 49156
  31.2 5.1 %copy-start.2 = (s32[8,256]{1,0:T(8,128)S(1)}, s32[8,256]{1,0:T(8,128)}, u32[]{:S(2)}) copy-start(s32[8,256]{1,0:T(8,128)} %index_ref.1) | copy-start | bytes 24580
  31.2 5.1 %copy-start.3 = (s32[128]{0:T(128)S(1)}, s32[128]{0:T(128)}, u32[]{:S(2)}) copy-start(s32[128]{0:T(128)} %param.11) | copy-start | bytes 1540
  31.2 5.1 %copy-start.4 = (s32[128]{0:T(128)S(1)}, s32[128]{0:T(128)}, u32[]{:S(2)}) copy-start(s32[128]{0:T(128)} %param.12) | copy-start | bytes 1540
  31.2 6.2 %collective-permute-start.10 = (bf16[320,256]{1,0:T(8,128)(2,1)S(1)}, bf16[320,256]{1,0:T(8,128)(2,1)S(1)}, u32[]{:S(2)}, u32[]{:S(2)}) collective-permute-start(bf16[320,256]{1,0:T(8,128)(2,1)S(1)} %resume.6), channel_id=1, source_target_pairs={{0,8},{4,12},{8,0},{12,4},{16,24},{20,28},{24,16},{28,20},{1,9},{5... | collective-permute-start | bytes 491528 | tf_op jit(solution)/shard_map/ppermute | solution.py:369

commit v5 on v4

--- a/solution.py
+++ b/solution.py
@@ -335,14 +335,20 @@
     out[:, half:] = b[:, half:] - 0.5 * xf[:, half:] - (first[:, half:] + second[:, :half])
 
 
-def final_kernel(count, base, own, *refs):
-    got, residual, far = refs[:count], refs[count], refs[count + 1]
-    piece = residual.shape[0]
+def collect_kernel(count, base, own, *refs):
+    got, out = refs[:count], refs[count]
+    piece = base.shape[0]
     total = own[...]
     for ref in got:
         total += ref[...].astype(F32)
-    residual[...] = base[...] - total[:piece]
-    far[...] = total[piece:]
+    out[:piece] = base[...] - total[:piece]
+    out[piece:] = total[piece:]
+
+
+def final_kernel(most, got, residual, far):
+    piece = residual.shape[0]
+    residual[...] = most[:piece] - got[:piece].astype(F32)
+    far[...] = most[piece:] + got[piece:].astype(F32)
 
 
 def call(kernel, out_shape, scratch=(), name=None, cost=None, inputs=None, limit=40):
@@ -469,23 +475,27 @@
         got += [xor_permute(held[pick], "rows", order[pick]) for pick in picks]
         coming = picks[-1] - 1
         held[coming] = after(held[coming], held[picks[-1]])
-    got[:1], held[0] = lax.optimization_barrier((got[:1], held[0]))
-    resume([0], columns, True)
-    own = held[0]
-
-    got[:-1], near_geometry = lax.optimization_barrier((got[:-1], after(geometry_here, own)))
+
     base = call(
         local_kernel,
         jax.ShapeDtypeStruct((piece, width), F32),
         name="near_and_incident",
         cost=NEAR_COST,
-    )(krylov, near_geometry, corr_index, corr_weight, blades.reshape(1, -1), harmonic.reshape(1, -1))
+    )(krylov, after(geometry_here, held[1]), corr_index, corr_weight, blades.reshape(1, -1), harmonic.reshape(1, -1))
+    got[:1], held[0] = lax.optimization_barrier((got[:1], after(held[0], base)))
+    resume([0], columns, True)
+    most = call(
+        functools.partial(collect_kernel, len(got) - 1),
+        jax.ShapeDtypeStruct((rows, width), F32),
+        name="collect",
+        cost=NEAR_COST,
+    )(base, held[0], *got[:-1])
 
     return call(
-        functools.partial(final_kernel, len(got)),
+        final_kernel,
         (jax.ShapeDtypeStruct((piece, width), F32), jax.ShapeDtypeStruct((each, width), F32)),
         name="combine",
-    )(base, own, *got)
+    )(most, got[-1])
 
 
 def solution(mesh):

time: 38.4 us -> 38.3 us (level)
    pallas_call x1 -> x2, Pallas kernels: 0.78 us -> 0.8 us  [the longest x1 0.74 us: local(): call(final_kernel, (jax.ShapeDtypeStruct((piece, width), F32), jax.ShapeD...]
where the time goes in v5:
time: 38.3 us; the launch traced here: 38 us
  Pallas kernels  18.8 us (49%)
  starting transfers between devices  15.3 us (40%)
  waiting for transfers between devices  3.1 us (8%)
  between operations  0.81 us (2%)
    ppermute x11, starting transfers between devices, xor_permute(): return lax.ppermute(value, axis, [(i, i ^ mask) for i in range(size)])  15.3 us
    pallas_call x4, Pallas kernels, resume(): call(functools.partial(tiles_kernel, soft_sq, True, picks, skip), tuple((...  11 us
    pallas_call x2, Pallas kernels, tiles(): call(functools.partial(tiles_kernel, soft_sq, False, picks, 0), (*kept *...  4.37 us
    ppermute x11, waiting for transfers between devices, xor_permute(): return lax.ppermute(value, axis, [(i, i ^ mask) for i in range(size)])  3.1 us
    pallas_call x1, Pallas kernels, local(): call(local_kernel, jax.ShapeDtypeStruct((piece, width), F32), name='near_...  1.07 us
    pallas_call x1, Pallas kernels, local(): call(functools.partial(payload_kernel, order), (pltpu.VMEM((piece + 32, w...  0.97 us
  transfers between devices with their start and end apart: 11, of which 4 were waited for; matrix products, arithmetic and copies ran while one was open for 0% of the time, Pallas kernels for 35%

profile of v5, /device:TPU:0, one launch (start us, length us, event | category | flops | bytes accessed | tf_op | source)
XLA Modules:
  0.0 38.0 jit_solution(15370351918575145822)
XLA Ops:
  0.6 1.0 %payload.1 = (bf16[288,256]{1,0:T(8,128)(2,1)S(1)}, f32[32,64]{1,0:T(8,128)S(1)}, f32[7,256]{1,0:T(8,128)S(1)}) custom-call(bf16[256,256]{1,0:T(8,128)(2,1)} %x_ref.1, f32[7,256]{1,0:T(8,128)} %g_hbm.1, f32[2,2048]{1,0:T(2,128)} %angle_hbm.1), custom_call_target="tpu_custom_call" | custom-call | tf_op jit(solution)/shard_map/payload/pallas_call | solution.py:388
  1.6 5.1 %collective-permute-start = (bf16[288,256]{1,0:T(8,128)(2,1)S(1)}, bf16[288,256]{1,0:T(8,128)(2,1)S(1)}, u32[]{:S(2)}, u32[]{:S(2)}) collective-permute-start(bf16[288,256]{1,0:T(8,128)(2,1)S(1)} %get-tuple-element.52.refs_1_), channel_id=1, source_target_pairs={{0,3},{1,2},{2,1},{3,0},{4,7},{5,6},{6,5},{7,4},{8,11},{9,10},{10,... | collective-permute-start | bytes 442376 | tf_op jit(solution)/shard_map/ppermute | solution.py:375
  6.7 0.6 %collective-permute-start.5 = (bf16[288,256]{1,0:T(8,128)(2,1)S(1)}, bf16[288,256]{1,0:T(8,128)(2,1)S(1)}, u32[]{:S(2)}, u32[]{:S(2)}) collective-permute-start(bf16[288,256]{1,0:T(8,128)(2,1)S(1)} %get-tuple-element.52.refs_1_), channel_id=1, source_target_pairs={{0,2},{1,3},{2,0},{3,1},{4,6},{5,7},{6,4},{7,5},{8,10},{9,11},{10,... | collective-permute-start | bytes 442376 | tf_op jit(solution)/shard_map/ppermute | solution.py:375
  7.4 1.7 %collective-permute-start.2 = (f32[7,256]{1,0:T(8,128)S(1)}, f32[7,256]{1,0:T(8,128)S(1)}, u32[]{:S(2)}, u32[]{:S(2)}) collective-permute-start(f32[7,256]{1,0:T(8,128)S(1)} %get-tuple-element.91.refs_0_.g_ref), channel_id=1, source_target_pairs={{0,16},{4,20},{8,24},{12,28},{16,0},{20,4},{24,8},{28,12},{1,17},{... | collective-permute-start | bytes 21512 | tf_op jit(solution)/shard_map/ppermute | solution.py:375
  9.0 1.5 %collective-permute-start.1 = (f32[7,256]{1,0:T(8,128)S(1)}, f32[7,256]{1,0:T(8,128)S(1)}, u32[]{:S(2)}, u32[]{:S(2)}) collective-permute-start(f32[7,256]{1,0:T(8,128)S(1)} %get-tuple-element.91.refs_0_.g_ref), channel_id=1, source_target_pairs={{0,8},{4,12},{8,0},{12,4},{16,24},{20,28},{24,16},{28,20},{1,9},{5... | collective-permute-start | bytes 21512 | tf_op jit(solution)/shard_map/ppermute | solution.py:375
  10.5 0.5 %collective-permute-done.2.refs_2_ = f32[7,256]{1,0:T(8,128)S(1)} collective-permute-done((f32[7,256]{1,0:T(8,128)S(1)}, f32[7,256]{1,0:T(8,128)S(1)}, u32[]{:S(2)}, u32[]{:S(2)}) %collective-permute-start.2) | collective-permute-done | bytes 7200 | tf_op jit(solution)/shard_map/ppermute | solution.py:375
  11.0 2.6 %collective-permute-start.3 = (f32[7,256]{1,0:T(8,128)S(1)}, f32[7,256]{1,0:T(8,128)S(1)}, u32[]{:S(2)}, u32[]{:S(2)}) collective-permute-start(f32[7,256]{1,0:T(8,128)S(1)} %get-tuple-element.91.refs_0_.g_ref), channel_id=1, source_target_pairs={{0,24},{4,28},{8,16},{12,20},{16,8},{20,12},{24,0},{28,4},{1,25},{... | collective-permute-start | bytes 21512 | tf_op jit(solution)/shard_map/ppermute | solution.py:375
  13.6 0.1 columns.3
  13.8 3.1 %tiles.2 = (bf16[320,48]{1,0:T(8,128)(2,1)S(1)}, bf16[320,48]{1,0:T(8,128)(2,1)S(1)}, bf16[256,48]{1,0:T(8,128)(2,1)S(1)}, bf16[320,48]{1,0:T(8,128)(2,1)S(1)}, ...) custom-call(f32[7,256]{1,0:T(8,128)S(1)} %get-tuple-element.91.refs_, ...), custom_call_target="tpu_custom_call" | custom-call | flops 1 | bytes 2000000 | tf_op jit(solution)/shard_map/tiles/pallas_call | solution.py:431
  17.0 1.2 %tiles.3 = (bf16[320,48]{1,0:T(8,128)(2,1)S(1)}, bf16[320,48]{1,0:T(8,128)(2,1)S(1)}, bf16[256,48]{1,0:T(8,128)(2,1)S(1)}, f32[320,256]{1,0:T(8,128)S(1)}) custom-call(f32[7,256]{1,0:T(8,128)S(1)} %collective-permute-done.3.refs_0_, f32[32,64]{1,0:T(8,128)S(1)} %get-tuple-element.56.refs_3_.refs_1_, bf16[48,512]{1,0:T(8,128)(2,1)S(1)} %get-tuple-element.58.refs_4_.refs_2_, ...), custom_call_target="tpu_custom_call" | custom-call | flops 1 | bytes 2000000 | tf_op jit(solution)/shard_map/tiles/pallas_call | solution.py:431
  18.2 1.0 %collective-permute-done.5.refs_0_.refs_2_ = bf16[288,256]{1,0:T(8,128)(2,1)S(1)} collective-permute-done((bf16[288,256]{1,0:T(8,128)(2,1)S(1)}, bf16[288,256]{1,0:T(8,128)(2,1)S(1)}, u32[]{:S(2)}, u32[]{:S(2)}) %collective-permute-start.5) | collective-permute-done | bytes 147488 | tf_op jit(solution)/shard_map/ppermute | solution.py:375
  19.3 0.1 columns.4
  19.4 1.9 %resume.4 = (f32[320,256]{1,0:T(8,128)S(1)}, f32[320,256]{1,0:T(8,128)S(1)}) custom-call(f32[320,256]{1,0:T(8,128)S(1)} %get-tuple-element.65.refs_0_, f32[320,256]{1,0:T(8,128)S(1)} %get-tuple-element.66.refs_1_, bf16[320,48]{1,0:T(8,128)(2,1)S(1)} %get-tuple-element.67.refs_2_, bf16[320,48]{1,0:T(8,128)(2,1)S(1)} %get-tuple-element.68.refs_3_, ...), custom_call_target="tpu_custom_call" | custom-call | flops 1 | bytes 2000000 | tf_op jit(solution)/shard_map/resume/pallas_call | solution.py:442
  21.4 0.3 columns.5
  21.7 3.5 %resume.5 = (bf16[320,256]{1,0:T(8,128)(2,1)S(1)}, bf16[320,256]{1,0:T(8,128)(2,1)S(1)}) custom-call(f32[320,256]{1,0:T(8,128)S(1)} %get-tuple-element.77.refs_0_, f32[320,256]{1,0:T(8,128)S(1)} %get-tuple-element.78.refs_1_, bf16[320,48]{1,0:T(8,128)(2,1)S(1)} %get-tuple-element.67.refs_2_, bf16[320,48]{1,0:T(8,128)(2,1)S(1)} %get-tuple-element.68.refs_3_, ...), custom_call_target="tpu_custom_call" | custom-call | flops 1 | bytes 2000000 | tf_op jit(solution)/shard_map/resume/pallas_call | solution.py:442
  25.3 2.5 %collective-permute-start.8 = (bf16[320,256]{1,0:T(8,128)(2,1)S(1)}, bf16[320,256]{1,0:T(8,128)(2,1)S(1)}, u32[]{:S(2)}, u32[]{:S(2)}) collective-permute-start(bf16[320,256]{1,0:T(8,128)(2,1)S(1)} %get-tuple-element.92), channel_id=1, source_target_pairs={{0,24},{4,28},{8,16},{12,20},{16,8},{20,12},{24,0},{28,4},{1,25},{... | collective-permute-start | bytes 491528 | tf_op jit(solution)/shard_map/ppermute | solution.py:375
  27.8 0.5 %collective-permute-start.9 = (bf16[320,256]{1,0:T(8,128)(2,1)S(1)}, bf16[320,256]{1,0:T(8,128)(2,1)S(1)}, u32[]{:S(2)}, u32[]{:S(2)}) collective-permute-start(bf16[320,256]{1,0:T(8,128)(2,1)S(1)} %get-tuple-element.86), channel_id=1, source_target_pairs={{0,16},{4,20},{8,24},{12,28},{16,0},{20,4},{24,8},{28,12},{1,17},{... | collective-permute-start | bytes 491528 | tf_op jit(solution)/shard_map/ppermute | solution.py:375
  28.3 2.9 %resume.6 = bf16[320,256]{1,0:T(8,128)(2,1)S(1)} custom-call(f32[320,256]{1,0:T(8,128)S(1)} %get-tuple-element.87.refs_0_, bf16[320,48]{1,0:T(8,128)(2,1)S(1)} %get-tuple-element.88.refs_1_, bf16[320,48]{1,0:T(8,128)(2,1)S(1)} %get-tuple-element.89.refs_2_, bf16[256,48]{1,0:T(8,128)(2,1)S(1)} %get-tuple-element.90.refs_3_, ...), custom_call_target="tpu_custom_call" | custom-call | flops 1 | bytes 2000000 | tf_op jit(solution)/shard_map/resume/pallas_call | solution.py:442
  31.2 0.6 %collective-permute-start.10 = (bf16[320,256]{1,0:T(8,128)(2,1)S(1)}, bf16[320,256]{1,0:T(8,128)(2,1)S(1)}, u32[]{:S(2)}, u32[]{:S(2)}) collective-permute-start(bf16[320,256]{1,0:T(8,128)(2,1)S(1)} %resume.6), channel_id=1, source_target_pairs={{0,8},{4,12},{8,0},{12,4},{16,24},{20,28},{24,16},{28,20},{1,9},{5... | collective-permute-start | bytes 491528 | tf_op jit(solution)/shard_map/ppermute | solution.py:375
  31.8 1.1 %near_and_incident.1.base = f32[256,256]{1,0:T(8,128)S(1)} custom-call(bf16[256,256]{1,0:T(8,128)(2,1)S(1)} %copy-done, f32[7,256]{1,0:T(8,128)S(1)} %get-tuple-element.91.refs_0_.g_ref, s32[8,256]{1,0:T(8,128)S(1)} %copy-done.2, f32[16,256]{1,0:T(8,128)S(1)} %copy-done.1, s32[1,128]{1,0:T(1,128)S(1)} %bitcast.2, s32[1,128]{1,0:T(1,128)S(1)} %bitcast.3), custom_call_target="tpu_custom_call" | custom-call | flops 1 | bytes 2000000 | tf_op jit(solution)/shard_map/near_and_incident/pallas_call | solution.py:479
  32.9 2.7 %resume.7.own = f32[320,256]{1,0:T(8,128)S(1)} custom-call(f32[320,256]{1,0:T(8,128)S(1)} %get-tuple-element.95.refs_0_, bf16[320,48]{1,0:T(8,128)(2,1)S(1)} %get-tuple-element.96.refs_1_, bf16[320,48]{1,0:T(8,128)(2,1)S(1)} %get-tuple-element.97.refs_2_, bf16[256,48]{1,0:T(8,128)(2,1)S(1)} %get-tuple-element.98.refs_3_, ...), custom_call_target="tpu_custom_call" | custom-call | flops 1 | bytes 2000000 | tf_op jit(solution)/shard_map/resume/pallas_call | solution.py:442
  35.7 0.7 %collective-permute-done.9.refs_1_ = bf16[320,256]{1,0:T(8,128)(2,1)S(1)} collective-permute-done((bf16[320,256]{1,0:T(8,128)(2,1)S(1)}, bf16[320,256]{1,0:T(8,128)(2,1)S(1)}, u32[]{:S(2)}, u32[]{:S(2)}) %collective-permute-start.9) | collective-permute-done | bytes 163872 | tf_op jit(solution)/shard_map/ppermute | solution.py:375
  36.4 0.9 %collective-permute-done.10.got = bf16[320,256]{1,0:T(8,128)(2,1)S(1)} collective-permute-done((bf16[320,256]{1,0:T(8,128)(2,1)S(1)}, bf16[320,256]{1,0:T(8,128)(2,1)S(1)}, u32[]{:S(2)}, u32[]{:S(2)}) %collective-permute-start.10) | collective-permute-done | bytes 163872 | tf_op jit(solution)/shard_map/ppermute | solution.py:375
  37.3 0.7 %combine.1 = (f32[256,256]{1,0:T(8,128)}, f32[64,256]{1,0:T(8,128)}) custom-call(f32[320,256]{1,0:T(8,128)S(1)} %collect.1.most, bf16[320,256]{1,0:T(8,128)(2,1)S(1)} %collective-permute-done.10.got), custom_call_target="tpu_custom_call" | custom-call | tf_op jit(solution)/shard_map/combine/pallas_call | solution.py:494
  (23 shorter events, 0.3 us)
Async XLA Ops:
  1.6 12.0 %collective-permute-start = (bf16[288,256]{1,0:T(8,128)(2,1)S(1)}, bf16[288,256]{1,0:T(8,128)(2,1)S(1)}, u32[]{:S(2)}, u32[]{:S(2)}) collective-permute-start(bf16[288,256]{1,0:T(8,128)(2,1)S(1)} %get-tuple-element.52.refs_1_), channel_id=1, source_target_pairs={{0,3},{1,2},{2,1},{3,0},{4,7},{5,6},{6,5},{7,4},{8,11},{9,10},{10,... | collective-permute-start | bytes 442376 | tf_op jit(solution)/shard_map/ppermute | solution.py:375
  6.7 11.5 %collective-permute-start.6 = (bf16[288,256]{1,0:T(8,128)(2,1)S(1)}, bf16[288,256]{1,0:T(8,128)(2,1)S(1)}, u32[]{:S(2)}, u32[]{:S(2)}) collective-permute-start(bf16[288,256]{1,0:T(8,128)(2,1)S(1)} %get-tuple-element.52.refs_1_), channel_id=1, source_target_pairs={{0,1},{1,0},{2,3},{3,2},{4,5},{5,4},{6,7},{7,6},{8,9},{9,8},{10,11... | collective-permute-start | bytes 442376 | tf_op jit(solution)/shard_map/ppermute | solution.py:375
  6.7 12.5 %collective-permute-start.5 = (bf16[288,256]{1,0:T(8,128)(2,1)S(1)}, bf16[288,256]{1,0:T(8,128)(2,1)S(1)}, u32[]{:S(2)}, u32[]{:S(2)}) collective-permute-start(bf16[288,256]{1,0:T(8,128)(2,1)S(1)} %get-tuple-element.52.refs_1_), channel_id=1, source_target_pairs={{0,2},{1,3},{2,0},{3,1},{4,6},{5,7},{6,4},{7,5},{8,10},{9,11},{10,... | collective-permute-start | bytes 442376 | tf_op jit(solution)/shard_map/ppermute | solution.py:375
  7.4 3.7 %collective-permute-start.2 = (f32[7,256]{1,0:T(8,128)S(1)}, f32[7,256]{1,0:T(8,128)S(1)}, u32[]{:S(2)}, u32[]{:S(2)}) collective-permute-start(f32[7,256]{1,0:T(8,128)S(1)} %get-tuple-element.91.refs_0_.g_ref), channel_id=1, source_target_pairs={{0,16},{4,20},{8,24},{12,28},{16,0},{20,4},{24,8},{28,12},{1,17},{... | collective-permute-start | bytes 21512 | tf_op jit(solution)/shard_map/ppermute | solution.py:375
  9.0 4.6 %collective-permute-start.1 = (f32[7,256]{1,0:T(8,128)S(1)}, f32[7,256]{1,0:T(8,128)S(1)}, u32[]{:S(2)}, u32[]{:S(2)}) collective-permute-start(f32[7,256]{1,0:T(8,128)S(1)} %get-tuple-element.91.refs_0_.g_ref), channel_id=1, source_target_pairs={{0,8},{4,12},{8,0},{12,4},{16,24},{20,28},{24,16},{28,20},{1,9},{5... | collective-permute-start | bytes 21512 | tf_op jit(solution)/shard_map/ppermute | solution.py:375
  11.0 6.0 %collective-permute-start.3 = (f32[7,256]{1,0:T(8,128)S(1)}, f32[7,256]{1,0:T(8,128)S(1)}, u32[]{:S(2)}, u32[]{:S(2)}) collective-permute-start(f32[7,256]{1,0:T(8,128)S(1)} %get-tuple-element.91.refs_0_.g_ref), channel_id=1, source_target_pairs={{0,24},{4,28},{8,16},{12,20},{16,8},{20,12},{24,0},{28,4},{1,25},{... | collective-permute-start | bytes 21512 | tf_op jit(solution)/shard_map/ppermute | solution.py:375
  13.8 5.6 %collective-permute-start.4 = (bf16[576,256]{1,0:T(8,128)(2,1)S(1)}, bf16[576,256]{1,0:T(8,128)(2,1)S(1)}, u32[]{:S(2)}, u32[]{:S(2)}) collective-permute-start(bf16[576,256]{1,0:T(8,128)(2,1)S(1)} %pack.2), channel_id=1, source_target_pairs={{0,4},{4,0},{8,12},{12,8},{16,20},{20,16},{24,28},{28,24},{1,5},{5... | collective-permute-start | bytes 884744 | tf_op jit(solution)/shard_map/ppermute | solution.py:375
  19.2 2.1 %collective-permute-start.7 = (bf16[576,256]{1,0:T(8,128)(2,1)S(1)}, bf16[576,256]{1,0:T(8,128)(2,1)S(1)}, u32[]{:S(2)}, u32[]{:S(2)}) collective-permute-start(bf16[576,256]{1,0:T(8,128)(2,1)S(1)} %pack.3), channel_id=1, source_target_pairs={{0,4},{4,0},{8,12},{12,8},{16,20},{20,16},{24,28},{28,24},{1,5},{5... | collective-permute-start | bytes 884744 | tf_op jit(solution)/shard_map/ppermute | solution.py:375
  25.2 6.6 %copy-start = (bf16[256,256]{1,0:T(8,128)(2,1)S(1)}, bf16[256,256]{1,0:T(8,128)(2,1)}, u32[]{:S(2)}) copy-start(bf16[256,256]{1,0:T(8,128)(2,1)} %x_ref.1) | copy-start | bytes 393220
  25.2 6.6 %copy-start.1 = (f32[16,256]{1,0:T(8,128)S(1)}, f32[16,256]{1,0:T(8,128)}, u32[]{:S(2)}) copy-start(f32[16,256]{1,0:T(8,128)} %weight_ref.1) | copy-start | bytes 49156
  25.2 6.6 %copy-start.2 = (s32[8,256]{1,0:T(8,128)S(1)}, s32[8,256]{1,0:T(8,128)}, u32[]{:S(2)}) copy-start(s32[8,256]{1,0:T(8,128)} %index_ref.1) | copy-start | bytes 24580
  25.3 6.6 %copy-start.3 = (s32[128]{0:T(128)S(1)}, s32[128]{0:T(128)}, u32[]{:S(2)}) copy-start(s32[128]{0:T(128)} %param.11) | copy-start | bytes 1540
  25.3 6.6 %copy-start.4 = (s32[128]{0:T(128)S(1)}, s32[128]{0:T(128)}, u32[]{:S(2)}) copy-start(s32[128]{0:T(128)} %param.12) | copy-start | bytes 1540
  25.3 7.7 %collective-permute-start.8 = (bf16[320,256]{1,0:T(8,128)(2,1)S(1)}, bf16[320,256]{1,0:T(8,128)(2,1)S(1)}, u32[]{:S(2)}, u32[]{:S(2)}) collective-permute-start(bf16[320,256]{1,0:T(8,128)(2,1)S(1)} %get-tuple-element.92), channel_id=1, source_target_pairs={{0,24},{4,28},{8,16},{12,20},{16,8},{20,12},{24,0},{28,4},{1,25},{... | collective-permute-start | bytes 491528 | tf_op jit(solution)/shard_map/ppermute | solution.py:375
  27.8 8.6 %collective-permute-start.9 = (bf16[320,256]{1,0:T(8,128)(2,1)S(1)}, bf16[320,256]{1,0:T(8,128)(2,1)S(1)}, u32[]{:S(2)}, u32[]{:S(2)}) collective-permute-start(bf16[320,256]{1,0:T(8,128)(2,1)S(1)} %get-tuple-element.86), channel_id=1, source_target_pairs={{0,16},{4,20},{8,24},{12,28},{16,0},{20,4},{24,8},{28,12},{1,17},{... | collective-permute-start | bytes 491528 | tf_op jit(solution)/shard_map/ppermute | solution.py:375
  31.2 6.1 %collective-permute-start.10 = (bf16[320,256]{1,0:T(8,128)(2,1)S(1)}, bf16[320,256]{1,0:T(8,128)(2,1)S(1)}, u32[]{:S(2)}, u32[]{:S(2)}) collective-permute-start(bf16[320,256]{1,0:T(8,128)(2,1)S(1)} %resume.6), channel_id=1, source_target_pairs={{0,8},{4,12},{8,0},{12,4},{16,24},{20,28},{24,16},{28,20},{1,9},{5... | collective-permute-start | bytes 491528 | tf_op jit(solution)/shard_map/ppermute | solution.py:375
